TPU v7x, 32 devices: a whole 2x2x4 slice. The times are simulated.
32 devices in a mesh: ctx: 8 (over z, x), fsdp: 4 (over y, core).
Axes of the slice: x: 2, y: 2, z: 4, core: 2. Of those that a mesh axis runs over, the one named last changes fastest.
Arguments:
- tokens: bfloat16 [12, 1024, 576], P('fsdp', 'ctx'), may hold values from -6 to 6
- cotangent: bfloat16 [12, 1024, 576], P('fsdp', 'ctx'), may hold values from -6 to 6
- attn_gain: bfloat16 [576], P('fsdp'), may hold values from 0.5 to 1.5
- w_query: bfloat16 [576, 576], P('fsdp'), may hold values from -0.25 to 0.25
- w_key: bfloat16 [576, 192], P('fsdp'), may hold values from -0.25 to 0.25
- w_value: bfloat16 [576, 192], P('fsdp'), may hold values from -0.25 to 0.25
- w_out: bfloat16 [576, 576], P('fsdp'), may hold values from -1 to 1
- mlp_gain: bfloat16 [576], P('fsdp'), may hold values from 0.5 to 1.5
- w_gate: bfloat16 [576, 1536], P('fsdp'), may hold values from -0.25 to 0.25
- w_up: bfloat16 [576, 1536], P('fsdp'), may hold values from -0.25 to 0.25
- w_down: bfloat16 [1536, 576], P('fsdp'), may hold values from -0.15625 to 0.15625
- seq_lengths: int32 [12], P('fsdp'), may hold values from 256 to 1024, as said below
- seq_starts: int32 [12], P('fsdp'), may hold values from 0 to 768, as said below
Outputs:
- mixed_out: float32 [12, 1024, 576], P('fsdp', 'ctx')
- input_grad: float32 [12, 1024, 576], P('fsdp', 'ctx')
- grad_attn_gain: float32 [576], P('fsdp')
- grad_query: float32 [576, 576], P('fsdp')
- grad_key: float32 [576, 192], P('fsdp')
- grad_value: float32 [576, 192], P('fsdp')
- grad_out: float32 [576, 576], P('fsdp')
- grad_mlp_gain: float32 [576], P('fsdp')
- grad_gate: float32 [576, 1536], P('fsdp')
- grad_up: float32 [576, 1536], P('fsdp')
- grad_down: float32 [1536, 576], P('fsdp')
Inputs may be any that keep to these rules, and one draw needn't show every extreme that they name: `seq_lengths`: in each group of 3 consecutive rows (the rows of one fsdp index) one row, chosen by the seed, holds a sequence of 1024 tokens starting at 0; every sequence ends within its row. seq_starts + seq_lengths <= 1024 in every row.
All inputs are finite; a program needn't handle non-finite values.
Results may differ from a plain program's by a relative error of at most 0.039.
Values may be sent and summed in bfloat16 or wider, within the bound.
No kernel may reach another device: no remote copies, remote signals or barrier semaphores. Data moves between devices by JAX's collectives and lax.ppermute only.
A program may use at most 192 MiB of HBM per device.

v0:
```python
import functools
import math

import jax
import jax.numpy as jnp
from jax import lax
from jax.experimental import pallas as pl
from jax.experimental.pallas import tpu as pltpu
from jax.sharding import PartitionSpec as P

HEADS = 9
KV_HEADS = 3
HEAD_DIM = 64
GROUP = HEADS // KV_HEADS
LANES = 128
EPSILON = 1e-05
THETA = 100000.0
SCALE = HEAD_DIM ** (-0.5)
MASKED = -2e30
LOWEST = -1e30
FAR = 1 << 29
CHUNKS = 8
SLOTS = (0, 2, 1, 3)
TOP = 40
BF16 = jnp.bfloat16
F32 = jnp.float32
NN = (((1,), (0,)), ((), ()))
NT = (((1,), (1,)), ((), ()))
TN = (((0,), (0,)), ((), ()))
VMEM_LIMIT = 63 * 1024 * 1024
PER_US = 1.0e9


def dot(a, b, dims=NN):
    return lax.dot_general(a, b, dims, preferred_element_type=F32)


def call(kernel, out_shape, in_specs=None, cost=1.0, **kwargs):
    return pl.pallas_call(
        kernel,
        out_shape=out_shape,
        in_specs=in_specs,
        compiler_params=pltpu.CompilerParams(vmem_limit_bytes=VMEM_LIMIT),
        cost_estimate=pl.CostEstimate(
            flops=int(cost * PER_US), bytes_accessed=0, transcendentals=0
        ),
        **kwargs,
    )


def sds(shape, dtype):
    return jax.ShapeDtypeStruct(shape, dtype)


def lane_of(shape):
    return lax.broadcasted_iota(jnp.int32, shape, 1)


def swap_halves(tile):
    lane = lane_of(tile.shape) % HEAD_DIM
    return jnp.where(
        lane < HEAD_DIM // 2, pltpu.roll(tile, LANES - 32, 1), pltpu.roll(tile, 32, 1)
    )


def half_roll(tile):
    return pltpu.roll(tile, HEAD_DIM, 1)


def assemble(target, index, shards, rows):
    for code, ref in zip((0, 1, 2, 3), shards):
        start = pl.multiple_of((index ^ code) * rows, 16)
        target[pl.ds(start, rows), :] = ref[...]


def inverse_rms(rows):
    return lax.rsqrt(jnp.mean(rows * rows, axis=-1, keepdims=True) + EPSILON)


def qkv_kernel(index_ref, x_ref, w0, w1, w2, w3, cos_ref, sin_ref, w_ref, normed_ref, q_ref, kv_ref, two_ref):
    assemble(w_ref, index_ref[0], (w0, w1, w2, w3), w0.shape[0])
    width = w_ref.shape[1]
    gains = jnp.transpose(w_ref[:, width - LANES :].astype(F32))
    x = x_ref[...].astype(F32)
    normed = (x * inverse_rms(x) * gains[HEAD_DIM : HEAD_DIM + 1, :]).astype(BF16)
    normed_ref[...] = normed
    two_ref[...] = gains[HEAD_DIM + 1 : HEAD_DIM + 2, :]
    cosines, sines = cos_ref[...], sin_ref[...]
    lane = lane_of(cosines.shape)
    low = lane < HEAD_DIM
    cos_kv = jnp.where(low, cosines, 1.0)
    sin_kv = jnp.where(low, sines, 0.0)
    rows = kv_ref.shape[1]
    seqs = x.shape[0] // rows
    for g in range(KV_HEADS):
        tile = dot(normed, w_ref[:, g * LANES : (g + 1) * LANES])
        turned = (tile * cos_kv + swap_halves(tile) * sin_kv).astype(BF16)
        for r in range(seqs):
            kv_ref[r * KV_HEADS + g] = turned[r * rows : (r + 1) * rows]
    first = KV_HEADS * LANES
    lin = dot(normed, w_ref[:, first:])
    for p in range((HEADS + 1) // 2):
        tile = lin[:, p * LANES : (p + 1) * LANES]
        turned = (tile * cosines + swap_halves(tile) * sines) * SCALE
        for h in (2 * p, 2 * p + 1):
            if h < HEADS:
                own = turned if h % 2 == 0 else half_roll(turned)
                own = jnp.where(low, own, 0.0).astype(BF16)
                g, i = divmod(h, GROUP)
                for r in range(seqs):
                    q_ref[r * KV_HEADS + g, i * rows : (i + 1) * rows] = own[
                        r * rows : (r + 1) * rows
                    ]


def pair_places(info_ref, step, rows, axis):
    shape = (1, 2 * rows) if axis == 1 else (2 * rows, 1)
    at = lax.broadcasted_iota(jnp.int32, shape, axis)
    first, second = info_ref[1 + 2 * step], info_ref[2 + 2 * step]
    return jnp.where(at < rows, first + at, second + at - rows)


def query_places(info_ref, rows, axis):
    total = GROUP * rows
    shape = (1, total) if axis == 1 else (total, 1)
    at = lax.broadcasted_iota(jnp.int32, shape, axis)
    return info_ref[0] * rows + at % rows


def seen_of(key_places, q_places, start, end, diagonal):
    key_in = (key_places >= start) & (key_places < end)
    query_in = (q_places >= start) & (q_places < end)
    seen = jnp.where(key_in, key_places, FAR) <= jnp.where(query_in, q_places, -1)
    if diagonal:
        seen = seen | (key_places == q_places)
    return seen


def row_active(info_ref, step, rows, start, end):
    own = info_ref[0] * rows
    first, second = info_ref[1 + 2 * step], info_ref[2 + 2 * step]
    keys_in = ((first < end) & (first + rows > start)) | ((second < end) & (second + rows > start))
    return (own < end) & (own + rows > start) & keys_in & (jnp.minimum(first, second) <= own)


def attend_kernel(steps, diagonal, fresh, info_ref, q_ref, a_ref, b_ref, *refs):
    if fresh:
        max_ref, sum_ref = refs
    else:
        max_in, sum_in, max_ref, sum_ref = refs
    step = pl.program_id(0)
    rows = a_ref.shape[2]
    seqs = q_ref.shape[0] // KV_HEADS
    spans = 1 + 2 * steps

    @pl.when(step == 0)
    def _():
        if fresh:
            max_ref[...] = jnp.full_like(max_ref, LOWEST)
            sum_ref[...] = jnp.zeros_like(sum_ref)
        else:
            max_ref[...] = max_in[...]
            sum_ref[...] = sum_in[...]

    def one_seq(r, unused):
        start = info_ref[spans + r]
        end = info_ref[spans + seqs + r]

        def one_row():
            seen = seen_of(
                pair_places(info_ref, step, rows, 1),
                query_places(info_ref, rows, 0),
                start,
                end,
                diagonal,
            )
            for g in range(KV_HEADS):
                rg = r * KV_HEADS + g
                kv = jnp.concatenate([a_ref[0, rg], b_ref[0, rg]], axis=0)
                scores = jnp.where(seen, dot(q_ref[rg], kv, NT), MASKED)
                old = max_ref[rg]
                new = jnp.maximum(old, jnp.max(scores, axis=-1, keepdims=True))
                weights = jnp.exp(scores - jnp.concatenate([new, new], axis=1)).astype(BF16)
                ones = jnp.where(lane_of(kv.shape) < HEAD_DIM, jnp.ones_like(kv), kv)
                sum_ref[rg] = sum_ref[rg] * jnp.exp(old - new) + dot(weights, ones)
                max_ref[rg] = new

        if diagonal:
            one_row()
        else:
            pl.when(row_active(info_ref, step, rows, start, end))(one_row)
        return unused

    lax.fori_loop(0, seqs, one_seq, 0)


def attend(info, queries, a, b, carry, diagonal):
    steps = a.shape[0]
    tiles, total, _ = queries.shape
    rows = a.shape[2]
    whole = pl.BlockSpec((tiles, total, LANES), lambda i: (0, 0, 0))
    piece = pl.BlockSpec((1, tiles, rows, LANES), lambda i: (i, 0, 0, 0))
    return call(
        functools.partial(attend_kernel, steps, diagonal, carry is None),
        (sds((tiles, total, LANES), F32),) * 2,
        [pl.BlockSpec(memory_space=pltpu.SMEM), whole, piece, piece]
        + ([] if carry is None else [whole] * 2),
        cost=4.0 + 2.0 * steps,
        out_specs=(whole, whole),
        grid=(steps,),
    )(info, queries, a, b, *(carry or ()))


def attend_back_kernel(
    steps, diagonal, fresh, extra, info_ref, q_ref, d_ref, stat_ref, a_ref, b_ref, *refs
):
    if extra:
        refs[-1][...] = total_of(refs[-6][...], refs[-5][...])
        dq_ref, da_ref, db_ref = refs[-4:-1]
    else:
        dq_ref, da_ref, db_ref = refs[-3:]
    dq_in = refs[0]
    step = pl.program_id(0)
    rows = a_ref.shape[2]
    seqs = q_ref.shape[0] // KV_HEADS
    spans = 1 + 2 * steps

    @pl.when(step == 0)
    def _():
        dq_ref[...] = jnp.zeros_like(dq_ref) if fresh else dq_in[...]

    def one_seq(r, unused):
        start = info_ref[spans + r]
        end = info_ref[spans + seqs + r]

        def one_row():
            seen = seen_of(
                pair_places(info_ref, step, rows, 0),
                query_places(info_ref, rows, 1),
                start,
                end,
                diagonal,
            )
            for g in range(KV_HEADS):
                rg = r * KV_HEADS + g
                kv = jnp.concatenate([a_ref[0, rg], b_ref[0, rg]], axis=0)
                q, d = q_ref[rg], d_ref[rg]
                log_sum = stat_ref[rg, 0:1, :]
                delta = stat_ref[rg, 1:2, :]
                scores = jnp.where(seen, dot(kv, q, NT), MASKED)
                probs = jnp.exp(scores - log_sum)
                d_scores = (probs * (dot(kv, d, NT) - delta)).astype(BF16)
                grad = (dot(d_scores, q) + dot(probs.astype(BF16), d)).astype(BF16)
                da_ref[0, rg] = grad[:rows]
                db_ref[0, rg] = grad[rows:]
                dq_ref[rg] = dq_ref[rg] + dot(d_scores, kv, TN)

        if diagonal:
            one_row()
        else:
            active = row_active(info_ref, step, rows, start, end)
            pl.when(active)(one_row)

            @pl.when(jnp.logical_not(active))
            def _():
                for g in range(KV_HEADS):
                    rg = r * KV_HEADS + g
                    da_ref[0, rg] = jnp.zeros((rows, LANES), BF16)
                    db_ref[0, rg] = jnp.zeros((rows, LANES), BF16)

        return unused

    lax.fori_loop(0, seqs, one_seq, 0)


def attend_back(info, queries, d_out, stats, a, b, carry, diagonal, after=(), slow=True, extra=()):
    steps = a.shape[0]
    tiles, total, _ = queries.shape
    rows = a.shape[2]
    whole = pl.BlockSpec((tiles, total, LANES), lambda i: (0, 0, 0))
    stat = pl.BlockSpec(stats.shape, lambda i: (0, 0, 0))
    one = pl.BlockSpec(a.shape[1:], lambda i: (0, 0, 0))
    piece = pl.BlockSpec((1, tiles, rows, LANES), lambda i: (i, 0, 0, 0))
    return call(
        functools.partial(attend_back_kernel, steps, diagonal, carry is None, bool(extra)),
        (sds((tiles, total, LANES), F32), sds(a.shape, BF16), sds(b.shape, BF16))
        + ((sds(a.shape[1:], BF16),) if extra else ()),
        [pl.BlockSpec(memory_space=pltpu.SMEM), whole, whole, stat, piece, piece]
        + ([] if carry is None else [whole])
        + [pl.BlockSpec(memory_space=pl.ANY)] * len(after)
        + [one] * len(extra),
        cost=3.0 + 3.0 * steps if slow else 1.0,
        out_specs=(whole, piece, piece) + ((one,) if extra else ()),
        grid=(steps,),
    )(info, queries, d_out, stats, a, b, *(() if carry is None else (carry,)), *after, *extra)


def middle_kernel(
    index_ref,
    x_ref,
    cot_ref,
    gain_ref,
    max_ref,
    sum_ref,
    gu0,
    gu1,
    gu2,
    gu3,
    do0,
    do1,
    do2,
    do3,
    turned_ref,
    d_mid_ref,
    d_ref,
    stat_ref,
    keep_ref,
    send_ref,
    out_ref,
    w_gu,
    w_down,
    w_out,
    att_ref,
    n2_ref,
    dn2_ref,
    g_gu,
    g_down,
    g_out,
    slot_ref,
    chunk_ref,
):
    index = index_ref[0]
    dim = x_ref.shape[1]
    ff = w_down.shape[0]
    fd, fs = ff // 4, dim // 4
    assemble(w_gu, index, (gu0, gu1, gu2, gu3), fs)
    for code, ref in zip((0, 1, 2, 3), (do0, do1, do2, do3)):
        shard = index ^ code
        w_down[pl.ds(pl.multiple_of(shard * fd, 16), fd), :] = ref[0:fd, :]
        w_out[pl.ds(pl.multiple_of(shard * fs, 16), fs), :] = ref[fd:, :]
    tiles, total, _ = max_ref.shape
    seqs = tiles // KV_HEADS
    rows = total // GROUP
    low = lane_of((total, LANES)) < HEAD_DIM
    low_rows = low[:rows]
    outs = []
    for rg in range(tiles):
        sums = sum_ref[rg]
        turned = half_roll(sums)
        both = jnp.where(low, sums, turned)
        log_sum = max_ref[rg] + jnp.log(both)
        stat_ref[rg, 0:1, :] = jnp.transpose(log_sum)[0:1, :]
        normal = jnp.where(low, 0.0, sums / both)
        sum_ref_row = normal
        outs.append(sum_ref_row)
    for r in range(seqs):
        for p in range((HEADS + 1) // 2):
            g, i = divmod(2 * p, GROUP)
            tile = half_roll(outs[r * KV_HEADS + g][i * rows : (i + 1) * rows])
            if 2 * p + 1 < HEADS:
                g, i = divmod(2 * p + 1, GROUP)
                tile = jnp.where(
                    low_rows, tile, outs[r * KV_HEADS + g][i * rows : (i + 1) * rows]
                )
                att_ref[r * rows : (r + 1) * rows, p * LANES : (p + 1) * LANES] = tile.astype(BF16)
            else:
                att_ref[r * rows : (r + 1) * rows, p * LANES :] = tile[:, :HEAD_DIM].astype(BF16)
    att = att_ref[...]
    cot = cot_ref[...]
    mid = x_ref[...].astype(F32) + dot(att, w_out[...])
    inv = inverse_rms(mid)
    gain = gain_ref[...]
    n2 = (mid * inv * gain).astype(BF16)
    n2_ref[...] = n2
    out_ref[...] = mid
    dn2_ref[...] = jnp.zeros_like(dn2_ref)
    width = ff // 2

    def ff_step(i, carry):
        at = pl.multiple_of(i * width, width)
        cols, cols_up = pl.ds(at, width), pl.ds(pl.multiple_of(at + ff, width), width)
        n2 = n2_ref[...]
        w_g, w_u, w_d = w_gu[:, cols], w_gu[:, cols_up], w_down[cols, :]
        gate = dot(n2, w_g)
        up = dot(n2, w_u)
        sig = 1.0 / (1.0 + jnp.exp(-gate))
        silu = gate * sig
        hidden = (silu * up).astype(BF16)
        out_ref[...] += dot(hidden, w_d)
        d_hidden = dot(cot_ref[...], w_d, NT)
        d_gate = (d_hidden * up * sig * (1.0 + gate * (1.0 - sig))).astype(BF16)
        d_up = (d_hidden * silu).astype(BF16)
        g_down[cols, :] = dot(hidden, cot_ref[...], TN)
        g_gu[:, cols] = dot(n2, d_gate, TN)
        g_gu[:, cols_up] = dot(n2, d_up, TN)
        dn2_ref[...] += dot(d_gate, w_g, NT) + dot(d_up, w_u, NT)
        return carry

    lax.fori_loop(0, 2, ff_step, 0)
    for r in range(seqs):
        turned_ref[r] = jnp.transpose(out_ref[r * rows : (r + 1) * rows, :])
    dn2 = dn2_ref[...]
    scaled = dn2 * gain
    gain_grad = jnp.sum(dn2 * mid * inv, axis=0, keepdims=True)
    d_mid = (
        cot.astype(F32)
        + inv * scaled
        - mid * (inv * inv * inv) * jnp.mean(scaled * mid, axis=-1, keepdims=True)
    )
    d_mid_ref[...] = d_mid
    d_low = d_mid.astype(BF16)
    g_out[...] = dot(att, d_low, TN)
    d_att = dot(d_low, w_out[...], NT)
    for r in range(seqs):
        for p in range((HEADS + 1) // 2):
            stop = min((p + 1) * LANES, dim)
            tile = d_att[r * rows : (r + 1) * rows, p * LANES : stop]
            if stop - p * LANES < LANES:
                tile = jnp.concatenate([tile, jnp.zeros_like(tile)], axis=1)
            for h in (2 * p, 2 * p + 1):
                if h < HEADS:
                    own = half_roll(tile) if h % 2 == 0 else tile
                    own = jnp.where(low_rows, 0.0, own).astype(BF16)
                    g, i = divmod(h, GROUP)
                    d_ref[r * KV_HEADS + g, i * rows : (i + 1) * rows] = own
    for rg in range(tiles):
        prod = d_ref[rg].astype(F32) * outs[rg]
        stat_ref[rg, 1:2, :] = jnp.sum(jnp.transpose(prod), axis=0, keepdims=True)
    cols = 2 * ff // CHUNKS
    part = dim // CHUNKS
    for slot in range(4):
        shard = index ^ SLOTS[slot]
        to = keep_ref if slot < 2 else send_ref
        at = pl.ds(pl.multiple_of(shard * fs, 16), fs)
        slot_ref[0:fd, :] = g_down[pl.ds(pl.multiple_of(shard * fd, 16), fd), :]
        slot_ref[fd : fd + fs, :] = g_out[at, :]
        slot_ref[fd + fs :, :] = jnp.broadcast_to(gain_grad, (dim - fd - fs, dim))
        for c in range(CHUNKS):
            chunk_ref[:fs, :] = g_gu[at, c * cols : (c + 1) * cols]
            chunk_ref[fs : fs + part, :] = slot_ref[c * part : (c + 1) * part, :cols]
            top = slot_ref[c * part : c * part + TOP, cols:]
            rest = slot_ref[c * part + TOP : (c + 1) * part, cols:]
            fill = jnp.zeros((2 * TOP - part, dim - cols), F32)
            chunk_ref[fs + part :, :] = jnp.concatenate(
                [top, jnp.concatenate([rest, fill], axis=0)], axis=1
            )
            to[slot % 2, c] = chunk_ref[...].astype(BF16)


def middle(index, x, cot, gain, top, sums, gu, do):
    n, dim = x.shape
    tiles, total, _ = top.shape
    ff2 = gu[0].shape[1]
    ff = ff2 // 2
    chunk = (dim // 4 + dim // CHUNKS + TOP, ff2 // CHUNKS)
    pair = sds((2, CHUNKS) + chunk, BF16)
    vm = pl.BlockSpec(memory_space=pltpu.VMEM)
    return call(
        middle_kernel,
        (
            sds((tiles // KV_HEADS, dim, total // GROUP), F32),
            sds((n, dim), F32),
            sds((tiles, total, LANES), BF16),
            sds((tiles, 8, total), F32),
            pair,
            pair,
        ),
        [pl.BlockSpec(memory_space=pltpu.SMEM)] + [vm] * 13,
        cost=20.0,
        out_specs=(vm,) * 6,
        scratch_shapes=[
            pltpu.VMEM((n, dim), F32),
            pltpu.VMEM((dim, ff2), BF16),
            pltpu.VMEM((ff, dim), BF16),
            pltpu.VMEM((dim, dim), BF16),
            pltpu.VMEM((n, dim), BF16),
            pltpu.VMEM((n, dim), BF16),
            pltpu.VMEM((n, dim), F32),
            pltpu.VMEM((dim, ff2), F32),
            pltpu.VMEM((ff, dim), F32),
            pltpu.VMEM((dim, dim), F32),
            pltpu.VMEM((dim, dim), F32),
            pltpu.VMEM(chunk, F32),
        ],
    )(index, x, cot, gain, top, sums, *gu, *do)


def end_kernel(
    index_ref,
    x_ref,
    normed_ref,
    w_ref,
    cos_ref,
    sin_ref,
    dq_ref,
    d_mid_ref,
    *refs,
    parts,
):
    dkv_refs = refs[:parts]
    grad_ref, keep, send, lin_ref, g_ref = refs[-5:]
    index = index_ref[0]
    width = w_ref.shape[1]
    tiles, rows, _ = dkv_refs[0].shape
    seqs = tiles // KV_HEADS
    low = lane_of((rows, LANES)) < HEAD_DIM
    for r in range(seqs):
        at = slice(r * rows, (r + 1) * rows)
        cosines, sines = cos_ref[at, :], sin_ref[at, :]
        cos_kv = jnp.where(low, cosines, 1.0)
        sin_kv = jnp.where(low, sines, 0.0)
        for g in range(KV_HEADS):
            tile = dkv_refs[0][r * KV_HEADS + g].astype(F32)
            for ref in dkv_refs[1:]:
                tile = tile + ref[r * KV_HEADS + g].astype(F32)
            back = tile * cos_kv - swap_halves(tile) * sin_kv
            lin_ref[at, g * LANES : (g + 1) * LANES] = back.astype(BF16)
        first = KV_HEADS * LANES
        for p in range((HEADS + 1) // 2):
            backs = []
            for h in (2 * p, 2 * p + 1):
                if h < HEADS:
                    g, i = divmod(h, GROUP)
                    tile = dq_ref[r * KV_HEADS + g, i * rows : (i + 1) * rows]
                    backs.append((tile * cosines - swap_halves(tile) * sines) * SCALE)
                else:
                    backs.append(jnp.zeros((rows, LANES), F32))
            tile = jnp.where(low, backs[0], half_roll(backs[1]))
            lin_ref[at, first + p * LANES : first + (p + 1) * LANES] = tile.astype(BF16)
    lin = lin_ref[...]
    g_ref[...] = dot(normed_ref[...], lin, TN)
    d_normed = dot(lin, w_ref[...], NT)
    gains = jnp.transpose(w_ref[:, width - LANES :].astype(F32))
    gain = gains[HEAD_DIM : HEAD_DIM + 1, :]
    x = x_ref[...].astype(F32)
    inv = inverse_rms(x)
    scaled = d_normed * gain
    grad = (
        d_mid_ref[...]
        + inv * scaled
        - x * (inv * inv * inv) * jnp.mean(scaled * x, axis=-1, keepdims=True)
    )
    for r in range(seqs):
        grad_ref[r] = jnp.transpose(grad[r * rows : (r + 1) * rows, :])
    gain_grad = jnp.sum(d_normed * x * inv, axis=0, keepdims=True)
    dim = x.shape[1]
    fs = dim // 4
    for slot in range(4):
        start = (index ^ SLOTS[slot]) * fs
        to = keep if slot < 2 else send
        for c in range(CHUNKS):
            half, quarter = divmod(c, 4)
            size, cols = fs // 2, width // 4
            at = pl.ds(pl.multiple_of(start + half * size, 8), size)
            tile = g_ref[at, quarter * cols : (quarter + 1) * cols]
            if c == 3:
                pad = jnp.concatenate(
                    [gain_grad[:, k * HEAD_DIM : (k + 1) * HEAD_DIM] for k in range(HEADS)]
                    + [jnp.zeros((size - HEADS, HEAD_DIM), F32)],
                    axis=0,
                )
                pad = jnp.concatenate([tile[:, : cols - HEAD_DIM], pad], axis=1)
                tile = pad
            to[slot % 2, c] = tile.astype(BF16)


def finish(index, x, normed, w, cosines, sines, dq, dkv, d_mid, after):
    n, dim = x.shape
    width = w.shape[1]
    vm = pl.BlockSpec(memory_space=pltpu.VMEM)
    pair = sds((2, CHUNKS, dim // 8, width // 4), BF16)
    tiles = dkv[0].shape[0]
    return call(
        functools.partial(end_kernel, parts=len(dkv)),
        (sds((tiles // KV_HEADS, dim, dkv[0].shape[1]), F32), pair, pair),
        [pl.BlockSpec(memory_space=pltpu.SMEM)] + [vm] * (7 + len(dkv))
        + [pl.BlockSpec(memory_space=pl.ANY)] * len(after),
        cost=7.0,
        out_specs=(vm,) * 3,
        scratch_shapes=[pltpu.VMEM((n, width), BF16), pltpu.VMEM((dim, width), F32)],
    )(index, x, normed, w, cosines, sines, dq, d_mid, *dkv, *after)


def both_halves(place_ref, parts, d):
    near, far = parts[2 * d][...].astype(F32), parts[2 * d + 1][...].astype(F32)
    flag = place_ref[0] == 0
    return place_ref[1] ^ d, jnp.where(flag, near, far), jnp.where(flag, far, near)


def own_gain(place_ref, row, out_ref):
    size = out_ref.shape[1]
    rows = jnp.broadcast_to(row, (8, row.shape[1]))
    fill = -row.shape[1] % LANES
    rows = jnp.concatenate([rows, jnp.zeros((8, fill), F32)], axis=1)
    turned = pltpu.roll(rows, rows.shape[1] - place_ref[2] * size, 1)
    out_ref[...] = turned[0:1, :size]


def own_kernel(place_ref, *refs):
    parts = refs[:CHUNKS]
    gate_ref, up_ref, down_ref, out_ref, gain_ref, all_ref = refs[CHUNKS:]
    own_body(place_ref, parts, gate_ref, up_ref, down_ref, out_ref, gain_ref, all_ref)


def own_body(place_ref, parts, gate_ref, up_ref, down_ref, out_ref, gain_ref, all_ref):
    cols = parts[0].shape[1]
    fs, dim = out_ref.shape
    fd = down_ref.shape[1]
    part = dim // CHUNKS
    width = dim - cols
    for d in range(4):
        quarter, first, second = both_halves(place_ref, parts, d)
        at = pl.ds(pl.multiple_of(quarter * cols, LANES), cols)
        gate_ref[:, at] = first[:fs]
        up_ref[:, at] = second[:fs]
        for c, chunk in ((quarter, first), (4 + quarter, second)):
            start = c * part
            all_ref[pl.ds(pl.multiple_of(start, 8), part), :cols] = chunk[fs : fs + part]
            right = chunk[fs + part :]
            all_ref[pl.ds(pl.multiple_of(start, 8), TOP), cols:] = right[:, :width]
            all_ref[pl.ds(pl.multiple_of(start + TOP, 8), part - TOP), cols:] = right[
                : part - TOP, width:
            ]
    down_ref[...] = jnp.transpose(all_ref[:fd, :])
    out_ref[...] = all_ref[fd : fd + fs, :]
    own_gain(place_ref, all_ref[fd + fs : fd + fs + 1, :], gain_ref)


def own_q_kernel(place_ref, *refs):
    parts = refs[:CHUNKS]
    query_ref, key_ref, value_ref, gain_ref, all_ref = refs[CHUNKS:]
    part, cols = parts[0].shape
    for d in range(4):
        quarter, first, second = both_halves(place_ref, parts, d)
        at = pl.ds(pl.multiple_of(quarter * cols, LANES), cols)
        all_ref[:part, at] = first
        all_ref[part:, at] = second
    first = KV_HEADS * LANES
    for g in range(KV_HEADS):
        to = slice(g * HEAD_DIM, (g + 1) * HEAD_DIM)
        key_ref[:, to] = all_ref[:, g * LANES : g * LANES + HEAD_DIM]
        value_ref[:, to] = all_ref[:, g * LANES + HEAD_DIM : (g + 1) * LANES]
    query_ref[...] = all_ref[:, first : first + HEADS * HEAD_DIM]
    start = all_ref.shape[1] - HEAD_DIM
    row = jnp.concatenate([all_ref[k : k + 1, start:] for k in range(HEADS)], axis=1)
    own_gain(place_ref, row, gain_ref)


def own(kernel, place, outs, parts, scratch):
    vm = pl.BlockSpec(memory_space=pltpu.VMEM)
    return call(
        kernel,
        tuple(sds(shape, F32) for shape in outs),
        [pl.BlockSpec(memory_space=pltpu.SMEM)] + [vm] * CHUNKS,
        cost=3.0,
        out_specs=(vm,) * len(outs),
        scratch_shapes=[pltpu.VMEM(scratch, F32)],
    )(place, *parts)


def pack_kernel(q_ref, k_ref, v_ref, one_ref, two_ref, out_ref):
    for g in range(KV_HEADS):
        at = slice(g * HEAD_DIM, (g + 1) * HEAD_DIM)
        out_ref[:, g * LANES : g * LANES + HEAD_DIM] = k_ref[:, at]
        out_ref[:, g * LANES + HEAD_DIM : (g + 1) * LANES] = v_ref[:, at]
    first = KV_HEADS * LANES
    full = HEADS * HEAD_DIM
    out_ref[:, first : first + full] = q_ref[...]
    fs = q_ref.shape[0]
    row = lax.broadcasted_iota(jnp.int32, (LANES, fs), 0)
    gains = jnp.where(row == HEAD_DIM, one_ref[...].astype(F32)[None, :], 0.0)
    gains = jnp.where(row == HEAD_DIM + 1, two_ref[...].astype(F32)[None, :], gains)
    out_ref[:, first + full :] = jnp.transpose(gains)[:, HEAD_DIM:].astype(BF16)


def gu_pack_kernel(gate_ref, up_ref, unused, out_ref):
    ff = gate_ref.shape[1]
    out_ref[:, :ff] = gate_ref[...]
    out_ref[:, ff:] = up_ref[...]


def flip(x, axis, mask):
    n = lax.axis_size(axis)
    return lax.ppermute(x, axis, [(i, i ^ mask) for i in range(n)])


def gather_shards(own):
    across = flip(own, "fsdp", 2)
    return own, flip(own, "fsdp", 1), across, flip(across, "fsdp", 1)


def add(a, b):
    return (a.astype(F32) + b.astype(F32)).astype(BF16)


def total_of(*parts):
    total = parts[0].astype(F32)
    for part in parts[1:]:
        total = total + part.astype(F32)
    return total.astype(BF16)


def add_kernel(place_ref, *refs):
    refs[-1][...] = total_of(*(ref[...] for ref in refs[:-1]))


def core_kernel(place_ref, keep, got, out):
    out[...] = total_of(keep[0], got[0])


def y_kernel(place_ref, keep, got, far, mine, away):
    x_bit = place_ref[0]
    for c in range(4):
        here, there = 4 * x_bit + c, 4 * (1 - x_bit) + c
        mine[c] = total_of(keep[0, here], got[0, here], far[here])
        away[c] = total_of(keep[0, there], got[0, there], far[there])


def y_direct_kernel(place_ref, keep, got, far, *outs):
    for d in range(CHUNKS):
        c = 4 * (place_ref[0] ^ (d & 1)) + (place_ref[1] ^ (d >> 1))
        outs[d][...] = total_of(keep[0, c], got[0, c], far[c])


def x_kernel(place_ref, keep, got, *outs):
    for d in range(4):
        c = place_ref[1] ^ d
        outs[d][...] = total_of(keep[c], got[c])


def fuse(kernel, place, outs, ins, after=(), specs=None, out_specs=None, grid=None):
    vm = pl.BlockSpec(memory_space=pltpu.VMEM)
    count = 1 + len(ins)

    def body(*refs):
        kernel(*refs[:count], *refs[count + len(after) :])

    return call(
        body,
        tuple(sds(shape, BF16) for shape in outs),
        [pl.BlockSpec(memory_space=pltpu.SMEM)]
        + (specs or [vm] * len(ins))
        + [pl.BlockSpec(memory_space=pl.ANY)] * len(after),
        cost=1.5,
        out_specs=out_specs or (vm,) * len(outs),
        **({"grid": grid} if grid else {}),
    )(place, *ins, *after)


class Sum:
    def __init__(self, place, keep, send):
        self.place, self.shape = place, keep.shape[2:]
        self.parts = (keep, flip(send, "fsdp", 1))

    def core(self, *after):
        keep, got = self.parts
        two = (2,) + self.shape
        source = pl.BlockSpec((1,) + two, lambda i: (1, i, 0, 0))
        target = pl.BlockSpec(two, lambda i: (i, 0, 0))
        (away,) = fuse(
            core_kernel,
            self.place,
            [(CHUNKS,) + self.shape],
            self.parts,
            after,
            [source, source],
            (target,),
            (CHUNKS // 2,),
        )
        self.parts = (keep, got, flip(away, "fsdp", 2))
        return away

    def y_specs(self):
        first = pl.BlockSpec((1, CHUNKS) + self.shape, lambda i: (0, 0, 0, 0))
        return [first, first, pl.BlockSpec(memory_space=pltpu.VMEM)]

    def y(self, *after):
        shape = (4,) + self.shape
        keep, send = fuse(
            y_kernel, self.place, [shape] * 2, self.parts, after, self.y_specs(), None, (1,)
        )
        self.parts = (keep, flip(send, "ctx", 1))
        return keep

    def y_direct(self, *after):
        mine, *away = fuse(
            y_direct_kernel,
            self.place,
            [self.shape] * CHUNKS,
            self.parts,
            after,
            self.y_specs(),
            None,
            (1,),
        )
        self.parts = (mine, *(flip(away[d - 1], "ctx", d) for d in range(1, CHUNKS)))
        return mine

    def x(self, *after):
        mine, *away = fuse(x_kernel, self.place, [self.shape] * 4, self.parts, after)
        self.parts = (mine, *(flip(away[d - 1], "ctx", 2 * d) for d in (1, 2, 3)))
        return mine

    def z(self, *after):
        n = lax.axis_size("ctx")
        (mine,) = fuse(add_kernel, self.place, [self.shape], self.parts, after)
        for b in range(3, n.bit_length() - 1):
            (mine,) = fuse(
                add_kernel, self.place, [self.shape], (mine, flip(mine, "ctx", 1 << b))
            )
        self.parts = (mine, *(flip(mine, "ctx", d) for d in range(1, CHUNKS)))
        return mine


def send_down(x, levels):
    n = lax.axis_size("ctx")
    return lax.ppermute(x, "ctx", [(i, i - 2 * levels) for i in range(2 * levels, n)])


def local(
    tokens,
    cotangent,
    attn_gain,
    w_query,
    w_key,
    w_value,
    w_out,
    mlp_gain,
    w_gate,
    w_up,
    w_down,
    seq_lengths,
    seq_starts,
):
    seqs, rows, dim = tokens.shape
    n = seqs * rows
    n_ctx = lax.axis_size("ctx")
    me = lax.axis_index("ctx")
    index = lax.axis_index("fsdp").reshape(1).astype(jnp.int32)
    fs = w_query.shape[0]
    x = tokens.reshape(n, dim)
    cot = cotangent.reshape(n, dim)

    used = KV_HEADS * LANES + HEADS * HEAD_DIM + 2
    width = used - used % -LANES
    vm = pl.BlockSpec(memory_space=pltpu.VMEM)
    first = call(pack_kernel, sds((fs, width), BF16), [vm] * 5, cost=1.5, out_specs=vm)(
        w_query, w_key, w_value, attn_gain, mlp_gain
    )
    first_shards = gather_shards(first)
    gu_shards = gather_shards(
        call(
            gu_pack_kernel,
            sds((fs, 2 * w_gate.shape[1]), BF16),
            [vm, vm, pl.BlockSpec(memory_space=pl.ANY)],
            cost=1.5,
            out_specs=vm,
        )(w_gate, w_up, first_shards[2])
    )
    do_shards = gather_shards(jnp.concatenate([w_down, w_out], axis=0))

    places = me * rows + jnp.arange(rows, dtype=jnp.int32)
    positions = (places[None, :] - seq_starts[:, None]).astype(F32)
    frequency = THETA ** (-(2.0 * jnp.arange(HEAD_DIM // 2, dtype=F32)) / HEAD_DIM)
    angles = (positions[:, :, None] * frequency).reshape(n, HEAD_DIM // 2)
    cos, sin = jnp.cos(angles), jnp.sin(angles)
    cosines = jnp.concatenate([cos] * 4, axis=1)
    sines = jnp.concatenate([-sin, sin] * 2, axis=1)

    tiles = seqs * KV_HEADS
    weights, normed, queries, kv, gain_two = call(
        qkv_kernel,
        (
            sds((dim, width), BF16),
            sds((n, dim), BF16),
            sds((tiles, GROUP * rows, LANES), BF16),
            sds((tiles, rows, LANES), BF16),
            sds((1, dim), F32),
        ),
        [pl.BlockSpec(memory_space=pltpu.SMEM)] + [vm] * 7,
        cost=4.0,
        out_specs=(vm,) * 5,
    )(index, x, *first_shards, cosines, sines)

    spans = [seq_starts.astype(jnp.int32), (seq_starts + seq_lengths).astype(jnp.int32)]

    def info_of(bases):
        return jnp.concatenate([me.reshape(1).astype(jnp.int32), bases.astype(jnp.int32)] + spans)

    x_bit = me % 2
    if n_ctx <= 8 and n_ctx % 2 == 0:
        levels = n_ctx // 2
        up = [(i, i + 2) for i in range(n_ctx - 2)]
        down = [(i + 2, i) for i in range(n_ctx - 2)]
        pieces = []
        piece = kv
        for k in range(levels):
            other = flip(piece, "ctx", 1)
            pair = (me // 2 - k) * 2
            bases = jnp.stack([pair + x_bit, pair + 1 - x_bit]) * rows
            bases = jnp.where(pair >= 0, bases, FAR)
            pieces.append((bases, piece[None], other[None]))
            if k + 1 < levels:
                piece = lax.ppermute(piece, "ctx", up)
        carry = None
        for k in range(levels):
            bases, a, b = pieces[k]
            carry = attend(info_of(bases), queries, a, b, carry, k == 0)
    else:
        every = lax.all_gather(kv, "ctx", axis=0)
        info = info_of(jnp.arange(n_ctx, dtype=jnp.int32) * rows)
        carry = attend(info, queries, every[0::2], every[1::2], None, True)

    result, d_mid, d_out, stats, keep_mlp, send_mlp = middle(
        index, x, cot, gain_two, carry[0], carry[1], gu_shards, do_shards
    )

    place = jnp.stack([me & 1, (me >> 1) & 3, index[0]]).astype(jnp.int32)
    mlp = Sum(place, keep_mlp, send_mlp)
    if n_ctx <= 8 and n_ctx % 2 == 0:
        dq, last = None, ()
        dkv, partials = [], []
        for k in reversed(range(levels)):
            bases, a, b = pieces[k]
            extra = partials[0][1:] if k < levels - 2 else ()
            dq, da, db, *both = attend_back(
                info_of(bases),
                queries,
                d_out,
                stats,
                a,
                b,
                dq,
                k == 0,
                last,
                k == levels - 1,
                extra,
            )
            if extra:
                dkv.append(send_down(both[0], partials.pop(0)[0]))
            partials.append((k, da[0], flip(db[0], "ctx", 1)))
            last = (mlp.core(dq),) if k == levels - 1 else ()
        while len(partials) > 1:
            far, near, other = partials.pop(0)
            (both,) = fuse(add_kernel, place, [near.shape], (near, other), (dq,))
            dkv.append(send_down(both, far))
            last = (both,)
        dkv = [partials[0][1], partials[0][2]] + dkv
        last = (mlp.y(*last),)
    else:
        dq, da, db = attend_back(
            info, queries, d_out, stats, every[0::2], every[1::2], None, True
        )
        partial = jnp.stack([da, db], axis=1).reshape((n_ctx,) + da.shape[1:])
        dkv = [lax.psum_scatter(partial, "ctx", scatter_dimension=0, tiled=False)]
        mlp.core(dq)
        last = (mlp.y(dq),)

    ff = w_gate.shape[1]
    fd = w_down.shape[0]
    input_grad, keep_q, send_q = finish(
        index, x, normed, weights, cosines, sines, dq, dkv, d_mid, last
    )
    qkv = Sum(place, keep_q, send_q)
    step = mlp.x(keep_q)
    step = qkv.core(step)
    step = mlp.z(step)
    step = qkv.y_direct(step)
    step = qkv.z(step)
    grad_gate, grad_up, grad_down, grad_out, gain_two_grad = own(
        own_kernel,
        place,
        [(fs, ff), (fs, ff), (dim, fd), (fs, dim), (1, fs)],
        mlp.parts,
        (dim, dim),
    )
    grad_down = grad_down.T
    kv_width = KV_HEADS * HEAD_DIM
    grad_query, grad_key, grad_value, gain_one_grad = own(
        own_q_kernel,
        place,
        [(fs, HEADS * HEAD_DIM), (fs, kv_width), (fs, kv_width), (1, fs)],
        qkv.parts,
        (fs, width),
    )
    grad_mlp_gain = gain_two_grad.reshape(fs)
    grad_attn_gain = gain_one_grad.reshape(fs)
    return (
        jnp.transpose(result, (0, 2, 1)),
        jnp.transpose(input_grad, (0, 2, 1)),
        grad_attn_gain,
        grad_query,
        grad_key,
        grad_value,
        grad_out,
        grad_mlp_gain,
        grad_gate,
        grad_up,
        grad_down,
    )


def solution(mesh):
    rows3 = P("fsdp", "ctx", None)
    mat = P("fsdp", None)
    vec = P("fsdp")
    return jax.shard_map(
        local,
        mesh=mesh,
        in_specs=(rows3, rows3, vec, mat, mat, mat, mat, vec, mat, mat, mat, vec, vec),
        out_specs=(rows3, rows3, vec, mat, mat, mat, mat, vec, mat, mat, mat),
        check_vma=False,
    )
```

profile of v0, /device:TPU:0, one launch (start us, length us, event | category | flops | bytes accessed | tf_op | source)
XLA Modules:
  0.0 254.9 jit_solution(7370382775330666227)
XLA Ops:
  0.7 2.0 shard_map.212.w0
  2.6 3.0 %collective-permute-start.1 = (bf16[144,1024]{1,0:T(8,128)(2,1)}, bf16[144,1024]{1,0:T(8,128)(2,1)S(1)}, u32[]{:S(2)}, u32[]{:S(2)}) collective-permute-start(bf16[144,1024]{1,0:T(8,128)(2,1)} %shard_map.212.w0), channel_id=1, source_target_pairs={{0,2},{1,3},{2,0},{3,1},{4,6},{5,7},{6,4},{7,5},{8,10},{9,11},{10,... | collective-permute-start | bytes 884744 | tf_op jit(solution)/shard_map/ppermute | solution.py:684
  8.6 5.1 %collective-permute-done.1.w2.unused = bf16[144,1024]{1,0:T(8,128)(2,1)S(1)} collective-permute-done((bf16[144,1024]{1,0:T(8,128)(2,1)}, bf16[144,1024]{1,0:T(8,128)(2,1)S(1)}, u32[]{:S(2)}, u32[]{:S(2)}) %collective-permute-start.1) | collective-permute-done | bytes 294944 | tf_op jit(solution)/shard_map/ppermute | solution.py:684
  17.0 4.0 %shard_map.213 = (bf16[576,1024]{1,0:T(8,128)(2,1)}, bf16[384,576]{1,0:T(8,128)(2,1)}, bf16[9,384,128]{2,1,0:T(8,128)(2,1)}, bf16[9,128,128]{2,1,0:T(8,128)(2,1)}, f32[1,576]{1,0:T(1,128)}) custom-call(s32[1]{0:T(128)} %bitcast.index_ref, bf16[384,576]{1,0:T(8,128)(2,1)} %bitcast.41, bf16[144,1024]{1,0:T(8,128)(2,1)} %shard_map.212.w0, ...), custom_call_target="tpu_custom_call" | custom-call | flops 4000000000 | tf_op jit(solution)/shard_map/pallas_call | solution.py:871
  21.1 2.0 collective-permute-start.9
  23.1 4.2 %collective-permute-start.3 = (bf16[9,128,128]{2,1,0:T(8,128)(2,1)}, bf16[9,128,128]{2,1,0:T(8,128)(2,1)}, u32[]{:S(2)}, u32[]{:S(2)}) collective-permute-start(bf16[9,128,128]{2,1,0:T(8,128)(2,1)} %get-tuple-element.72), channel_id=1, source_target_pairs={{0,8},{4,12},{8,16},{12,20},{16,24},{20,28},{1,9},{5,13},{9,17},{1... | collective-permute-start | bytes 884744 | tf_op jit(solution)/shard_map/ppermute | solution.py:904
  27.4 2.0 copy.28
  30.0 2.1 shard_map.218.gu0
  34.2 5.0 %collective-permute-start.4 = (bf16[9,128,128]{2,1,0:T(8,128)(2,1)}, bf16[9,128,128]{2,1,0:T(8,128)(2,1)}, u32[]{:S(2)}, u32[]{:S(2)}) collective-permute-start(bf16[9,128,128]{2,1,0:T(8,128)(2,1)} %collective-permute-done.3), channel_id=1, source_target_pairs={{0,8},{4,12},{8,16},{12,20},{16,24},{20,28},{1,9},{5,13},{9,17},{1... | collective-permute-start | bytes 884744 | tf_op jit(solution)/shard_map/ppermute | solution.py:904
  39.2 5.4 %shard_map.214 = (f32[9,384,128]{2,1,0:T(8,128)}, f32[9,384,128]{2,1,0:T(8,128)}) custom-call(s32[9]{0:T(128)} %get-tuple-element.132.info_ref, bf16[9,384,128]{2,1,0:T(8,128)(2,1)} %get-tuple-element.71.q_ref, bf16[1,9,128,128]{3,2,1,0:T(8,128)(2,1)} %bitcast.45, bf16[1,9,128,128]{3,2,1,0:T(8,128)(2,1)} %bitcast.47), custom_call_target="tpu_custom_call" | custom-call | flops 6000000000 | tf_op jit(solution)/shard_map/pallas_call | solution.py:203
  46.0 4.9 %collective-permute-start.5 = (bf16[9,128,128]{2,1,0:T(8,128)(2,1)}, bf16[9,128,128]{2,1,0:T(8,128)(2,1)}, u32[]{:S(2)}, u32[]{:S(2)}) collective-permute-start(bf16[9,128,128]{2,1,0:T(8,128)(2,1)} %collective-permute-done.4), channel_id=1, source_target_pairs={{0,8},{4,12},{8,16},{12,20},{16,24},{20,28},{1,9},{5,13},{9,17},{1... | collective-permute-start | bytes 884744 | tf_op jit(solution)/shard_map/ppermute | solution.py:904
  50.9 4.5 %shard_map.215 = (f32[9,384,128]{2,1,0:T(8,128)}, f32[9,384,128]{2,1,0:T(8,128)}) custom-call(s32[9]{0:T(128)} %get-tuple-element.134.info_ref, bf16[9,384,128]{2,1,0:T(8,128)(2,1)} %get-tuple-element.71.q_ref, bf16[1,9,128,128]{3,2,1,0:T(8,128)(2,1)} %bitcast.15.a_ref, bf16[1,9,128,128]{3,2,1,0:T(8,128)(2,1)} %bitcast.16.b_ref, ...), custom_call_target="tpu_custom_call" | custom-call | flops 6000000000 | tf_op jit(solution)/shard_map/pallas_call | solution.py:203
  56.7 4.6 %shard_map.216 = (f32[9,384,128]{2,1,0:T(8,128)}, f32[9,384,128]{2,1,0:T(8,128)}) custom-call(s32[9]{0:T(128)} %get-tuple-element.133.info_ref, bf16[9,384,128]{2,1,0:T(8,128)(2,1)} %get-tuple-element.71.q_ref, bf16[1,9,128,128]{3,2,1,0:T(8,128)(2,1)} %bitcast.11.a_ref, bf16[1,9,128,128]{3,2,1,0:T(8,128)(2,1)} %bitcast.51, ...), custom_call_target="tpu_custom_call" | custom-call | flops 6000000000 | tf_op jit(solution)/shard_map/pallas_call | solution.py:203
  61.3 4.5 %collective-permute-done.6 = bf16[9,128,128]{2,1,0:T(8,128)(2,1)} collective-permute-done((bf16[9,128,128]{2,1,0:T(8,128)(2,1)}, bf16[9,128,128]{2,1,0:T(8,128)(2,1)}, u32[]{:S(2)}, u32[]{:S(2)}) %collective-permute-start.6) | collective-permute-done | bytes 294944 | tf_op jit(solution)/shard_map/ppermute | solution.py:684
  65.7 4.6 %shard_map.217 = (f32[9,384,128]{2,1,0:T(8,128)}, f32[9,384,128]{2,1,0:T(8,128)}) custom-call(s32[9]{0:T(128)} %get-tuple-element.135.info_ref, bf16[9,384,128]{2,1,0:T(8,128)(2,1)} %get-tuple-element.71.q_ref, bf16[1,9,128,128]{3,2,1,0:T(8,128)(2,1)} %bitcast.7.a_ref, bf16[1,9,128,128]{3,2,1,0:T(8,128)(2,1)} %bitcast.8.b_ref, ...), custom_call_target="tpu_custom_call" | custom-call | flops 6000000000 | tf_op jit(solution)/shard_map/pallas_call | solution.py:203
  70.3 21.4 %shard_map.219 = (f32[3,576,128]{2,1,0:T(8,128)}, f32[384,576]{1,0:T(8,128)}, bf16[9,384,128]{2,1,0:T(8,128)(2,1)}, f32[9,8,384]{2,1,0:T(8,128)}, bf16[2,8,256,3...) custom-call(s32[1]{0:T(128)} %bitcast.index_ref, bf16[384,576]{1,0:T(8,128)(2,1)} %bitcast.42, ...), custom_call_target="tpu_custom_call" | custom-call | flops 20000000000 | tf_op jit(solution)/shard_map/pallas_call | solution.py:458
  92.4 3.3 %shard_map.220 = (f32[9,384,128]{2,1,0:T(8,128)}, bf16[1,9,128,128]{3,2,1,0:T(8,128)(2,1)}, bf16[1,9,128,128]{3,2,1,0:T(8,128)(2,1)}) custom-call(s32[9]{0:T(128)} %get-tuple-element.135.info_ref, bf16[9,384,128]{2,1,0:T(8,128)(2,1)} %get-tuple-element.71.q_ref, bf16[9,384,128]{2,1,0:T(8,128)(2,1)} %get-tuple-element.84.d_ref, ...), custom_call_target="tpu_custom_call" | custom-call | flops 6000000000 | tf_op jit(solution)/shard_map/pallas_call | solution.py:284
  95.7 2.1 collective-permute-done.16.refs_2_
  97.8 4.1 %shard_map.221.refs_1_ = bf16[8,256,384]{2,1,0:T(8,128)(2,1)} custom-call(s32[3]{0:T(128)} %pad_add_fusion.refs_0_.place_ref, bf16[2,8,256,384]{3,2,1,0:T(8,128)(2,1)} %get-tuple-element.87.refs_1_, bf16[2,8,256,384]{3,2,1,0:T(8,128)(2,1)} %collective-permute-done.16.refs_2_, f32[9,384,128]{2,1,0:T(8,128)} %get-tuple-element.86.refs_3_.refs_0_), custom_call_target="tpu_custom_call" | custom-call | flops 1500000000 | tf_op jit(solution)/shard_map/pallas_call | solution.py:738
  103.9 3.9 %shard_map.222 = (f32[9,384,128]{2,1,0:T(8,128)}, bf16[1,9,128,128]{3,2,1,0:T(8,128)(2,1)}, bf16[1,9,128,128]{3,2,1,0:T(8,128)(2,1)}) custom-call(s32[9]{0:T(128)} %get-tuple-element.133.info_ref, bf16[9,384,128]{2,1,0:T(8,128)(2,1)} %get-tuple-element.71.q_ref, bf16[9,384,128]{2,1,0:T(8,128)(2,1)} %get-tuple-element.84.d_ref, ...), custom_call_target="tpu_custom_call" | custom-call | flops 1000000000 | tf_op jit(solution)/shard_map/pallas_call | solution.py:284
  109.3 4.0 %collective-permute-done.17.refs_2_ = bf16[9,128,128]{2,1,0:T(8,128)(2,1)S(1)} collective-permute-done((bf16[9,128,128]{2,1,0:T(8,128)(2,1)S(1)}, bf16[9,128,128]{2,1,0:T(8,128)(2,1)S(1)}, u32[]{:S(2)}, u32[]{:S(2)}) %collective-permute-start.17) | collective-permute-done | bytes 294944 | tf_op jit(solution)/shard_map/ppermute | solution.py:684
  114.0 4.1 %shard_map.223 = (f32[9,384,128]{2,1,0:T(8,128)}, bf16[1,9,128,128]{3,2,1,0:T(8,128)(2,1)}, bf16[1,9,128,128]{3,2,1,0:T(8,128)(2,1)}, bf16[9,128,128]{2,1,0:T(8,128)(2,1)}) custom-call(s32[9]{0:T(128)} %get-tuple-element.134.info_ref, bf16[9,384,128]{2,1,0:T(8,128)(2,1)} %get-tuple-element.71.q_ref, bf16[9,384,128]{2,1,0:T(8,128)(2,1)} %get-tuple-element.84.d_ref, ...), custom_call_target="tpu_custom_call" | custom-call | flops 1000000000 | tf_op jit(solution)/shard_map/pallas_call | solution.py:284
  120.4 7.8 %shard_map.224 = (f32[9,384,128]{2,1,0:T(8,128)}, bf16[1,9,128,128]{3,2,1,0:T(8,128)(2,1)}, bf16[1,9,128,128]{3,2,1,0:T(8,128)(2,1)}, bf16[9,128,128]{2,1,0:T(8,128)(2,1)}) custom-call(s32[9]{0:T(128)} %get-tuple-element.132.info_ref, bf16[9,384,128]{2,1,0:T(8,128)(2,1)} %get-tuple-element.71.q_ref, bf16[9,384,128]{2,1,0:T(8,128)(2,1)} %get-tuple-element.84.d_ref, ...), custom_call_target="tpu_custom_call" | custom-call | flops 1000000000 | tf_op jit(solution)/shard_map/pallas_call | solution.py:284
  132.0 1.8 shard_map.225.refs_4_
  135.3 3.2 %collective-permute-done.24.refs_3_ = bf16[8,256,384]{2,1,0:T(8,128)(2,1)} collective-permute-done((bf16[8,256,384]{2,1,0:T(8,128)(2,1)}, bf16[8,256,384]{2,1,0:T(8,128)(2,1)}, u32[]{:S(2)}, u32[]{:S(2)}) %collective-permute-start.24) | collective-permute-done | bytes 1572896 | tf_op jit(solution)/shard_map/ppermute | solution.py:684
  138.6 4.0 %shard_map.226 = (bf16[4,256,384]{2,1,0:T(8,128)(2,1)}, bf16[4,256,384]{2,1,0:T(8,128)(2,1)}) custom-call(s32[3]{0:T(128)} %pad_add_fusion.refs_0_.place_ref, bf16[2,8,256,384]{3,2,1,0:T(8,128)(2,1)} %get-tuple-element.87.refs_1_, bf16[2,8,256,384]{3,2,1,0:T(8,128)(2,1)} %collective-permute-done.16.refs_2_, ...), custom_call_target="tpu_custom_call" | custom-call | flops 1500000000 | tf_op jit(solution)/shard_map/pallas_call | solution.py:738
  143.1 7.6 %collective-permute-done.21.refs_3_ = bf16[9,128,128]{2,1,0:T(8,128)(2,1)} collective-permute-done((bf16[9,128,128]{2,1,0:T(8,128)(2,1)}, bf16[9,128,128]{2,1,0:T(8,128)(2,1)}, u32[]{:S(2)}, u32[]{:S(2)}) %collective-permute-start.21) | collective-permute-done | bytes 294944 | tf_op jit(solution)/shard_map/ppermute | solution.py:817
  152.0 7.3 %shard_map.227 = (f32[3,576,128]{2,1,0:T(8,128)}, bf16[2,8,72,256]{3,2,1,0:T(8,128)(2,1)}, bf16[2,8,72,256]{3,2,1,0:T(8,128)(2,1)}) custom-call(s32[1]{0:T(128)} %bitcast.index_ref, bf16[384,576]{1,0:T(8,128)(2,1)} %bitcast.43, bf16[384,576]{1,0:T(8,128)(2,1)} %get-tuple-element.82.normed_ref, bf16[576,1024]{1,0:T(8,128)(2,1)} %get-tuple-element.83.w_ref, ...), custom_call_target="tpu_custom_call" | custom-call | flops 7000000000 | tf_op jit(solution)/shard_map/pallas_call | solution.py:573
  159.3 2.3 collective-permute-done.26.refs_2_
  162.4 2.3 shard_map.228
  164.8 3.0 %collective-permute-start.28 = (bf16[256,384]{1,0:T(8,128)(2,1)}, bf16[256,384]{1,0:T(8,128)(2,1)S(1)}, u32[]{:S(2)}, u32[]{:S(2)}) collective-permute-start(bf16[256,384]{1,0:T(8,128)(2,1)} %get-tuple-element.109), channel_id=1, source_target_pairs={{0,8},{4,12},{8,0},{12,4},{16,24},{20,28},{24,16},{28,20},{1,9},{5... | collective-permute-start | bytes 589832 | tf_op jit(solution)/shard_map/ppermute | solution.py:684
  167.7 3.3 %collective-permute-start.29 = (bf16[256,384]{1,0:T(8,128)(2,1)}, bf16[256,384]{1,0:T(8,128)(2,1)S(1)}, u32[]{:S(2)}, u32[]{:S(2)}) collective-permute-start(bf16[256,384]{1,0:T(8,128)(2,1)} %get-tuple-element.110), channel_id=1, source_target_pairs={{0,16},{4,20},{8,24},{12,28},{16,0},{20,4},{24,8},{28,12},{1,17},{... | collective-permute-start | bytes 589832 | tf_op jit(solution)/shard_map/ppermute | solution.py:684
  171.0 3.2 %shard_map.229.refs_5_ = bf16[8,72,256]{2,1,0:T(8,128)(2,1)} custom-call(s32[3]{0:T(128)} %pad_add_fusion.refs_0_.place_ref, bf16[2,8,72,256]{3,2,1,0:T(8,128)(2,1)} %get-tuple-element.105.refs_3_.refs_1_, bf16[2,8,72,256]{3,2,1,0:T(8,128)(2,1)} %collective-permute-done.25.refs_2_, bf16[256,384]{1,0:T(8,128)(2,1)} %get-tuple-element.108.refs_3_.refs_1_), custom_call_target="tpu_custom_call" | custom-call | flops 1500000000 | tf_op jit(solution)/shard_map/pallas_call | solution.py:738
  175.9 9.3 %collective-permute-done.29.refs_3_ = bf16[256,384]{1,0:T(8,128)(2,1)S(1)} collective-permute-done((bf16[256,384]{1,0:T(8,128)(2,1)}, bf16[256,384]{1,0:T(8,128)(2,1)S(1)}, u32[]{:S(2)}, u32[]{:S(2)}) %collective-permute-start.29) | collective-permute-done | bytes 196640 | tf_op jit(solution)/shard_map/ppermute | solution.py:684
  186.5 2.0 shard_map.230.refs_4_.refs_0_
  189.2 1.9 shard_map.231
  191.4 3.3 %collective-permute-start.32 = (bf16[72,256]{1,0:T(8,128)(2,1)}, bf16[72,256]{1,0:T(8,128)(2,1)S(1)}, u32[]{:S(2)}, u32[]{:S(2)}) collective-permute-start(bf16[72,256]{1,0:T(8,128)(2,1)} %get-tuple-element.114), channel_id=1, source_target_pairs={{0,8},{4,12},{8,0},{12,4},{16,24},{20,28},{24,16},{28,20},{1,9},{5... | collective-permute-start | bytes 110600 | tf_op jit(solution)/shard_map/ppermute | solution.py:684
  200.3 3.2 %collective-permute-start.37 = (bf16[72,256]{1,0:T(8,128)(2,1)}, bf16[72,256]{1,0:T(8,128)(2,1)S(1)}, u32[]{:S(2)}, u32[]{:S(2)}) collective-permute-start(bf16[72,256]{1,0:T(8,128)(2,1)} %get-tuple-element.119), channel_id=1, source_target_pairs={{0,28},{4,24},{8,20},{12,16},{16,12},{20,8},{24,4},{28,0},{1,29},{... | collective-permute-start | bytes 110600 | tf_op jit(solution)/shard_map/ppermute | solution.py:684
  205.1 2.3 collective-permute-start.50
  209.7 3.3 %collective-permute-start.44 = (bf16[72,256]{1,0:T(8,128)(2,1)}, bf16[72,256]{1,0:T(8,128)(2,1)S(1)}, u32[]{:S(2)}, u32[]{:S(2)}) collective-permute-start(bf16[72,256]{1,0:T(8,128)(2,1)} %shard_map.232.refs_0_), channel_id=1, source_target_pairs={{0,28},{4,24},{8,20},{12,16},{16,12},{20,8},{24,4},{28,0},{1,29},{... | collective-permute-start | bytes 110600 | tf_op jit(solution)/shard_map/ppermute | solution.py:684
  214.5 9.1 %collective-permute-start.42 = (bf16[72,256]{1,0:T(8,128)(2,1)}, bf16[72,256]{1,0:T(8,128)(2,1)S(1)}, u32[]{:S(2)}, u32[]{:S(2)}) collective-permute-start(bf16[72,256]{1,0:T(8,128)(2,1)} %shard_map.232.refs_0_), channel_id=1, source_target_pairs={{0,20},{4,16},{8,28},{12,24},{16,4},{20,0},{24,12},{28,8},{1,21},{... | collective-permute-start | bytes 110600 | tf_op jit(solution)/shard_map/ppermute | solution.py:684
  223.6 3.9 %collective-permute-start.41 = (bf16[72,256]{1,0:T(8,128)(2,1)}, bf16[72,256]{1,0:T(8,128)(2,1)S(1)}, u32[]{:S(2)}, u32[]{:S(2)}) collective-permute-start(bf16[72,256]{1,0:T(8,128)(2,1)} %shard_map.232.refs_0_), channel_id=1, source_target_pairs={{0,16},{4,20},{8,24},{12,28},{16,0},{20,4},{24,8},{28,12},{1,17},{... | collective-permute-start | bytes 110600 | tf_op jit(solution)/shard_map/ppermute | solution.py:684
  228.0 1.9 collective-permute-start.39
  234.0 2.0 collective-permute-start.48
  239.6 1.9 shard_map.233
  241.5 5.2 %collective-permute-done.49.refs_5_ = bf16[256,384]{1,0:T(8,128)(2,1)S(1)} collective-permute-done((bf16[256,384]{1,0:T(8,128)(2,1)S(1)}, bf16[256,384]{1,0:T(8,128)(2,1)S(1)}, u32[]{:S(2)}, u32[]{:S(2)}) %collective-permute-start.49) | collective-permute-done | bytes 196640 | tf_op jit(solution)/shard_map/ppermute | solution.py:684
  246.7 3.4 %collective-permute-done.48.refs_4_ = bf16[256,384]{1,0:T(8,128)(2,1)} collective-permute-done((bf16[256,384]{1,0:T(8,128)(2,1)S(1)}, bf16[256,384]{1,0:T(8,128)(2,1)}, u32[]{:S(2)}, u32[]{:S(2)}) %collective-permute-start.48) | collective-permute-done | bytes 196640 | tf_op jit(solution)/shard_map/ppermute | solution.py:684
  251.4 3.6 %shard_map.234 = (f32[144,1536]{1,0:T(8,128)}, f32[144,1536]{1,0:T(8,128)}, f32[576,384]{1,0:T(8,128)}, f32[144,576]{1,0:T(8,128)}, f32[1,144]{1,0:T(1,128)}) custom-call(s32[3]{0:T(128)} %pad_add_fusion.refs_0_.place_ref, bf16[256,384]{1,0:T(8,128)(2,1)} %shard_map.230.refs_4_.refs_0_, bf16[256,384]{1,0:T(8,128)(2,1)} %collective-permute-done.45.refs_1_, ...), custom_call_target="tpu_custom_call" | custom-call | flops 3000000000 | tf_op jit(solution)/shard_map/pallas_call | solution.py:651
  (169 shorter events, 51.3 us)
Async XLA Ops:
  2.6 11.1 %collective-permute-start.1 = (bf16[144,1024]{1,0:T(8,128)(2,1)}, bf16[144,1024]{1,0:T(8,128)(2,1)S(1)}, u32[]{:S(2)}, u32[]{:S(2)}) collective-permute-start(bf16[144,1024]{1,0:T(8,128)(2,1)} %shard_map.212.w0), channel_id=1, source_target_pairs={{0,2},{1,3},{2,0},{3,1},{4,6},{5,7},{6,4},{7,5},{8,10},{9,11},{10,... | collective-permute-start | bytes 884744 | tf_op jit(solution)/shard_map/ppermute | solution.py:684
  5.7 9.9 %collective-permute-start = (bf16[144,1024]{1,0:T(8,128)(2,1)}, bf16[144,1024]{1,0:T(8,128)(2,1)S(1)}, u32[]{:S(2)}, u32[]{:S(2)}) collective-permute-start(bf16[144,1024]{1,0:T(8,128)(2,1)} %shard_map.212.w0), channel_id=1, source_target_pairs={{0,1},{1,0},{2,3},{3,2},{4,5},{5,4},{6,7},{7,6},{8,9},{9,8},{10,11... | collective-permute-start | bytes 884744 | tf_op jit(solution)/shard_map/ppermute | solution.py:684
  6.0 49.4 %collective-permute-start.14 = (bf16[528,576]{1,0:T(8,128)(2,1)S(1)}, bf16[528,576]{1,0:T(8,128)(2,1)}, u32[]{:S(2)}, u32[]{:S(2)}) collective-permute-start(bf16[528,576]{1,0:T(8,128)(2,1)S(1)} %pad_maximum_fusion.do0), channel_id=1, source_target_pairs={{0,2},{1,3},{2,0},{3,1},{4,6},{5,7},{6,4},{7,5},{8,10},{9,11},{10,... | collective-permute-start | bytes 1824776 | tf_op jit(solution)/shard_map/ppermute | solution.py:684
  6.2 64.1 %collective-permute-start.13 = (bf16[528,576]{1,0:T(8,128)(2,1)S(1)}, bf16[528,576]{1,0:T(8,128)(2,1)}, u32[]{:S(2)}, u32[]{:S(2)}) collective-permute-start(bf16[528,576]{1,0:T(8,128)(2,1)S(1)} %pad_maximum_fusion.do0), channel_id=1, source_target_pairs={{0,1},{1,0},{2,3},{3,2},{4,5},{5,4},{6,7},{7,6},{8,9},{9,8},{10,11... | collective-permute-start | bytes 1824776 | tf_op jit(solution)/shard_map/ppermute | solution.py:684
  21.1 13.1 %collective-permute-start.9 = (bf16[9,128,128]{2,1,0:T(8,128)(2,1)}, bf16[9,128,128]{2,1,0:T(8,128)(2,1)S(1)}, u32[]{:S(2)}, u32[]{:S(2)}) collective-permute-start(bf16[9,128,128]{2,1,0:T(8,128)(2,1)} %get-tuple-element.72), channel_id=1, source_target_pairs={{0,4},{4,0},{8,12},{12,8},{16,20},{20,16},{24,28},{28,24},{1,5},{5... | collective-permute-start | bytes 884744 | tf_op jit(solution)/shard_map/ppermute | solution.py:684
  23.1 10.6 %collective-permute-start.3 = (bf16[9,128,128]{2,1,0:T(8,128)(2,1)}, bf16[9,128,128]{2,1,0:T(8,128)(2,1)}, u32[]{:S(2)}, u32[]{:S(2)}) collective-permute-start(bf16[9,128,128]{2,1,0:T(8,128)(2,1)} %get-tuple-element.72), channel_id=1, source_target_pairs={{0,8},{4,12},{8,16},{12,20},{16,24},{20,28},{1,9},{5,13},{9,17},{1... | collective-permute-start | bytes 884744 | tf_op jit(solution)/shard_map/ppermute | solution.py:904
  32.1 23.4 %collective-permute-start.11 = (bf16[144,3072]{1,0:T(8,128)(2,1)}, bf16[144,3072]{1,0:T(8,128)(2,1)}, u32[]{:S(2)}, u32[]{:S(2)}) collective-permute-start(bf16[144,3072]{1,0:T(8,128)(2,1)} %shard_map.218.gu0), channel_id=1, source_target_pairs={{0,2},{1,3},{2,0},{3,1},{4,6},{5,7},{6,4},{7,5},{8,10},{9,11},{10,... | collective-permute-start | bytes 2654216 | tf_op jit(solution)/shard_map/ppermute | solution.py:684
  33.6 12.4 %collective-permute-start.8 = (bf16[9,128,128]{2,1,0:T(8,128)(2,1)}, bf16[9,128,128]{2,1,0:T(8,128)(2,1)}, u32[]{:S(2)}, u32[]{:S(2)}) collective-permute-start(bf16[9,128,128]{2,1,0:T(8,128)(2,1)} %collective-permute-done.3), channel_id=1, source_target_pairs={{0,4},{4,0},{8,12},{12,8},{16,20},{20,16},{24,28},{28,24},{1,5},{5... | collective-permute-start | bytes 884744 | tf_op jit(solution)/shard_map/ppermute | solution.py:684
  34.2 10.4 %collective-permute-start.4 = (bf16[9,128,128]{2,1,0:T(8,128)(2,1)}, bf16[9,128,128]{2,1,0:T(8,128)(2,1)}, u32[]{:S(2)}, u32[]{:S(2)}) collective-permute-start(bf16[9,128,128]{2,1,0:T(8,128)(2,1)} %collective-permute-done.3), channel_id=1, source_target_pairs={{0,8},{4,12},{8,16},{12,20},{16,24},{20,28},{1,9},{5,13},{9,17},{1... | collective-permute-start | bytes 884744 | tf_op jit(solution)/shard_map/ppermute | solution.py:904
  44.5 11.4 %collective-permute-start.7 = (bf16[9,128,128]{2,1,0:T(8,128)(2,1)}, bf16[9,128,128]{2,1,0:T(8,128)(2,1)S(1)}, u32[]{:S(2)}, u32[]{:S(2)}) collective-permute-start(bf16[9,128,128]{2,1,0:T(8,128)(2,1)} %collective-permute-done.4), channel_id=1, source_target_pairs={{0,4},{4,0},{8,12},{12,8},{16,20},{20,16},{24,28},{28,24},{1,5},{5... | collective-permute-start | bytes 884744 | tf_op jit(solution)/shard_map/ppermute | solution.py:684
  46.0 10.0 %collective-permute-start.5 = (bf16[9,128,128]{2,1,0:T(8,128)(2,1)}, bf16[9,128,128]{2,1,0:T(8,128)(2,1)}, u32[]{:S(2)}, u32[]{:S(2)}) collective-permute-start(bf16[9,128,128]{2,1,0:T(8,128)(2,1)} %collective-permute-done.4), channel_id=1, source_target_pairs={{0,8},{4,12},{8,16},{12,20},{16,24},{20,28},{1,9},{5,13},{9,17},{1... | collective-permute-start | bytes 884744 | tf_op jit(solution)/shard_map/ppermute | solution.py:904
  55.5 14.8 %collective-permute-start.10 = (bf16[144,3072]{1,0:T(8,128)(2,1)}, bf16[144,3072]{1,0:T(8,128)(2,1)}, u32[]{:S(2)}, u32[]{:S(2)}) collective-permute-start(bf16[144,3072]{1,0:T(8,128)(2,1)} %shard_map.218.gu0), channel_id=1, source_target_pairs={{0,1},{1,0},{2,3},{3,2},{4,5},{5,4},{6,7},{7,6},{8,9},{9,8},{10,11... | collective-permute-start | bytes 2654216 | tf_op jit(solution)/shard_map/ppermute | solution.py:684
  55.5 14.8 %collective-permute-start.15 = (bf16[528,576]{1,0:T(8,128)(2,1)}, bf16[528,576]{1,0:T(8,128)(2,1)}, u32[]{:S(2)}, u32[]{:S(2)}) collective-permute-start(bf16[528,576]{1,0:T(8,128)(2,1)} %collective-permute-done.14.do2), channel_id=1, source_target_pairs={{0,1},{1,0},{2,3},{3,2},{4,5},{5,4},{6,7},{7,6},{8,9},{9,8},{10,11... | collective-permute-start | bytes 1824776 | tf_op jit(solution)/shard_map/ppermute | solution.py:684
  56.0 14.3 %collective-permute-start.12 = (bf16[144,3072]{1,0:T(8,128)(2,1)}, bf16[144,3072]{1,0:T(8,128)(2,1)}, u32[]{:S(2)}, u32[]{:S(2)}) collective-permute-start(bf16[144,3072]{1,0:T(8,128)(2,1)} %collective-permute-done.11.gu2), channel_id=1, source_target_pairs={{0,1},{1,0},{2,3},{3,2},{4,5},{5,4},{6,7},{7,6},{8,9},{9,8},{10,11... | collective-permute-start | bytes 2654216 | tf_op jit(solution)/shard_map/ppermute | solution.py:684
  56.1 9.7 %collective-permute-start.6 = (bf16[9,128,128]{2,1,0:T(8,128)(2,1)}, bf16[9,128,128]{2,1,0:T(8,128)(2,1)}, u32[]{:S(2)}, u32[]{:S(2)}) collective-permute-start(bf16[9,128,128]{2,1,0:T(8,128)(2,1)} %collective-permute-done.5), channel_id=1, source_target_pairs={{0,4},{4,0},{8,12},{12,8},{16,20},{20,16},{24,28},{28,24},{1,5},{5... | collective-permute-start | bytes 884744 | tf_op jit(solution)/shard_map/ppermute | solution.py:684
  101.8 36.8 %collective-permute-start.24 = (bf16[8,256,384]{2,1,0:T(8,128)(2,1)}, bf16[8,256,384]{2,1,0:T(8,128)(2,1)}, u32[]{:S(2)}, u32[]{:S(2)}) collective-permute-start(bf16[8,256,384]{2,1,0:T(8,128)(2,1)} %shard_map.221.refs_1_), channel_id=1, source_target_pairs={{0,2},{1,3},{2,0},{3,1},{4,6},{5,7},{6,4},{7,5},{8,10},{9,11},{10,... | collective-permute-start | bytes 4718600 | tf_op jit(solution)/shard_map/ppermute | solution.py:684
  103.4 9.9 %collective-permute-start.17 = (bf16[9,128,128]{2,1,0:T(8,128)(2,1)S(1)}, bf16[9,128,128]{2,1,0:T(8,128)(2,1)S(1)}, u32[]{:S(2)}, u32[]{:S(2)}) collective-permute-start(bf16[9,128,128]{2,1,0:T(8,128)(2,1)S(1)} %bitcast.58), channel_id=1, source_target_pairs={{0,4},{4,0},{8,12},{12,8},{16,20},{20,16},{24,28},{28,24},{1,5},{5... | collective-permute-start | bytes 884744 | tf_op jit(solution)/shard_map/ppermute | solution.py:684
  107.8 11.9 %collective-permute-start.18 = (bf16[9,128,128]{2,1,0:T(8,128)(2,1)}, bf16[9,128,128]{2,1,0:T(8,128)(2,1)S(1)}, u32[]{:S(2)}, u32[]{:S(2)}) collective-permute-start(bf16[9,128,128]{2,1,0:T(8,128)(2,1)} %bitcast.57), channel_id=1, source_target_pairs={{0,4},{4,0},{8,12},{12,8},{16,20},{20,16},{24,28},{28,24},{1,5},{5... | collective-permute-start | bytes 884744 | tf_op jit(solution)/shard_map/ppermute | solution.py:684
  118.1 13.1 %collective-permute-start.22 = (bf16[9,128,128]{2,1,0:T(8,128)(2,1)}, bf16[9,128,128]{2,1,0:T(8,128)(2,1)S(1)}, u32[]{:S(2)}, u32[]{:S(2)}) collective-permute-start(bf16[9,128,128]{2,1,0:T(8,128)(2,1)} %bitcast.56), channel_id=1, source_target_pairs={{0,4},{4,0},{8,12},{12,8},{16,20},{20,16},{24,28},{28,24},{1,5},{5... | collective-permute-start | bytes 884744 | tf_op jit(solution)/shard_map/ppermute | solution.py:684
  118.4 24.7 %collective-permute-start.20 = (bf16[9,128,128]{2,1,0:T(8,128)(2,1)}, bf16[9,128,128]{2,1,0:T(8,128)(2,1)}, u32[]{:S(2)}, u32[]{:S(2)}) collective-permute-start(bf16[9,128,128]{2,1,0:T(8,128)(2,1)} %get-tuple-element.99), channel_id=1, source_target_pairs={{24,0},{28,4},{25,1},{29,5},{26,2},{30,6},{27,3},{31,7}} | collective-permute-start | bytes 884744 | tf_op jit(solution)/shard_map/ppermute | solution.py:817
  128.2 14.9 %collective-permute-start.19 = (bf16[9,128,128]{2,1,0:T(8,128)(2,1)}, bf16[9,128,128]{2,1,0:T(8,128)(2,1)}, u32[]{:S(2)}, u32[]{:S(2)}) collective-permute-start(bf16[9,128,128]{2,1,0:T(8,128)(2,1)} %bitcast.54), channel_id=1, source_target_pairs={{0,4},{4,0},{8,12},{12,8},{16,20},{20,16},{24,28},{28,24},{1,5},{5... | collective-permute-start | bytes 884744 | tf_op jit(solution)/shard_map/ppermute | solution.py:684
  129.9 20.8 %collective-permute-start.21 = (bf16[9,128,128]{2,1,0:T(8,128)(2,1)}, bf16[9,128,128]{2,1,0:T(8,128)(2,1)}, u32[]{:S(2)}, u32[]{:S(2)}) collective-permute-start(bf16[9,128,128]{2,1,0:T(8,128)(2,1)} %get-tuple-element.100), channel_id=1, source_target_pairs={{16,0},{20,4},{24,8},{28,12},{17,1},{21,5},{25,9},{29,13},{18,2},{... | collective-permute-start | bytes 884744 | tf_op jit(solution)/shard_map/ppermute | solution.py:817
  133.8 18.2 %collective-permute-start.23 = (bf16[9,128,128]{2,1,0:T(8,128)(2,1)}, bf16[9,128,128]{2,1,0:T(8,128)(2,1)}, u32[]{:S(2)}, u32[]{:S(2)}) collective-permute-start(bf16[9,128,128]{2,1,0:T(8,128)(2,1)} %shard_map.225.refs_4_), channel_id=1, source_target_pairs={{8,0},{12,4},{16,8},{20,12},{24,16},{28,20},{9,1},{13,5},{17,9},{2... | collective-permute-start | bytes 884744 | tf_op jit(solution)/shard_map/ppermute | solution.py:817
  142.6 19.0 %collective-permute-start.26 = (bf16[4,256,384]{2,1,0:T(8,128)(2,1)}, bf16[4,256,384]{2,1,0:T(8,128)(2,1)S(1)}, u32[]{:S(2)}, u32[]{:S(2)}) collective-permute-start(bf16[4,256,384]{2,1,0:T(8,128)(2,1)} %get-tuple-element.107), channel_id=1, source_target_pairs={{0,4},{4,0},{8,12},{12,8},{16,20},{20,16},{24,28},{28,24},{1,5},{5... | collective-permute-start | bytes 2359304 | tf_op jit(solution)/shard_map/ppermute | solution.py:684
  159.2 11.8 %collective-permute-start.25 = (bf16[2,8,72,256]{3,2,1,0:T(8,128)(2,1)}, bf16[2,8,72,256]{3,2,1,0:T(8,128)(2,1)}, u32[]{:S(2)}, u32[]{:S(2)}) collective-permute-start(bf16[2,8,72,256]{3,2,1,0:T(8,128)(2,1)} %get-tuple-element.106), channel_id=1, source_target_pairs={{0,1},{1,0},{2,3},{3,2},{4,5},{5,4},{6,7},{7,6},{8,9},{9,8},{10,11... | collective-permute-start | bytes 1769480 | tf_op jit(solution)/shard_map/ppermute | solution.py:684
  164.8 11.1 %collective-permute-start.28 = (bf16[256,384]{1,0:T(8,128)(2,1)}, bf16[256,384]{1,0:T(8,128)(2,1)S(1)}, u32[]{:S(2)}, u32[]{:S(2)}) collective-permute-start(bf16[256,384]{1,0:T(8,128)(2,1)} %get-tuple-element.109), channel_id=1, source_target_pairs={{0,8},{4,12},{8,0},{12,4},{16,24},{20,28},{24,16},{28,20},{1,9},{5... | collective-permute-start | bytes 589832 | tf_op jit(solution)/shard_map/ppermute | solution.py:684
  167.7 17.5 %collective-permute-start.29 = (bf16[256,384]{1,0:T(8,128)(2,1)}, bf16[256,384]{1,0:T(8,128)(2,1)S(1)}, u32[]{:S(2)}, u32[]{:S(2)}) collective-permute-start(bf16[256,384]{1,0:T(8,128)(2,1)} %get-tuple-element.110), channel_id=1, source_target_pairs={{0,16},{4,20},{8,24},{12,28},{16,0},{20,4},{24,8},{28,12},{1,17},{... | collective-permute-start | bytes 589832 | tf_op jit(solution)/shard_map/ppermute | solution.py:684
  171.0 14.1 %collective-permute-start.30 = (bf16[256,384]{1,0:T(8,128)(2,1)}, bf16[256,384]{1,0:T(8,128)(2,1)S(1)}, u32[]{:S(2)}, u32[]{:S(2)}) collective-permute-start(bf16[256,384]{1,0:T(8,128)(2,1)} %get-tuple-element.111), channel_id=1, source_target_pairs={{0,24},{4,28},{8,16},{12,20},{16,8},{20,12},{24,0},{28,4},{1,25},{... | collective-permute-start | bytes 589832 | tf_op jit(solution)/shard_map/ppermute | solution.py:684
  174.2 14.3 %collective-permute-start.27 = (bf16[8,72,256]{2,1,0:T(8,128)(2,1)}, bf16[8,72,256]{2,1,0:T(8,128)(2,1)S(1)}, u32[]{:S(2)}, u32[]{:S(2)}) collective-permute-start(bf16[8,72,256]{2,1,0:T(8,128)(2,1)} %shard_map.229.refs_5_), channel_id=1, source_target_pairs={{0,2},{1,3},{2,0},{3,1},{4,6},{5,7},{6,4},{7,5},{8,10},{9,11},{10,... | collective-permute-start | bytes 884744 | tf_op jit(solution)/shard_map/ppermute | solution.py:684
  191.1 7.6 %collective-permute-start.31 = (bf16[72,256]{1,0:T(8,128)(2,1)}, bf16[72,256]{1,0:T(8,128)(2,1)S(1)}, u32[]{:S(2)}, u32[]{:S(2)}) collective-permute-start(bf16[72,256]{1,0:T(8,128)(2,1)} %get-tuple-element.113), channel_id=1, source_target_pairs={{0,4},{4,0},{8,12},{12,8},{16,20},{20,16},{24,28},{28,24},{1,5},{5... | collective-permute-start | bytes 110600 | tf_op jit(solution)/shard_map/ppermute | solution.py:684
  191.4 8.9 %collective-permute-start.32 = (bf16[72,256]{1,0:T(8,128)(2,1)}, bf16[72,256]{1,0:T(8,128)(2,1)S(1)}, u32[]{:S(2)}, u32[]{:S(2)}) collective-permute-start(bf16[72,256]{1,0:T(8,128)(2,1)} %get-tuple-element.114), channel_id=1, source_target_pairs={{0,8},{4,12},{8,0},{12,4},{16,24},{20,28},{24,16},{28,20},{1,9},{5... | collective-permute-start | bytes 110600 | tf_op jit(solution)/shard_map/ppermute | solution.py:684
  194.7 8.8 %collective-permute-start.33 = (bf16[72,256]{1,0:T(8,128)(2,1)}, bf16[72,256]{1,0:T(8,128)(2,1)S(1)}, u32[]{:S(2)}, u32[]{:S(2)}) collective-permute-start(bf16[72,256]{1,0:T(8,128)(2,1)} %get-tuple-element.115), channel_id=1, source_target_pairs={{0,12},{4,8},{8,4},{12,0},{16,28},{20,24},{24,20},{28,16},{1,13},{... | collective-permute-start | bytes 110600 | tf_op jit(solution)/shard_map/ppermute | solution.py:684
  195.8 9.3 %collective-permute-start.34 = (bf16[72,256]{1,0:T(8,128)(2,1)}, bf16[72,256]{1,0:T(8,128)(2,1)S(1)}, u32[]{:S(2)}, u32[]{:S(2)}) collective-permute-start(bf16[72,256]{1,0:T(8,128)(2,1)} %get-tuple-element.116), channel_id=1, source_target_pairs={{0,16},{4,20},{8,24},{12,28},{16,0},{20,4},{24,8},{28,12},{1,17},{... | collective-permute-start | bytes 110600 | tf_op jit(solution)/shard_map/ppermute | solution.py:684
  197.6 9.8 %collective-permute-start.35 = (bf16[72,256]{1,0:T(8,128)(2,1)}, bf16[72,256]{1,0:T(8,128)(2,1)S(1)}, u32[]{:S(2)}, u32[]{:S(2)}) collective-permute-start(bf16[72,256]{1,0:T(8,128)(2,1)} %get-tuple-element.117), channel_id=1, source_target_pairs={{0,20},{4,16},{8,28},{12,24},{16,4},{20,0},{24,12},{28,8},{1,21},{... | collective-permute-start | bytes 110600 | tf_op jit(solution)/shard_map/ppermute | solution.py:684
  198.8 8.6 %collective-permute-start.36 = (bf16[72,256]{1,0:T(8,128)(2,1)}, bf16[72,256]{1,0:T(8,128)(2,1)S(1)}, u32[]{:S(2)}, u32[]{:S(2)}) collective-permute-start(bf16[72,256]{1,0:T(8,128)(2,1)} %get-tuple-element.118), channel_id=1, source_target_pairs={{0,24},{4,28},{8,16},{12,20},{16,8},{20,12},{24,0},{28,4},{1,25},{... | collective-permute-start | bytes 110600 | tf_op jit(solution)/shard_map/ppermute | solution.py:684
  200.3 7.3 %collective-permute-start.37 = (bf16[72,256]{1,0:T(8,128)(2,1)}, bf16[72,256]{1,0:T(8,128)(2,1)S(1)}, u32[]{:S(2)}, u32[]{:S(2)}) collective-permute-start(bf16[72,256]{1,0:T(8,128)(2,1)} %get-tuple-element.119), channel_id=1, source_target_pairs={{0,28},{4,24},{8,20},{12,16},{16,12},{20,8},{24,4},{28,0},{1,29},{... | collective-permute-start | bytes 110600 | tf_op jit(solution)/shard_map/ppermute | solution.py:684
  203.5 33.8 %collective-permute-start.51 = (bf16[256,384]{1,0:T(8,128)(2,1)S(1)}, bf16[256,384]{1,0:T(8,128)(2,1)S(1)}, u32[]{:S(2)}, u32[]{:S(2)}) collective-permute-start(bf16[256,384]{1,0:T(8,128)(2,1)S(1)} %copy-done.16), channel_id=1, source_target_pairs={{0,28},{4,24},{8,20},{12,16},{16,12},{20,8},{24,4},{28,0},{1,29},{... | collective-permute-start | bytes 589832 | tf_op jit(solution)/shard_map/ppermute | solution.py:684
  205.1 33.5 %collective-permute-start.50 = (bf16[256,384]{1,0:T(8,128)(2,1)S(1)}, bf16[256,384]{1,0:T(8,128)(2,1)S(1)}, u32[]{:S(2)}, u32[]{:S(2)}) collective-permute-start(bf16[256,384]{1,0:T(8,128)(2,1)S(1)} %copy-done.16), channel_id=1, source_target_pairs={{0,24},{4,28},{8,16},{12,20},{16,8},{20,12},{24,0},{28,4},{1,25},{... | collective-permute-start | bytes 589832 | tf_op jit(solution)/shard_map/ppermute | solution.py:684
  209.7 13.8 %collective-permute-start.44 = (bf16[72,256]{1,0:T(8,128)(2,1)}, bf16[72,256]{1,0:T(8,128)(2,1)S(1)}, u32[]{:S(2)}, u32[]{:S(2)}) collective-permute-start(bf16[72,256]{1,0:T(8,128)(2,1)} %shard_map.232.refs_0_), channel_id=1, source_target_pairs={{0,28},{4,24},{8,20},{12,16},{16,12},{20,8},{24,4},{28,0},{1,29},{... | collective-permute-start | bytes 110600 | tf_op jit(solution)/shard_map/ppermute | solution.py:684
  213.0 14.5 %collective-permute-start.43 = (bf16[72,256]{1,0:T(8,128)(2,1)}, bf16[72,256]{1,0:T(8,128)(2,1)S(1)}, u32[]{:S(2)}, u32[]{:S(2)}) collective-permute-start(bf16[72,256]{1,0:T(8,128)(2,1)} %shard_map.232.refs_0_), channel_id=1, source_target_pairs={{0,24},{4,28},{8,16},{12,20},{16,8},{20,12},{24,0},{28,4},{1,25},{... | collective-permute-start | bytes 110600 | tf_op jit(solution)/shard_map/ppermute | solution.py:684
  214.5 13.6 %collective-permute-start.42 = (bf16[72,256]{1,0:T(8,128)(2,1)}, bf16[72,256]{1,0:T(8,128)(2,1)S(1)}, u32[]{:S(2)}, u32[]{:S(2)}) collective-permute-start(bf16[72,256]{1,0:T(8,128)(2,1)} %shard_map.232.refs_0_), channel_id=1, source_target_pairs={{0,20},{4,16},{8,28},{12,24},{16,4},{20,0},{24,12},{28,8},{1,21},{... | collective-permute-start | bytes 110600 | tf_op jit(solution)/shard_map/ppermute | solution.py:684
  223.6 6.4 %collective-permute-start.41 = (bf16[72,256]{1,0:T(8,128)(2,1)}, bf16[72,256]{1,0:T(8,128)(2,1)S(1)}, u32[]{:S(2)}, u32[]{:S(2)}) collective-permute-start(bf16[72,256]{1,0:T(8,128)(2,1)} %shard_map.232.refs_0_), channel_id=1, source_target_pairs={{0,16},{4,20},{8,24},{12,28},{16,0},{20,4},{24,8},{28,12},{1,17},{... | collective-permute-start | bytes 110600 | tf_op jit(solution)/shard_map/ppermute | solution.py:684
  229.9 6.1 %collective-permute-start.38 = (bf16[72,256]{1,0:T(8,128)(2,1)}, bf16[72,256]{1,0:T(8,128)(2,1)S(1)}, u32[]{:S(2)}, u32[]{:S(2)}) collective-permute-start(bf16[72,256]{1,0:T(8,128)(2,1)} %shard_map.232.refs_0_), channel_id=1, source_target_pairs={{0,4},{4,0},{8,12},{12,8},{16,20},{20,16},{24,28},{28,24},{1,5},{5... | collective-permute-start | bytes 110600 | tf_op jit(solution)/shard_map/ppermute | solution.py:684
  232.7 14.0 %collective-permute-start.49 = (bf16[256,384]{1,0:T(8,128)(2,1)S(1)}, bf16[256,384]{1,0:T(8,128)(2,1)S(1)}, u32[]{:S(2)}, u32[]{:S(2)}) collective-permute-start(bf16[256,384]{1,0:T(8,128)(2,1)S(1)} %copy-done.16), channel_id=1, source_target_pairs={{0,20},{4,16},{8,28},{12,24},{16,4},{20,0},{24,12},{28,8},{1,21},{... | collective-permute-start | bytes 589832 | tf_op jit(solution)/shard_map/ppermute | solution.py:684
  234.0 16.0 %collective-permute-start.48 = (bf16[256,384]{1,0:T(8,128)(2,1)S(1)}, bf16[256,384]{1,0:T(8,128)(2,1)}, u32[]{:S(2)}, u32[]{:S(2)}) collective-permute-start(bf16[256,384]{1,0:T(8,128)(2,1)S(1)} %copy-done.16), channel_id=1, source_target_pairs={{0,16},{4,20},{8,24},{12,28},{16,0},{20,4},{24,8},{28,12},{1,17},{... | collective-permute-start | bytes 589832 | tf_op jit(solution)/shard_map/ppermute | solution.py:684
  236.0 14.0 %collective-permute-start.47 = (bf16[256,384]{1,0:T(8,128)(2,1)S(1)}, bf16[256,384]{1,0:T(8,128)(2,1)}, u32[]{:S(2)}, u32[]{:S(2)}) collective-permute-start(bf16[256,384]{1,0:T(8,128)(2,1)S(1)} %copy-done.16), channel_id=1, source_target_pairs={{0,12},{4,8},{8,4},{12,0},{16,28},{20,24},{24,20},{28,16},{1,13},{... | collective-permute-start | bytes 589832 | tf_op jit(solution)/shard_map/ppermute | solution.py:684
  237.3 14.0 %collective-permute-start.46 = (bf16[256,384]{1,0:T(8,128)(2,1)S(1)}, bf16[256,384]{1,0:T(8,128)(2,1)}, u32[]{:S(2)}, u32[]{:S(2)}) collective-permute-start(bf16[256,384]{1,0:T(8,128)(2,1)S(1)} %copy-done.16), channel_id=1, source_target_pairs={{0,8},{4,12},{8,0},{12,4},{16,24},{20,28},{24,16},{28,20},{1,9},{5... | collective-permute-start | bytes 589832 | tf_op jit(solution)/shard_map/ppermute | solution.py:684
  238.6 12.8 %collective-permute-start.45 = (bf16[256,384]{1,0:T(8,128)(2,1)S(1)}, bf16[256,384]{1,0:T(8,128)(2,1)}, u32[]{:S(2)}, u32[]{:S(2)}) collective-permute-start(bf16[256,384]{1,0:T(8,128)(2,1)S(1)} %copy-done.16), channel_id=1, source_target_pairs={{0,4},{4,0},{8,12},{12,8},{16,20},{20,16},{24,28},{28,24},{1,5},{5... | collective-permute-start | bytes 589832 | tf_op jit(solution)/shard_map/ppermute | solution.py:684
  (41 other events, 193.6 us)
where the time goes:
time: 255 us
  Pallas kernels  101 us (40%)
  starting transfers between devices  86.6 us (34%)
  waiting for transfers between devices  51.4 us (20%)
  local copies, waits for them, and re-layouts  10.6 us (4%)
  other arithmetic  4.13 us (2%)
    ppermute x46, starting transfers between devices, flip(): return lax.ppermute(x, axis, [(i, i ^ mask) for i in range(n)])  68.4 us
    ppermute x46, waiting for transfers between devices, flip(): return lax.ppermute(x, axis, [(i, i ^ mask) for i in range(n)])  42.5 us
    pallas_call x1, Pallas kernels, middle(): call(middle_kernel, (sds((tiles // KV_HEADS, dim, total // GROUP), F32),...  21.4 us
    pallas_call x8, Pallas kernels, fuse(): call(body, tuple((sds(shape, BF16) for shape in outs)), [pl.BlockSpec(mem...  20.9 us
    pallas_call x4, Pallas kernels, attend_back(): call(functools.partial(attend_back_kernel, steps, diagonal, carry is None...  19.1 us
    pallas_call x4, Pallas kernels, attend(): call(functools.partial(attend_kernel, steps, diagonal, carry is None), (s...  19 us
    ppermute x3, starting transfers between devices, local(): piece = lax.ppermute(piece, 'ctx', up)  14.1 us
    unnamed x77, local copies, waits for them, and re-layouts  10.5 us
  transfers between devices with their start and end apart: 52, of which 16 were waited for; matrix products, arithmetic and copies ran while one was open for 3% of the time, Pallas kernels for 27%

commit v1 on v0

--- a/solution.py
+++ b/solution.py
@@ -77,11 +77,15 @@
     return lax.rsqrt(jnp.mean(rows * rows, axis=-1, keepdims=True) + EPSILON)
 
 
-def qkv_kernel(index_ref, x_ref, w0, w1, w2, w3, cos_ref, sin_ref, w_ref, normed_ref, q_ref, kv_ref, two_ref):
+def qkv_kernel(index_ref, x_ref, w0, w1, w2, w3, cos_ref, sin_ref, w_ref, normed_ref, q_ref, kv_ref, two_ref, rows_ref):
     assemble(w_ref, index_ref[0], (w0, w1, w2, w3), w0.shape[0])
     width = w_ref.shape[1]
     gains = jnp.transpose(w_ref[:, width - LANES :].astype(F32))
-    x = x_ref[...].astype(F32)
+    count = x_ref.shape[2]
+    for r in range(x_ref.shape[0]):
+        turned = jnp.transpose(x_ref[r].astype(F32))
+        rows_ref[r * count : (r + 1) * count, :] = turned.astype(BF16)
+    x = rows_ref[...].astype(F32)
     normed = (x * inverse_rms(x) * gains[HEAD_DIM : HEAD_DIM + 1, :]).astype(BF16)
     normed_ref[...] = normed
     two_ref[...] = gains[HEAD_DIM + 1 : HEAD_DIM + 2, :]
@@ -143,24 +147,12 @@
     return (own < end) & (own + rows > start) & keys_in & (jnp.minimum(first, second) <= own)
 
 
-def attend_kernel(steps, diagonal, fresh, info_ref, q_ref, a_ref, b_ref, *refs):
-    if fresh:
-        max_ref, sum_ref = refs
-    else:
-        max_in, sum_in, max_ref, sum_ref = refs
-    step = pl.program_id(0)
+def attend_rows(
+    info_ref, step, steps, diagonal, q_ref, a_ref, b_ref, max_in, sum_in, max_ref, sum_ref
+):
     rows = a_ref.shape[2]
     seqs = q_ref.shape[0] // KV_HEADS
     spans = 1 + 2 * steps
-
-    @pl.when(step == 0)
-    def _():
-        if fresh:
-            max_ref[...] = jnp.full_like(max_ref, LOWEST)
-            sum_ref[...] = jnp.zeros_like(sum_ref)
-        else:
-            max_ref[...] = max_in[...]
-            sum_ref[...] = sum_in[...]
 
     def one_seq(r, unused):
         start = info_ref[spans + r]
@@ -178,20 +170,49 @@
                 rg = r * KV_HEADS + g
                 kv = jnp.concatenate([a_ref[0, rg], b_ref[0, rg]], axis=0)
                 scores = jnp.where(seen, dot(q_ref[rg], kv, NT), MASKED)
-                old = max_ref[rg]
+                old = max_in[rg]
                 new = jnp.maximum(old, jnp.max(scores, axis=-1, keepdims=True))
                 weights = jnp.exp(scores - jnp.concatenate([new, new], axis=1)).astype(BF16)
                 ones = jnp.where(lane_of(kv.shape) < HEAD_DIM, jnp.ones_like(kv), kv)
-                sum_ref[rg] = sum_ref[rg] * jnp.exp(old - new) + dot(weights, ones)
+                sum_ref[rg] = sum_in[rg] * jnp.exp(old - new) + dot(weights, ones)
                 max_ref[rg] = new
+
+        def keep_row():
+            for g in range(KV_HEADS):
+                max_ref[r * KV_HEADS + g] = max_in[r * KV_HEADS + g]
+                sum_ref[r * KV_HEADS + g] = sum_in[r * KV_HEADS + g]
 
         if diagonal:
             one_row()
         else:
-            pl.when(row_active(info_ref, step, rows, start, end))(one_row)
+            active = row_active(info_ref, step, rows, start, end)
+            pl.when(active)(one_row)
+            if max_in is not max_ref:
+                pl.when(jnp.logical_not(active))(keep_row)
         return unused
 
     lax.fori_loop(0, seqs, one_seq, 0)
+
+
+def attend_kernel(steps, diagonal, fresh, info_ref, q_ref, a_ref, b_ref, *refs):
+    if fresh:
+        max_ref, sum_ref = refs
+    else:
+        max_in, sum_in, max_ref, sum_ref = refs
+    step = pl.program_id(0)
+
+    @pl.when(step == 0)
+    def _():
+        if fresh:
+            max_ref[...] = jnp.full_like(max_ref, LOWEST)
+            sum_ref[...] = jnp.zeros_like(sum_ref)
+        else:
+            max_ref[...] = max_in[...]
+            sum_ref[...] = sum_in[...]
+
+    attend_rows(
+        info_ref, step, steps, diagonal, q_ref, a_ref, b_ref, max_ref, sum_ref, max_ref, sum_ref
+    )
 
 
 def attend(info, queries, a, b, carry, diagonal):
@@ -205,7 +226,7 @@
         (sds((tiles, total, LANES), F32),) * 2,
         [pl.BlockSpec(memory_space=pltpu.SMEM), whole, piece, piece]
         + ([] if carry is None else [whole] * 2),
-        cost=4.0 + 2.0 * steps,
+        cost=10.0 * steps,
         out_specs=(whole, whole),
         grid=(steps,),
     )(info, queries, a, b, *(carry or ()))
@@ -273,7 +294,7 @@
     lax.fori_loop(0, seqs, one_seq, 0)
 
 
-def attend_back(info, queries, d_out, stats, a, b, carry, diagonal, after=(), slow=True, extra=()):
+def attend_back(info, queries, d_out, stats, a, b, carry, diagonal, after=(), extra=()):
     steps = a.shape[0]
     tiles, total, _ = queries.shape
     rows = a.shape[2]
@@ -289,19 +310,24 @@
         + ([] if carry is None else [whole])
         + [pl.BlockSpec(memory_space=pl.ANY)] * len(after)
         + [one] * len(extra),
-        cost=3.0 + 3.0 * steps if slow else 1.0,
+        cost=0.05,
         out_specs=(whole, piece, piece) + ((one,) if extra else ()),
         grid=(steps,),
     )(info, queries, d_out, stats, a, b, *(() if carry is None else (carry,)), *after, *extra)
 
 
 def middle_kernel(
+    fused,
     index_ref,
+    info_ref,
     x_ref,
-    cot_ref,
+    cot_in,
     gain_ref,
     max_ref,
     sum_ref,
+    q_ref,
+    a_ref,
+    b_ref,
     gu0,
     gu1,
     gu2,
@@ -328,16 +354,35 @@
     g_out,
     slot_ref,
     chunk_ref,
+    stage_ref,
+    max_out,
+    sum_out,
+    cot_ref,
+    in_sems,
+    out_sems,
 ):
     index = index_ref[0]
     dim = x_ref.shape[1]
     ff = w_down.shape[0]
     fd, fs = ff // 4, dim // 4
-    assemble(w_gu, index, (gu0, gu1, gu2, gu3), fs)
-    for code, ref in zip((0, 1, 2, 3), (do0, do1, do2, do3)):
+    loads = []
+    for code, gu, do in zip((0, 1, 2, 3), (gu0, gu1, gu2, gu3), (do0, do1, do2, do3)):
         shard = index ^ code
-        w_down[pl.ds(pl.multiple_of(shard * fd, 16), fd), :] = ref[0:fd, :]
-        w_out[pl.ds(pl.multiple_of(shard * fs, 16), fs), :] = ref[fd:, :]
+        down_at = pl.ds(pl.multiple_of(shard * fd, 16), fd)
+        at = pl.ds(pl.multiple_of(shard * fs, 16), fs)
+        for source, target in (
+            (do.at[pl.ds(fd, fs)], w_out.at[at]),
+            (gu, w_gu.at[at]),
+            (do.at[pl.ds(0, fd)], w_down.at[down_at]),
+        ):
+            loads.append(pltpu.make_async_copy(source, target, in_sems.at[len(loads)]))
+    for copy in loads:
+        copy.start()
+    if fused:
+        attend_rows(
+            info_ref, 0, 1, False, q_ref, a_ref, b_ref, max_ref, sum_ref, max_out, sum_out
+        )
+        max_ref, sum_ref = max_out, sum_out
     tiles, total, _ = max_ref.shape
     seqs = tiles // KV_HEADS
     rows = total // GROUP
@@ -365,6 +410,11 @@
                 att_ref[r * rows : (r + 1) * rows, p * LANES : (p + 1) * LANES] = tile.astype(BF16)
             else:
                 att_ref[r * rows : (r + 1) * rows, p * LANES :] = tile[:, :HEAD_DIM].astype(BF16)
+    for r in range(seqs):
+        turned = jnp.transpose(cot_in[r].astype(F32))
+        cot_ref[r * rows : (r + 1) * rows, :] = turned.astype(BF16)
+    for copy in loads:
+        copy.wait()
     att = att_ref[...]
     cot = cot_ref[...]
     mid = x_ref[...].astype(F32) + dot(att, w_out[...])
@@ -391,12 +441,26 @@
         d_gate = (d_hidden * up * sig * (1.0 + gate * (1.0 - sig))).astype(BF16)
         d_up = (d_hidden * silu).astype(BF16)
         g_down[cols, :] = dot(hidden, cot_ref[...], TN)
-        g_gu[:, cols] = dot(n2, d_gate, TN)
-        g_gu[:, cols_up] = dot(n2, d_up, TN)
+        g_gu[:, cols] = dot(n2, d_gate, TN).astype(BF16)
+        g_gu[:, cols_up] = dot(n2, d_up, TN).astype(BF16)
         dn2_ref[...] += dot(d_gate, w_g, NT) + dot(d_up, w_u, NT)
         return carry
 
     lax.fori_loop(0, 2, ff_step, 0)
+    part = dim // CHUNKS
+    quarter = 2 * ff // CHUNKS
+    stores = []
+    for slot in (2, 3, 0, 1):
+        to = keep_ref if slot < 2 else send_ref
+        at = pl.ds(pl.multiple_of((index ^ SLOTS[slot]) * fs, 16), fs)
+        for c in range(CHUNKS):
+            copy = pltpu.make_async_copy(
+                g_gu.at[at, pl.ds(c * quarter, quarter)],
+                to.at[slot % 2, c, pl.ds(0, fs)],
+                out_sems.at[len(stores)],
+            )
+            copy.start()
+            stores.append(copy)
     for r in range(seqs):
         turned_ref[r] = jnp.transpose(out_ref[r * rows : (r + 1) * rows, :])
     dn2 = dn2_ref[...]
@@ -426,9 +490,7 @@
     for rg in range(tiles):
         prod = d_ref[rg].astype(F32) * outs[rg]
         stat_ref[rg, 1:2, :] = jnp.sum(jnp.transpose(prod), axis=0, keepdims=True)
-    cols = 2 * ff // CHUNKS
-    part = dim // CHUNKS
-    for slot in range(4):
+    for slot in (2, 3, 0, 1):
         shard = index ^ SLOTS[slot]
         to = keep_ref if slot < 2 else send_ref
         at = pl.ds(pl.multiple_of(shard * fs, 16), fs)
@@ -436,27 +498,38 @@
         slot_ref[fd : fd + fs, :] = g_out[at, :]
         slot_ref[fd + fs :, :] = jnp.broadcast_to(gain_grad, (dim - fd - fs, dim))
         for c in range(CHUNKS):
-            chunk_ref[:fs, :] = g_gu[at, c * cols : (c + 1) * cols]
-            chunk_ref[fs : fs + part, :] = slot_ref[c * part : (c + 1) * part, :cols]
-            top = slot_ref[c * part : c * part + TOP, cols:]
-            rest = slot_ref[c * part + TOP : (c + 1) * part, cols:]
-            fill = jnp.zeros((2 * TOP - part, dim - cols), F32)
-            chunk_ref[fs + part :, :] = jnp.concatenate(
+            chunk_ref[:part, :] = slot_ref[c * part : (c + 1) * part, :quarter]
+            top = slot_ref[c * part : c * part + TOP, quarter:]
+            rest = slot_ref[c * part + TOP : (c + 1) * part, quarter:]
+            fill = jnp.zeros((2 * TOP - part, dim - quarter), F32)
+            chunk_ref[part:, :] = jnp.concatenate(
                 [top, jnp.concatenate([rest, fill], axis=0)], axis=1
             )
-            to[slot % 2, c] = chunk_ref[...].astype(BF16)
-
-
-def middle(index, x, cot, gain, top, sums, gu, do):
+            stage_ref[slot, c] = chunk_ref[...].astype(BF16)
+        copy = pltpu.make_async_copy(
+            stage_ref.at[slot],
+            to.at[slot % 2, pl.ds(0, CHUNKS), pl.ds(fs, part + TOP)],
+            out_sems.at[len(stores)],
+        )
+        copy.start()
+        stores.append(copy)
+    for copy in stores:
+        copy.wait()
+
+
+def middle(index, x, cot, gain, top, sums, gu, do, info, queries, a, b, fused):
     n, dim = x.shape
     tiles, total, _ = top.shape
     ff2 = gu[0].shape[1]
     ff = ff2 // 2
     chunk = (dim // 4 + dim // CHUNKS + TOP, ff2 // CHUNKS)
+    small = (dim // CHUNKS + TOP, ff2 // CHUNKS)
     pair = sds((2, CHUNKS) + chunk, BF16)
     vm = pl.BlockSpec(memory_space=pltpu.VMEM)
+    sm = pl.BlockSpec(memory_space=pltpu.SMEM)
+    hbm = pl.BlockSpec(memory_space=pl.ANY)
     return call(
-        middle_kernel,
+        functools.partial(middle_kernel, fused),
         (
             sds((tiles // KV_HEADS, dim, total // GROUP), F32),
             sds((n, dim), F32),
@@ -465,9 +538,9 @@
             pair,
             pair,
         ),
-        [pl.BlockSpec(memory_space=pltpu.SMEM)] + [vm] * 13,
+        [sm, sm] + [vm] * 8 + [hbm] * 8,
         cost=20.0,
-        out_specs=(vm,) * 6,
+        out_specs=(vm,) * 4 + (hbm,) * 2,
         scratch_shapes=[
             pltpu.VMEM((n, dim), F32),
             pltpu.VMEM((dim, ff2), BF16),
@@ -476,13 +549,19 @@
             pltpu.VMEM((n, dim), BF16),
             pltpu.VMEM((n, dim), BF16),
             pltpu.VMEM((n, dim), F32),
-            pltpu.VMEM((dim, ff2), F32),
+            pltpu.VMEM((dim, ff2), BF16),
             pltpu.VMEM((ff, dim), F32),
             pltpu.VMEM((dim, dim), F32),
             pltpu.VMEM((dim, dim), F32),
-            pltpu.VMEM(chunk, F32),
+            pltpu.VMEM(small, F32),
+            pltpu.VMEM((4, CHUNKS) + small, BF16),
+            pltpu.VMEM((tiles, total, LANES), F32),
+            pltpu.VMEM((tiles, total, LANES), F32),
+            pltpu.VMEM((n, dim), BF16),
+            pltpu.SemaphoreType.DMA((12,)),
+            pltpu.SemaphoreType.DMA((4 * CHUNKS + 4,)),
         ],
-    )(index, x, cot, gain, top, sums, *gu, *do)
+    )(index, info, x, cot, gain, top, sums, queries, a, b, *gu, *do)
 
 
 def end_kernel(
@@ -575,14 +654,14 @@
         (sds((tiles // KV_HEADS, dim, dkv[0].shape[1]), F32), pair, pair),
         [pl.BlockSpec(memory_space=pltpu.SMEM)] + [vm] * (7 + len(dkv))
         + [pl.BlockSpec(memory_space=pl.ANY)] * len(after),
-        cost=7.0,
+        cost=0.05,
         out_specs=(vm,) * 3,
         scratch_shapes=[pltpu.VMEM((n, width), BF16), pltpu.VMEM((dim, width), F32)],
     )(index, x, normed, w, cosines, sines, dq, d_mid, *dkv, *after)
 
 
 def both_halves(place_ref, parts, d):
-    near, far = parts[2 * d][...].astype(F32), parts[2 * d + 1][...].astype(F32)
+    near, far = parts[0][d].astype(F32), parts[1][d].astype(F32)
     flag = place_ref[0] == 0
     return place_ref[1] ^ d, jnp.where(flag, near, far), jnp.where(flag, far, near)
 
@@ -597,13 +676,13 @@
 
 
 def own_kernel(place_ref, *refs):
-    parts = refs[:CHUNKS]
-    gate_ref, up_ref, down_ref, out_ref, gain_ref, all_ref = refs[CHUNKS:]
+    parts = refs[:-6]
+    gate_ref, up_ref, down_ref, out_ref, gain_ref, all_ref = refs[-6:]
     own_body(place_ref, parts, gate_ref, up_ref, down_ref, out_ref, gain_ref, all_ref)
 
 
 def own_body(place_ref, parts, gate_ref, up_ref, down_ref, out_ref, gain_ref, all_ref):
-    cols = parts[0].shape[1]
+    cols = parts[0].shape[-1]
     fs, dim = out_ref.shape
     fd = down_ref.shape[1]
     part = dim // CHUNKS
@@ -627,9 +706,9 @@
 
 
 def own_q_kernel(place_ref, *refs):
-    parts = refs[:CHUNKS]
-    query_ref, key_ref, value_ref, gain_ref, all_ref = refs[CHUNKS:]
-    part, cols = parts[0].shape
+    parts = refs[:2]
+    query_ref, key_ref, value_ref, gain_ref, all_ref = refs[-5:]
+    part, cols = parts[0].shape[1:]
     for d in range(4):
         quarter, first, second = both_halves(place_ref, parts, d)
         at = pl.ds(pl.multiple_of(quarter * cols, LANES), cols)
@@ -646,16 +725,18 @@
     own_gain(place_ref, row, gain_ref)
 
 
-def own(kernel, place, outs, parts, scratch):
+def own(kernel, place, outs, parts, scratch, after=()):
     vm = pl.BlockSpec(memory_space=pltpu.VMEM)
     return call(
         kernel,
         tuple(sds(shape, F32) for shape in outs),
-        [pl.BlockSpec(memory_space=pltpu.SMEM)] + [vm] * CHUNKS,
-        cost=3.0,
+        [pl.BlockSpec(memory_space=pltpu.SMEM)]
+        + [vm] * len(parts)
+        + [pl.BlockSpec(memory_space=pl.ANY)] * len(after),
+        cost=0.05,
         out_specs=(vm,) * len(outs),
         scratch_shapes=[pltpu.VMEM(scratch, F32)],
-    )(place, *parts)
+    )(place, *parts, *after)
 
 
 def pack_kernel(q_ref, k_ref, v_ref, one_ref, two_ref, out_ref):
@@ -673,10 +754,13 @@
     out_ref[:, first + full :] = jnp.transpose(gains)[:, HEAD_DIM:].astype(BF16)
 
 
-def gu_pack_kernel(gate_ref, up_ref, unused, out_ref):
+def rest_pack_kernel(gate_ref, up_ref, down_ref, w_ref, gu_ref, do_ref):
     ff = gate_ref.shape[1]
-    out_ref[:, :ff] = gate_ref[...]
-    out_ref[:, ff:] = up_ref[...]
+    gu_ref[:, :ff] = gate_ref[...]
+    gu_ref[:, ff:] = up_ref[...]
+    fd = down_ref.shape[1]
+    do_ref[:fd, :] = jnp.transpose(down_ref[...].astype(F32)).astype(BF16)
+    do_ref[fd:, :] = w_ref[...]
 
 
 def flip(x, axis, mask):
@@ -716,16 +800,15 @@
         away[c] = total_of(keep[0, there], got[0, there], far[there])
 
 
-def y_direct_kernel(place_ref, keep, got, far, *outs):
-    for d in range(CHUNKS):
-        c = 4 * (place_ref[0] ^ (d & 1)) + (place_ref[1] ^ (d >> 1))
-        outs[d][...] = total_of(keep[0, c], got[0, c], far[c])
-
-
 def x_kernel(place_ref, keep, got, *outs):
     for d in range(4):
         c = place_ref[1] ^ d
         outs[d][...] = total_of(keep[c], got[c])
+
+
+def stack_kernel(place_ref, *refs):
+    for d in range(4):
+        refs[4][d] = refs[d][...]
 
 
 def fuse(kernel, place, outs, ins, after=(), specs=None, out_specs=None, grid=None):
@@ -741,7 +824,7 @@
         [pl.BlockSpec(memory_space=pltpu.SMEM)]
         + (specs or [vm] * len(ins))
         + [pl.BlockSpec(memory_space=pl.ANY)] * len(after),
-        cost=1.5,
+        cost=0.05,
         out_specs=out_specs or (vm,) * len(outs),
         **({"grid": grid} if grid else {}),
     )(place, *ins, *after)
@@ -782,20 +865,6 @@
         self.parts = (keep, flip(send, "ctx", 1))
         return keep
 
-    def y_direct(self, *after):
-        mine, *away = fuse(
-            y_direct_kernel,
-            self.place,
-            [self.shape] * CHUNKS,
-            self.parts,
-            after,
-            self.y_specs(),
-            None,
-            (1,),
-        )
-        self.parts = (mine, *(flip(away[d - 1], "ctx", d) for d in range(1, CHUNKS)))
-        return mine
-
     def x(self, *after):
         mine, *away = fuse(x_kernel, self.place, [self.shape] * 4, self.parts, after)
         self.parts = (mine, *(flip(away[d - 1], "ctx", 2 * d) for d in (1, 2, 3)))
@@ -808,8 +877,13 @@
             (mine,) = fuse(
                 add_kernel, self.place, [self.shape], (mine, flip(mine, "ctx", 1 << b))
             )
-        self.parts = (mine, *(flip(mine, "ctx", d) for d in range(1, CHUNKS)))
+        self.parts = (mine, *(flip(mine, "ctx", d) for d in (2, 4, 6)))
         return mine
+
+    def stack(self, *after):
+        (every,) = fuse(stack_kernel, self.place, [(4,) + self.shape], self.parts, after)
+        self.parts = (every, flip(every, "ctx", 1))
+        return every
 
 
 def send_down(x, levels):
@@ -838,8 +912,7 @@
     me = lax.axis_index("ctx")
     index = lax.axis_index("fsdp").reshape(1).astype(jnp.int32)
     fs = w_query.shape[0]
-    x = tokens.reshape(n, dim)
-    cot = cotangent.reshape(n, dim)
+    cot = jnp.transpose(cotangent, (0, 2, 1))
 
     used = KV_HEADS * LANES + HEADS * HEAD_DIM + 2
     width = used - used % -LANES
@@ -848,17 +921,6 @@
         w_query, w_key, w_value, attn_gain, mlp_gain
     )
     first_shards = gather_shards(first)
-    gu_shards = gather_shards(
-        call(
-            gu_pack_kernel,
-            sds((fs, 2 * w_gate.shape[1]), BF16),
-            [vm, vm, pl.BlockSpec(memory_space=pl.ANY)],
-            cost=1.5,
-            out_specs=vm,
-        )(w_gate, w_up, first_shards[2])
-    )
-    do_shards = gather_shards(jnp.concatenate([w_down, w_out], axis=0))
-
     places = me * rows + jnp.arange(rows, dtype=jnp.int32)
     positions = (places[None, :] - seq_starts[:, None]).astype(F32)
     frequency = THETA ** (-(2.0 * jnp.arange(HEAD_DIM // 2, dtype=F32)) / HEAD_DIM)
@@ -867,8 +929,10 @@
     cosines = jnp.concatenate([cos] * 4, axis=1)
     sines = jnp.concatenate([-sin, sin] * 2, axis=1)
 
+    ff, fd = w_gate.shape[1], w_down.shape[0]
+    hbm = pl.BlockSpec(memory_space=pl.ANY)
     tiles = seqs * KV_HEADS
-    weights, normed, queries, kv, gain_two = call(
+    weights, normed, queries, kv, gain_two, x = call(
         qkv_kernel,
         (
             sds((dim, width), BF16),
@@ -876,11 +940,22 @@
             sds((tiles, GROUP * rows, LANES), BF16),
             sds((tiles, rows, LANES), BF16),
             sds((1, dim), F32),
+            sds((n, dim), BF16),
         ),
         [pl.BlockSpec(memory_space=pltpu.SMEM)] + [vm] * 7,
         cost=4.0,
-        out_specs=(vm,) * 5,
-    )(index, x, *first_shards, cosines, sines)
+        out_specs=(vm,) * 6,
+    )(index, jnp.transpose(tokens, (0, 2, 1)), *first_shards, cosines, sines)
+
+    gu_own, do_own = call(
+        rest_pack_kernel,
+        (sds((fs, 2 * ff), BF16), sds((fd + fs, dim), BF16)),
+        [vm] * 4,
+        cost=3.0,
+        out_specs=(vm, vm),
+    )(w_gate, w_up, w_down.T, w_out)
+    gu_shards = gather_shards(gu_own)
+    do_shards = gather_shards(do_own)
 
     spans = [seq_starts.astype(jnp.int32), (seq_starts + seq_lengths).astype(jnp.int32)]
 
@@ -903,16 +978,19 @@
             if k + 1 < levels:
                 piece = lax.ppermute(piece, "ctx", up)
         carry = None
-        for k in range(levels):
+        for k in range(levels - 1):
             bases, a, b = pieces[k]
             carry = attend(info_of(bases), queries, a, b, carry, k == 0)
+        bases, a, b = pieces[-1]
+        last_piece = (info_of(bases), queries, a, b, True)
     else:
         every = lax.all_gather(kv, "ctx", axis=0)
         info = info_of(jnp.arange(n_ctx, dtype=jnp.int32) * rows)
         carry = attend(info, queries, every[0::2], every[1::2], None, True)
+        last_piece = (info, queries, every[:1], every[:1], False)
 
     result, d_mid, d_out, stats, keep_mlp, send_mlp = middle(
-        index, x, cot, gain_two, carry[0], carry[1], gu_shards, do_shards
+        index, x, cot, gain_two, carry[0], carry[1], gu_shards, do_shards, *last_piece
     )
 
     place = jnp.stack([me & 1, (me >> 1) & 3, index[0]]).astype(jnp.int32)
@@ -933,7 +1011,6 @@
                 dq,
                 k == 0,
                 last,
-                k == levels - 1,
                 extra,
             )
             if extra:
@@ -956,8 +1033,6 @@
         mlp.core(dq)
         last = (mlp.y(dq),)
 
-    ff = w_gate.shape[1]
-    fd = w_down.shape[0]
     input_grad, keep_q, send_q = finish(
         index, x, normed, weights, cosines, sines, dq, dkv, d_mid, last
     )
@@ -965,8 +1040,11 @@
     step = mlp.x(keep_q)
     step = qkv.core(step)
     step = mlp.z(step)
-    step = qkv.y_direct(step)
+    step = qkv.y(step)
+    step = qkv.x(step)
+    step = mlp.stack(step)
     step = qkv.z(step)
+    step = qkv.stack(step)
     grad_gate, grad_up, grad_down, grad_out, gain_two_grad = own(
         own_kernel,
         place,
@@ -982,6 +1060,7 @@
         [(fs, HEADS * HEAD_DIM), (fs, kv_width), (fs, kv_width), (1, fs)],
         qkv.parts,
         (fs, width),
+        (grad_gate,),
     )
     grad_mlp_gain = gain_two_grad.reshape(fs)
     grad_attn_gain = gain_one_grad.reshape(fs)

time: 255 us -> 240 us (0.941)
  starting transfers between devices: 86.6 us -> 59.6 us
  waiting for transfers between devices: 51.4 us -> 59.8 us
    ppermute x46 -> x37, starting transfers between devices: 68.4 us -> 43.2 us  [flip(): return lax.ppermute(x, axis, [(i, i ^ mask) for i in range(n)])]
    ppermute x3, waiting for transfers between devices: 0.01 us -> 5.52 us  [local(): piece = lax.ppermute(piece, 'ctx', up)]
    pallas_call x8 -> x11, Pallas kernels: 20.9 us -> 26.1 us  [fuse(): call(body, tuple((sds(shape, BF16) for shape in outs)), [pl.BlockSpec(mem...]
    pallas_call x4 -> x3, Pallas kernels: 19 us -> 14.5 us  [attend(): call(functools.partial(attend_kernel, steps, diagonal, carry is None), (s...]
    ppermute x46 -> x37, waiting for transfers between devices: 42.5 us -> 44.9 us  [flip(): return lax.ppermute(x, axis, [(i, i ^ mask) for i in range(n)])]
    unnamed x77 -> x68, local copies, waits for them, and re-layouts: 10.5 us -> 12 us
  transfers between devices with their start and end apart: 52 -> 43, of which waited for: 16 -> 18; matrix products, arithmetic and copies ran while one was open for 3% -> 2% of each run, Pallas kernels for 27% -> 28%
where the time goes in v1:
time: 240 us; the launch traced here: 239 us
  Pallas kernels  103 us (43%)
  waiting for transfers between devices  59.8 us (25%)
  starting transfers between devices  59.6 us (25%)
  local copies, waits for them, and re-layouts  12.1 us (5%)
  other arithmetic  4.09 us (2%)
    ppermute x37, waiting for transfers between devices, flip(): return lax.ppermute(x, axis, [(i, i ^ mask) for i in range(n)])  44.9 us
    ppermute x37, starting transfers between devices, flip(): return lax.ppermute(x, axis, [(i, i ^ mask) for i in range(n)])  43.2 us
    pallas_call x11, Pallas kernels, fuse(): call(body, tuple((sds(shape, BF16) for shape in outs)), [pl.BlockSpec(mem...  26.1 us
    pallas_call x1, Pallas kernels, middle(): call(functools.partial(middle_kernel, fused), (sds((tiles // KV_HEADS, di...  21.3 us
    pallas_call x4, Pallas kernels, attend_back(): call(functools.partial(attend_back_kernel, steps, diagonal, carry is None...  19.3 us
    pallas_call x3, Pallas kernels, attend(): call(functools.partial(attend_kernel, steps, diagonal, carry is None), (s...  14.5 us
    ppermute x3, starting transfers between devices, local(): piece = lax.ppermute(piece, 'ctx', up)  12.6 us
    unnamed x68, local copies, waits for them, and re-layouts  12 us
  transfers between devices with their start and end apart: 43, of which 18 were waited for; matrix products, arithmetic and copies ran while one was open for 2% of the time, Pallas kernels for 28%

profile of v1, /device:TPU:0, one launch (start us, length us, event | category | flops | bytes accessed | tf_op | source)
XLA Modules:
  0.0 239.3 jit_solution(9478574311200928115)
XLA Ops:
  0.6 1.9 shard_map.212.w0
  2.6 3.0 %collective-permute-start.1 = (bf16[144,1024]{1,0:T(8,128)(2,1)}, bf16[144,1024]{1,0:T(8,128)(2,1)S(1)}, u32[]{:S(2)}, u32[]{:S(2)}) collective-permute-start(bf16[144,1024]{1,0:T(8,128)(2,1)} %shard_map.212.w0), channel_id=1, source_target_pairs={{0,2},{1,3},{2,0},{3,1},{4,6},{5,7},{6,4},{7,5},{8,10},{9,11},{10,... | collective-permute-start | bytes 884744 | tf_op jit(solution)/shard_map/ppermute | solution.py:768
  5.5 2.7 %shard_map.217 = (bf16[144,3072]{1,0:T(8,128)(2,1)}, bf16[528,576]{1,0:T(8,128)(2,1)}) custom-call(bf16[144,1536]{1,0:T(8,128)(2,1)} %gate_ref.1, bf16[144,1536]{1,0:T(8,128)(2,1)} %up_ref.1, bf16[576,384]{1,0:T(8,128)(2,1)} %bitcast.60, bf16[144,576]{1,0:T(8,128)(2,1)} %w_ref.1), custom_call_target="tpu_custom_call" | custom-call | flops 3000000000 | tf_op jit(solution)/shard_map/pallas_call | solution.py:950
  10.6 3.0 %collective-permute-done.1.w2 = bf16[144,1024]{1,0:T(8,128)(2,1)S(1)} collective-permute-done((bf16[144,1024]{1,0:T(8,128)(2,1)}, bf16[144,1024]{1,0:T(8,128)(2,1)S(1)}, u32[]{:S(2)}, u32[]{:S(2)}) %collective-permute-start.1) | collective-permute-done | bytes 294944 | tf_op jit(solution)/shard_map/ppermute | solution.py:768
  16.4 4.2 %shard_map.213 = (bf16[576,1024]{1,0:T(8,128)(2,1)}, bf16[384,576]{1,0:T(8,128)(2,1)}, bf16[9,384,128]{2,1,0:T(8,128)(2,1)}, bf16[9,128,128]{2,1,0:T(8,128)(2,1)...) custom-call(s32[1]{0:T(128)} %bitcast.index_ref, bf16[3,576,128]{2,1,0:T(8,128)(2,1)} %bitcast.61, ...), custom_call_target="tpu_custom_call" | custom-call | flops 4000000000 | tf_op jit(solution)/shard_map/pallas_call | solution.py:935
  20.6 2.0 collective-permute-start.7
  22.6 3.5 %collective-permute-start.3 = (bf16[9,128,128]{2,1,0:T(8,128)(2,1)}, bf16[9,128,128]{2,1,0:T(8,128)(2,1)S(1)}, u32[]{:S(2)}, u32[]{:S(2)}) collective-permute-start(bf16[9,128,128]{2,1,0:T(8,128)(2,1)} %get-tuple-element.72), channel_id=1, source_target_pairs={{0,8},{4,12},{8,16},{12,20},{16,24},{20,28},{1,9},{5,13},{9,17},{1... | collective-permute-start | bytes 884744 | tf_op jit(solution)/shard_map/ppermute | solution.py:979
  27.6 5.5 %collective-permute-done.3 = bf16[9,128,128]{2,1,0:T(8,128)(2,1)S(1)} collective-permute-done((bf16[9,128,128]{2,1,0:T(8,128)(2,1)}, bf16[9,128,128]{2,1,0:T(8,128)(2,1)S(1)}, u32[]{:S(2)}, u32[]{:S(2)}) %collective-permute-start.3) | collective-permute-done | bytes 294944 | tf_op jit(solution)/shard_map/ppermute | solution.py:979
  33.6 5.0 %collective-permute-start.4 = (bf16[9,128,128]{2,1,0:T(8,128)(2,1)S(1)}, bf16[9,128,128]{2,1,0:T(8,128)(2,1)}, u32[]{:S(2)}, u32[]{:S(2)}) collective-permute-start(bf16[9,128,128]{2,1,0:T(8,128)(2,1)S(1)} %collective-permute-done.3), channel_id=1, source_target_pairs={{0,8},{4,12},{8,16},{12,20},{16,24},{20,28},{1,9},{5,13},{9,17},{1... | collective-permute-start | bytes 884744 | tf_op jit(solution)/shard_map/ppermute | solution.py:979
  38.6 5.5 %shard_map.214 = (f32[9,384,128]{2,1,0:T(8,128)}, f32[9,384,128]{2,1,0:T(8,128)}) custom-call(s32[9]{0:T(128)} %get-tuple-element.130.info_ref, bf16[9,384,128]{2,1,0:T(8,128)(2,1)} %get-tuple-element.71.q_ref, bf16[1,9,128,128]{3,2,1,0:T(8,128)(2,1)} %bitcast.42, bf16[1,9,128,128]{3,2,1,0:T(8,128)(2,1)} %bitcast.44), custom_call_target="tpu_custom_call" | custom-call | flops 10000000000 | tf_op jit(solution)/shard_map/pallas_call | solution.py:224
  44.1 4.1 %collective-permute-start.8 = (bf16[9,128,128]{2,1,0:T(8,128)(2,1)}, bf16[9,128,128]{2,1,0:T(8,128)(2,1)S(1)}, u32[]{:S(2)}, u32[]{:S(2)}) collective-permute-start(bf16[9,128,128]{2,1,0:T(8,128)(2,1)} %collective-permute-done.4), channel_id=1, source_target_pairs={{0,8},{4,12},{8,16},{12,20},{16,24},{20,28},{1,9},{5,13},{9,17},{1... | collective-permute-start | bytes 884744 | tf_op jit(solution)/shard_map/ppermute | solution.py:979
  49.8 4.5 %shard_map.215 = (f32[9,384,128]{2,1,0:T(8,128)}, f32[9,384,128]{2,1,0:T(8,128)}) custom-call(s32[9]{0:T(128)} %get-tuple-element.132.info_ref, bf16[9,384,128]{2,1,0:T(8,128)(2,1)} %get-tuple-element.71.q_ref, bf16[1,9,128,128]{3,2,1,0:T(8,128)(2,1)} %bitcast.46, bf16[1,9,128,128]{3,2,1,0:T(8,128)(2,1)} %bitcast.48, ...), custom_call_target="tpu_custom_call" | custom-call | flops 10000000000 | tf_op jit(solution)/shard_map/pallas_call | solution.py:224
  57.1 4.6 %shard_map.216 = (f32[9,384,128]{2,1,0:T(8,128)}, f32[9,384,128]{2,1,0:T(8,128)}) custom-call(s32[9]{0:T(128)} %get-tuple-element.131.info_ref, bf16[9,384,128]{2,1,0:T(8,128)(2,1)} %get-tuple-element.71.q_ref, bf16[1,9,128,128]{3,2,1,0:T(8,128)(2,1)} %bitcast.9.a_ref, bf16[1,9,128,128]{3,2,1,0:T(8,128)(2,1)} %bitcast.10.b_ref, ...), custom_call_target="tpu_custom_call" | custom-call | flops 10000000000 | tf_op jit(solution)/shard_map/pallas_call | solution.py:224
  61.7 2.6 %collective-permute-done.9 = bf16[9,128,128]{2,1,0:T(8,128)(2,1)S(1)} collective-permute-done((bf16[9,128,128]{2,1,0:T(8,128)(2,1)S(1)}, bf16[9,128,128]{2,1,0:T(8,128)(2,1)S(1)}, u32[]{:S(2)}, u32[]{:S(2)}) %collective-permute-start.9) | collective-permute-done | bytes 294944 | tf_op jit(solution)/shard_map/ppermute | solution.py:768
  65.0 21.3 %shard_map.218 = (f32[3,576,128]{2,1,0:T(8,128)}, f32[384,576]{1,0:T(8,128)}, bf16[9,384,128]{2,1,0:T(8,128)(2,1)}, f32[9,8,384]{2,1,0:T(8,128)}, bf16[2,8,256,3...) custom-call(s32[1]{0:T(128)} %bitcast.index_ref, s32[9]{0:T(128)} %get-tuple-element.133.info_ref, ...), custom_call_target="tpu_custom_call" | custom-call | flops 20000000000 | tf_op jit(solution)/shard_map/pallas_call | solution.py:531
  87.0 3.5 %shard_map.219 = (f32[9,384,128]{2,1,0:T(8,128)}, bf16[1,9,128,128]{3,2,1,0:T(8,128)(2,1)}, bf16[1,9,128,128]{3,2,1,0:T(8,128)(2,1)}) custom-call(s32[9]{0:T(128)} %get-tuple-element.133.info_ref, bf16[9,384,128]{2,1,0:T(8,128)(2,1)} %get-tuple-element.71.q_ref, bf16[9,384,128]{2,1,0:T(8,128)(2,1)} %get-tuple-element.84.d_ref, ...), custom_call_target="tpu_custom_call" | custom-call | flops 50000000 | tf_op jit(solution)/shard_map/pallas_call | solution.py:305
  90.5 1.9 collective-permute-done.16.refs_2_
  92.3 4.0 %shard_map.220.refs_1_ = bf16[8,256,384]{2,1,0:T(8,128)(2,1)} custom-call(s32[3]{0:T(128)} %pad_add_fusion.refs_0_.place_ref, bf16[2,8,256,384]{3,2,1,0:T(8,128)(2,1)} %get-tuple-element.87.refs_1_, bf16[2,8,256,384]{3,2,1,0:T(8,128)(2,1)} %collective-permute-done.16.refs_2_, f32[9,384,128]{2,1,0:T(8,128)} %get-tuple-element.86.refs_3_.refs_0_), custom_call_target="tpu_custom_call" | custom-call | flops 50000000 | tf_op jit(solution)/shard_map/pallas_call | solution.py:821
  98.6 3.9 %shard_map.221 = (f32[9,384,128]{2,1,0:T(8,128)}, bf16[1,9,128,128]{3,2,1,0:T(8,128)(2,1)}, bf16[1,9,128,128]{3,2,1,0:T(8,128)(2,1)}) custom-call(s32[9]{0:T(128)} %get-tuple-element.131.info_ref, bf16[9,384,128]{2,1,0:T(8,128)(2,1)} %get-tuple-element.71.q_ref, bf16[9,384,128]{2,1,0:T(8,128)(2,1)} %get-tuple-element.84.d_ref, ...), custom_call_target="tpu_custom_call" | custom-call | flops 50000000 | tf_op jit(solution)/shard_map/pallas_call | solution.py:305
  103.8 4.0 %collective-permute-done.17.refs_2_ = bf16[9,128,128]{2,1,0:T(8,128)(2,1)S(1)} collective-permute-done((bf16[9,128,128]{2,1,0:T(8,128)(2,1)S(1)}, bf16[9,128,128]{2,1,0:T(8,128)(2,1)S(1)}, u32[]{:S(2)}, u32[]{:S(2)}) %collective-permute-start.17) | collective-permute-done | bytes 294944 | tf_op jit(solution)/shard_map/ppermute | solution.py:768
  108.5 4.1 %shard_map.222 = (f32[9,384,128]{2,1,0:T(8,128)}, bf16[1,9,128,128]{3,2,1,0:T(8,128)(2,1)}, bf16[1,9,128,128]{3,2,1,0:T(8,128)(2,1)}, bf16[9,128,128]{2,1,0:T(8,128)(2,1)}) custom-call(s32[9]{0:T(128)} %get-tuple-element.132.info_ref, bf16[9,384,128]{2,1,0:T(8,128)(2,1)} %get-tuple-element.71.q_ref, bf16[9,384,128]{2,1,0:T(8,128)(2,1)} %get-tuple-element.84.d_ref, ...), custom_call_target="tpu_custom_call" | custom-call | flops 50000000 | tf_op jit(solution)/shard_map/pallas_call | solution.py:305
  115.2 7.8 %shard_map.223 = (f32[9,384,128]{2,1,0:T(8,128)}, bf16[1,9,128,128]{3,2,1,0:T(8,128)(2,1)}, bf16[1,9,128,128]{3,2,1,0:T(8,128)(2,1)}, bf16[9,128,128]{2,1,0:T(8,128)(2,1)}) custom-call(s32[9]{0:T(128)} %get-tuple-element.130.info_ref, bf16[9,384,128]{2,1,0:T(8,128)(2,1)} %get-tuple-element.71.q_ref, bf16[9,384,128]{2,1,0:T(8,128)(2,1)} %get-tuple-element.84.d_ref, ...), custom_call_target="tpu_custom_call" | custom-call | flops 50000000 | tf_op jit(solution)/shard_map/pallas_call | solution.py:305
  126.5 1.8 shard_map.224.refs_4_
  129.6 3.5 %collective-permute-done.24.refs_3_ = bf16[8,256,384]{2,1,0:T(8,128)(2,1)} collective-permute-done((bf16[8,256,384]{2,1,0:T(8,128)(2,1)}, bf16[8,256,384]{2,1,0:T(8,128)(2,1)}, u32[]{:S(2)}, u32[]{:S(2)}) %collective-permute-start.24) | collective-permute-done | bytes 1572896 | tf_op jit(solution)/shard_map/ppermute | solution.py:768
  133.1 4.0 %shard_map.225 = (bf16[4,256,384]{2,1,0:T(8,128)(2,1)}, bf16[4,256,384]{2,1,0:T(8,128)(2,1)}) custom-call(s32[3]{0:T(128)} %pad_add_fusion.refs_0_.place_ref, bf16[2,8,256,384]{3,2,1,0:T(8,128)(2,1)} %get-tuple-element.87.refs_1_, bf16[2,8,256,384]{3,2,1,0:T(8,128)(2,1)} %collective-permute-done.16.refs_2_, ...), custom_call_target="tpu_custom_call" | custom-call | flops 50000000 | tf_op jit(solution)/shard_map/pallas_call | solution.py:821
  137.8 7.7 %collective-permute-done.21.refs_3_ = bf16[9,128,128]{2,1,0:T(8,128)(2,1)} collective-permute-done((bf16[9,128,128]{2,1,0:T(8,128)(2,1)}, bf16[9,128,128]{2,1,0:T(8,128)(2,1)}, u32[]{:S(2)}, u32[]{:S(2)}) %collective-permute-start.21) | collective-permute-done | bytes 294944 | tf_op jit(solution)/shard_map/ppermute | solution.py:891
  147.9 7.2 %shard_map.226 = (f32[3,576,128]{2,1,0:T(8,128)}, bf16[2,8,72,256]{3,2,1,0:T(8,128)(2,1)}, bf16[2,8,72,256]{3,2,1,0:T(8,128)(2,1)}) custom-call(s32[1]{0:T(128)} %bitcast.index_ref, bf16[384,576]{1,0:T(8,128)(2,1)} %get-tuple-element.69.x_ref, bf16[384,576]{1,0:T(8,128)(2,1)} %get-tuple-element.82.normed_ref, bf16[576,1024]{1,0:T(8,128)(2,1)} %get-tuple-element.83.w_ref, ...), custom_call_target="tpu_custom_call" | custom-call | flops 50000000 | tf_op jit(solution)/shard_map/pallas_call | solution.py:652
  156.2 2.3 shard_map.227
  159.3 3.2 %shard_map.228.refs_5_ = bf16[8,72,256]{2,1,0:T(8,128)(2,1)} custom-call(s32[3]{0:T(128)} %pad_add_fusion.refs_0_.place_ref, bf16[2,8,72,256]{3,2,1,0:T(8,128)(2,1)} %get-tuple-element.105.refs_3_.refs_1_, bf16[2,8,72,256]{3,2,1,0:T(8,128)(2,1)} %copy-done, bf16[256,384]{1,0:T(8,128)(2,1)} %get-tuple-element.108.refs_3_.refs_1_), custom_call_target="tpu_custom_call" | custom-call | flops 50000000 | tf_op jit(solution)/shard_map/pallas_call | solution.py:821
  164.1 3.6 %collective-permute-start.28 = (bf16[256,384]{1,0:T(8,128)(2,1)}, bf16[256,384]{1,0:T(8,128)(2,1)S(1)}, u32[]{:S(2)}, u32[]{:S(2)}) collective-permute-start(bf16[256,384]{1,0:T(8,128)(2,1)} %get-tuple-element.109), channel_id=1, source_target_pairs={{0,8},{4,12},{8,0},{12,4},{16,24},{20,28},{24,16},{28,20},{1,9},{5... | collective-permute-start | bytes 589832 | tf_op jit(solution)/shard_map/ppermute | solution.py:768
  170.1 3.9 %collective-permute-done.28.refs_2_ = bf16[256,384]{1,0:T(8,128)(2,1)S(1)} collective-permute-done((bf16[256,384]{1,0:T(8,128)(2,1)}, bf16[256,384]{1,0:T(8,128)(2,1)S(1)}, u32[]{:S(2)}, u32[]{:S(2)}) %collective-permute-start.28) | collective-permute-done | bytes 196640 | tf_op jit(solution)/shard_map/ppermute | solution.py:768
  174.0 10.0 %collective-permute-done.29.refs_3_ = bf16[256,384]{1,0:T(8,128)(2,1)S(1)} collective-permute-done((bf16[256,384]{1,0:T(8,128)(2,1)}, bf16[256,384]{1,0:T(8,128)(2,1)S(1)}, u32[]{:S(2)}, u32[]{:S(2)}) %collective-permute-start.29) | collective-permute-done | bytes 196640 | tf_op jit(solution)/shard_map/ppermute | solution.py:768
  185.3 2.0 shard_map.229.refs_4_.refs_1_
  187.3 2.4 %collective-permute-start.37 = (bf16[256,384]{1,0:T(8,128)(2,1)}, bf16[256,384]{1,0:T(8,128)(2,1)S(1)}, u32[]{:S(2)}, u32[]{:S(2)}) collective-permute-start(bf16[256,384]{1,0:T(8,128)(2,1)} %shard_map.229.refs_4_.refs_1_), channel_id=1, source_target_pairs={{0,24},{4,28},{8,16},{12,20},{16,8},{20,12},{24,0},{28,4},{1,25},{... | collective-permute-start | bytes 589832 | tf_op jit(solution)/shard_map/ppermute | solution.py:768
  189.8 2.2 collective-permute-start.36
  192.7 2.0 shard_map.230
  194.7 2.4 %collective-permute-start.31 = (bf16[4,72,256]{2,1,0:T(8,128)(2,1)}, bf16[4,72,256]{2,1,0:T(8,128)(2,1)S(1)}, u32[]{:S(2)}, u32[]{:S(2)}) collective-permute-start(bf16[4,72,256]{2,1,0:T(8,128)(2,1)} %get-tuple-element.113), channel_id=1, source_target_pairs={{0,4},{4,0},{8,12},{12,8},{16,20},{20,16},{24,28},{28,24},{1,5},{5... | collective-permute-start | bytes 442376 | tf_op jit(solution)/shard_map/ppermute | solution.py:768
  197.1 3.3 %collective-permute-done.31.refs_2_ = bf16[4,72,256]{2,1,0:T(8,128)(2,1)S(1)} collective-permute-done((bf16[4,72,256]{2,1,0:T(8,128)(2,1)}, bf16[4,72,256]{2,1,0:T(8,128)(2,1)S(1)}, u32[]{:S(2)}, u32[]{:S(2)}) %collective-permute-start.31) | collective-permute-done | bytes 147488 | tf_op jit(solution)/shard_map/ppermute | solution.py:768
  202.8 4.3 %collective-permute-done.36.refs_3_ = bf16[256,384]{1,0:T(8,128)(2,1)S(1)} collective-permute-done((bf16[256,384]{1,0:T(8,128)(2,1)}, bf16[256,384]{1,0:T(8,128)(2,1)S(1)}, u32[]{:S(2)}, u32[]{:S(2)}) %collective-permute-start.36) | collective-permute-done | bytes 196640 | tf_op jit(solution)/shard_map/ppermute | solution.py:768
  207.8 2.2 shard_map.232.refs_5_.refs_0_
  211.4 3.0 %collective-permute-start.34 = (bf16[72,256]{1,0:T(8,128)(2,1)}, bf16[72,256]{1,0:T(8,128)(2,1)S(1)}, u32[]{:S(2)}, u32[]{:S(2)}) collective-permute-start(bf16[72,256]{1,0:T(8,128)(2,1)} %get-tuple-element.117), channel_id=1, source_target_pairs={{0,24},{4,28},{8,16},{12,20},{16,8},{20,12},{24,0},{28,4},{1,25},{... | collective-permute-start | bytes 110600 | tf_op jit(solution)/shard_map/ppermute | solution.py:768
  215.5 1.9 collective-permute-done.34.refs_4_
  219.5 3.0 %collective-permute-start.40 = (bf16[72,256]{1,0:T(8,128)(2,1)}, bf16[72,256]{1,0:T(8,128)(2,1)S(1)}, u32[]{:S(2)}, u32[]{:S(2)}) collective-permute-start(bf16[72,256]{1,0:T(8,128)(2,1)} %shard_map.233.refs_1_.refs_5_), channel_id=1, source_target_pairs={{0,24},{4,28},{8,16},{12,20},{16,8},{20,12},{24,0},{28,4},{1,25},{... | collective-permute-start | bytes 110600 | tf_op jit(solution)/shard_map/ppermute | solution.py:768
  223.9 1.8 collective-permute-done.40.refs_4_
  225.6 1.9 collective-permute-done.39.refs_3_
  230.2 2.0 collective-permute-start.41
  233.1 3.5 %shard_map.235 = (f32[144,1536]{1,0:T(8,128)}, f32[144,1536]{1,0:T(8,128)}, f32[576,384]{1,0:T(8,128)}, f32[144,576]{1,0:T(8,128)}, f32[1,144]{1,0:T(1,128)}) custom-call(s32[3]{0:T(128)} %pad_add_fusion.refs_0_.place_ref, bf16[4,256,384]{2,1,0:T(8,128)(2,1)} %shard_map.232.refs_5_.refs_0_, bf16[4,256,384]{2,1,0:T(8,128)(2,1)} %copy-done.1), custom_call_target="tpu_custom_call" | custom-call | flops 50000000 | tf_op jit(solution)/shard_map/pallas_call | solution.py:730
  237.3 2.0 shard_map.236
  (143 shorter events, 48.8 us)
Async XLA Ops:
  2.6 11.0 %collective-permute-start.1 = (bf16[144,1024]{1,0:T(8,128)(2,1)}, bf16[144,1024]{1,0:T(8,128)(2,1)S(1)}, u32[]{:S(2)}, u32[]{:S(2)}) collective-permute-start(bf16[144,1024]{1,0:T(8,128)(2,1)} %shard_map.212.w0), channel_id=1, source_target_pairs={{0,2},{1,3},{2,0},{3,1},{4,6},{5,7},{6,4},{7,5},{8,10},{9,11},{10,... | collective-permute-start | bytes 884744 | tf_op jit(solution)/shard_map/ppermute | solution.py:768
  5.5 10.1 %collective-permute-start = (bf16[144,1024]{1,0:T(8,128)(2,1)}, bf16[144,1024]{1,0:T(8,128)(2,1)S(1)}, u32[]{:S(2)}, u32[]{:S(2)}) collective-permute-start(bf16[144,1024]{1,0:T(8,128)(2,1)} %shard_map.212.w0), channel_id=1, source_target_pairs={{0,1},{1,0},{2,3},{3,2},{4,5},{5,4},{6,7},{7,6},{8,9},{9,8},{10,11... | collective-permute-start | bytes 884744 | tf_op jit(solution)/shard_map/ppermute | solution.py:768
  5.5 8.9 %copy-start.33 = (s32[3]{0:T(128)S(1)}, s32[3]{0:T(128)}, u32[]{:S(2)}) copy-start(s32[3]{0:T(128)} %param.24) | copy-start | bytes 40
  8.2 46.1 %collective-permute-start.14 = (bf16[528,576]{1,0:T(8,128)(2,1)}, bf16[528,576]{1,0:T(8,128)(2,1)}, u32[]{:S(2)}, u32[]{:S(2)}) collective-permute-start(bf16[528,576]{1,0:T(8,128)(2,1)} %get-tuple-element.80.do0), channel_id=1, source_target_pairs={{0,2},{1,3},{2,0},{3,1},{4,6},{5,7},{6,4},{7,5},{8,10},{9,11},{10,... | collective-permute-start | bytes 1824776 | tf_op jit(solution)/shard_map/ppermute | solution.py:768
  8.2 53.4 %collective-permute-start.13 = (bf16[528,576]{1,0:T(8,128)(2,1)}, bf16[528,576]{1,0:T(8,128)(2,1)}, u32[]{:S(2)}, u32[]{:S(2)}) collective-permute-start(bf16[528,576]{1,0:T(8,128)(2,1)} %get-tuple-element.80.do0), channel_id=1, source_target_pairs={{0,1},{1,0},{2,3},{3,2},{4,5},{5,4},{6,7},{7,6},{8,9},{9,8},{10,11... | collective-permute-start | bytes 1824776 | tf_op jit(solution)/shard_map/ppermute | solution.py:768
  8.7 45.6 %collective-permute-start.11 = (bf16[144,3072]{1,0:T(8,128)(2,1)}, bf16[144,3072]{1,0:T(8,128)(2,1)}, u32[]{:S(2)}, u32[]{:S(2)}) collective-permute-start(bf16[144,3072]{1,0:T(8,128)(2,1)} %get-tuple-element.79.gu0), channel_id=1, source_target_pairs={{0,2},{1,3},{2,0},{3,1},{4,6},{5,7},{6,4},{7,5},{8,10},{9,11},{10,... | collective-permute-start | bytes 2654216 | tf_op jit(solution)/shard_map/ppermute | solution.py:768
  13.6 2.1 collective-permute-start.2
  20.6 13.0 %collective-permute-start.7 = (bf16[9,128,128]{2,1,0:T(8,128)(2,1)}, bf16[9,128,128]{2,1,0:T(8,128)(2,1)S(1)}, u32[]{:S(2)}, u32[]{:S(2)}) collective-permute-start(bf16[9,128,128]{2,1,0:T(8,128)(2,1)} %get-tuple-element.72), channel_id=1, source_target_pairs={{0,4},{4,0},{8,12},{12,8},{16,20},{20,16},{24,28},{28,24},{1,5},{5... | collective-permute-start | bytes 884744 | tf_op jit(solution)/shard_map/ppermute | solution.py:768
  22.6 10.4 %collective-permute-start.3 = (bf16[9,128,128]{2,1,0:T(8,128)(2,1)}, bf16[9,128,128]{2,1,0:T(8,128)(2,1)S(1)}, u32[]{:S(2)}, u32[]{:S(2)}) collective-permute-start(bf16[9,128,128]{2,1,0:T(8,128)(2,1)} %get-tuple-element.72), channel_id=1, source_target_pairs={{0,8},{4,12},{8,16},{12,20},{16,24},{20,28},{1,9},{5,13},{9,17},{1... | collective-permute-start | bytes 884744 | tf_op jit(solution)/shard_map/ppermute | solution.py:979
  33.1 11.0 %copy-start.3 = (bf16[9,128,128]{2,1,0:T(8,128)(2,1)}, bf16[9,128,128]{2,1,0:T(8,128)(2,1)S(1)}, u32[]{:S(2)}) copy-start(bf16[9,128,128]{2,1,0:T(8,128)(2,1)S(1)} %collective-permute-done.3) | copy-start | bytes 884740
  33.1 15.2 %collective-permute-start.6 = (bf16[9,128,128]{2,1,0:T(8,128)(2,1)S(1)}, bf16[9,128,128]{2,1,0:T(8,128)(2,1)S(1)}, u32[]{:S(2)}, u32[]{:S(2)}) collective-permute-start(bf16[9,128,128]{2,1,0:T(8,128)(2,1)S(1)} %collective-permute-done.3), channel_id=1, source_target_pairs={{0,4},{4,0},{8,12},{12,8},{16,20},{20,16},{24,28},{28,24},{1,5},{5... | collective-permute-start | bytes 884744 | tf_op jit(solution)/shard_map/ppermute | solution.py:768
  33.6 10.5 %collective-permute-start.4 = (bf16[9,128,128]{2,1,0:T(8,128)(2,1)S(1)}, bf16[9,128,128]{2,1,0:T(8,128)(2,1)}, u32[]{:S(2)}, u32[]{:S(2)}) collective-permute-start(bf16[9,128,128]{2,1,0:T(8,128)(2,1)S(1)} %collective-permute-done.3), channel_id=1, source_target_pairs={{0,8},{4,12},{8,16},{12,20},{16,24},{20,28},{1,9},{5,13},{9,17},{1... | collective-permute-start | bytes 884744 | tf_op jit(solution)/shard_map/ppermute | solution.py:979
  44.1 10.8 %collective-permute-start.8 = (bf16[9,128,128]{2,1,0:T(8,128)(2,1)}, bf16[9,128,128]{2,1,0:T(8,128)(2,1)S(1)}, u32[]{:S(2)}, u32[]{:S(2)}) collective-permute-start(bf16[9,128,128]{2,1,0:T(8,128)(2,1)} %collective-permute-done.4), channel_id=1, source_target_pairs={{0,8},{4,12},{8,16},{12,20},{16,24},{20,28},{1,9},{5,13},{9,17},{1... | collective-permute-start | bytes 884744 | tf_op jit(solution)/shard_map/ppermute | solution.py:979
  48.3 7.3 %collective-permute-start.5 = (bf16[9,128,128]{2,1,0:T(8,128)(2,1)}, bf16[9,128,128]{2,1,0:T(8,128)(2,1)}, u32[]{:S(2)}, u32[]{:S(2)}) collective-permute-start(bf16[9,128,128]{2,1,0:T(8,128)(2,1)} %collective-permute-done.4), channel_id=1, source_target_pairs={{0,4},{4,0},{8,12},{12,8},{16,20},{20,16},{24,28},{28,24},{1,5},{5... | collective-permute-start | bytes 884744 | tf_op jit(solution)/shard_map/ppermute | solution.py:768
  54.3 7.3 %collective-permute-start.10 = (bf16[144,3072]{1,0:T(8,128)(2,1)}, bf16[144,3072]{1,0:T(8,128)(2,1)}, u32[]{:S(2)}, u32[]{:S(2)}) collective-permute-start(bf16[144,3072]{1,0:T(8,128)(2,1)} %get-tuple-element.79.gu0), channel_id=1, source_target_pairs={{0,1},{1,0},{2,3},{3,2},{4,5},{5,4},{6,7},{7,6},{8,9},{9,8},{10,11... | collective-permute-start | bytes 2654216 | tf_op jit(solution)/shard_map/ppermute | solution.py:768
  54.3 7.3 %collective-permute-start.15 = (bf16[528,576]{1,0:T(8,128)(2,1)}, bf16[528,576]{1,0:T(8,128)(2,1)}, u32[]{:S(2)}, u32[]{:S(2)}) collective-permute-start(bf16[528,576]{1,0:T(8,128)(2,1)} %collective-permute-done.14.do2), channel_id=1, source_target_pairs={{0,1},{1,0},{2,3},{3,2},{4,5},{5,4},{6,7},{7,6},{8,9},{9,8},{10,11... | collective-permute-start | bytes 1824776 | tf_op jit(solution)/shard_map/ppermute | solution.py:768
  54.8 6.8 %collective-permute-start.12 = (bf16[144,3072]{1,0:T(8,128)(2,1)}, bf16[144,3072]{1,0:T(8,128)(2,1)}, u32[]{:S(2)}, u32[]{:S(2)}) collective-permute-start(bf16[144,3072]{1,0:T(8,128)(2,1)} %collective-permute-done.11.gu2), channel_id=1, source_target_pairs={{0,1},{1,0},{2,3},{3,2},{4,5},{5,4},{6,7},{7,6},{8,9},{9,8},{10,11... | collective-permute-start | bytes 2654216 | tf_op jit(solution)/shard_map/ppermute | solution.py:768
  55.6 8.7 %collective-permute-start.9 = (bf16[9,128,128]{2,1,0:T(8,128)(2,1)S(1)}, bf16[9,128,128]{2,1,0:T(8,128)(2,1)S(1)}, u32[]{:S(2)}, u32[]{:S(2)}) collective-permute-start(bf16[9,128,128]{2,1,0:T(8,128)(2,1)S(1)} %collective-permute-done.8), channel_id=1, source_target_pairs={{0,4},{4,0},{8,12},{12,8},{16,20},{20,16},{24,28},{28,24},{1,5},{5... | collective-permute-start | bytes 884744 | tf_op jit(solution)/shard_map/ppermute | solution.py:768
  86.3 6.1 %collective-permute-start.16 = (bf16[2,8,256,384]{3,2,1,0:T(8,128)(2,1)}, bf16[2,8,256,384]{3,2,1,0:T(8,128)(2,1)}, u32[]{:S(2)}, u32[]{:S(2)}) collective-permute-start(bf16[2,8,256,384]{3,2,1,0:T(8,128)(2,1)} %get-tuple-element.88), channel_id=1, source_target_pairs={{0,1},{1,0},{2,3},{3,2},{4,5},{5,4},{6,7},{7,6},{8,9},{9,8},{10,11... | collective-permute-start | bytes 9437192 | tf_op jit(solution)/shard_map/ppermute | solution.py:768
  96.4 36.8 %collective-permute-start.24 = (bf16[8,256,384]{2,1,0:T(8,128)(2,1)}, bf16[8,256,384]{2,1,0:T(8,128)(2,1)}, u32[]{:S(2)}, u32[]{:S(2)}) collective-permute-start(bf16[8,256,384]{2,1,0:T(8,128)(2,1)} %shard_map.220.refs_1_), channel_id=1, source_target_pairs={{0,2},{1,3},{2,0},{3,1},{4,6},{5,7},{6,4},{7,5},{8,10},{9,11},{10,... | collective-permute-start | bytes 4718600 | tf_op jit(solution)/shard_map/ppermute | solution.py:768
  97.9 9.9 %collective-permute-start.17 = (bf16[9,128,128]{2,1,0:T(8,128)(2,1)S(1)}, bf16[9,128,128]{2,1,0:T(8,128)(2,1)S(1)}, u32[]{:S(2)}, u32[]{:S(2)}) collective-permute-start(bf16[9,128,128]{2,1,0:T(8,128)(2,1)S(1)} %bitcast.66), channel_id=1, source_target_pairs={{0,4},{4,0},{8,12},{12,8},{16,20},{20,16},{24,28},{28,24},{1,5},{5... | collective-permute-start | bytes 884744 | tf_op jit(solution)/shard_map/ppermute | solution.py:768
  102.4 12.0 %collective-permute-start.18 = (bf16[9,128,128]{2,1,0:T(8,128)(2,1)}, bf16[9,128,128]{2,1,0:T(8,128)(2,1)S(1)}, u32[]{:S(2)}, u32[]{:S(2)}) collective-permute-start(bf16[9,128,128]{2,1,0:T(8,128)(2,1)} %bitcast.65), channel_id=1, source_target_pairs={{0,4},{4,0},{8,12},{12,8},{16,20},{20,16},{24,28},{28,24},{1,5},{5... | collective-permute-start | bytes 884744 | tf_op jit(solution)/shard_map/ppermute | solution.py:768
  112.7 13.1 %collective-permute-start.22 = (bf16[9,128,128]{2,1,0:T(8,128)(2,1)}, bf16[9,128,128]{2,1,0:T(8,128)(2,1)S(1)}, u32[]{:S(2)}, u32[]{:S(2)}) collective-permute-start(bf16[9,128,128]{2,1,0:T(8,128)(2,1)} %bitcast.64), channel_id=1, source_target_pairs={{0,4},{4,0},{8,12},{12,8},{16,20},{20,16},{24,28},{28,24},{1,5},{5... | collective-permute-start | bytes 884744 | tf_op jit(solution)/shard_map/ppermute | solution.py:768
  113.2 24.6 %collective-permute-start.20 = (bf16[9,128,128]{2,1,0:T(8,128)(2,1)}, bf16[9,128,128]{2,1,0:T(8,128)(2,1)S(1)}, u32[]{:S(2)}, u32[]{:S(2)}) collective-permute-start(bf16[9,128,128]{2,1,0:T(8,128)(2,1)} %get-tuple-element.99), channel_id=1, source_target_pairs={{24,0},{28,4},{25,1},{29,5},{26,2},{30,6},{27,3},{31,7}} | collective-permute-start | bytes 884744 | tf_op jit(solution)/shard_map/ppermute | solution.py:891
  123.0 14.8 %collective-permute-start.19 = (bf16[9,128,128]{2,1,0:T(8,128)(2,1)}, bf16[9,128,128]{2,1,0:T(8,128)(2,1)S(1)}, u32[]{:S(2)}, u32[]{:S(2)}) collective-permute-start(bf16[9,128,128]{2,1,0:T(8,128)(2,1)} %bitcast.63), channel_id=1, source_target_pairs={{0,4},{4,0},{8,12},{12,8},{16,20},{20,16},{24,28},{28,24},{1,5},{5... | collective-permute-start | bytes 884744 | tf_op jit(solution)/shard_map/ppermute | solution.py:768
  124.5 21.0 %collective-permute-start.21 = (bf16[9,128,128]{2,1,0:T(8,128)(2,1)}, bf16[9,128,128]{2,1,0:T(8,128)(2,1)}, u32[]{:S(2)}, u32[]{:S(2)}) collective-permute-start(bf16[9,128,128]{2,1,0:T(8,128)(2,1)} %get-tuple-element.100), channel_id=1, source_target_pairs={{16,0},{20,4},{24,8},{28,12},{17,1},{21,5},{25,9},{29,13},{18,2},{... | collective-permute-start | bytes 884744 | tf_op jit(solution)/shard_map/ppermute | solution.py:891
  128.3 18.8 %collective-permute-start.23 = (bf16[9,128,128]{2,1,0:T(8,128)(2,1)}, bf16[9,128,128]{2,1,0:T(8,128)(2,1)S(1)}, u32[]{:S(2)}, u32[]{:S(2)}) collective-permute-start(bf16[9,128,128]{2,1,0:T(8,128)(2,1)} %shard_map.224.refs_4_), channel_id=1, source_target_pairs={{8,0},{12,4},{16,8},{20,12},{24,16},{28,20},{9,1},{13,5},{17,9},{2... | collective-permute-start | bytes 884744 | tf_op jit(solution)/shard_map/ppermute | solution.py:891
  137.2 19.1 %collective-permute-start.26 = (bf16[4,256,384]{2,1,0:T(8,128)(2,1)}, bf16[4,256,384]{2,1,0:T(8,128)(2,1)}, u32[]{:S(2)}, u32[]{:S(2)}) collective-permute-start(bf16[4,256,384]{2,1,0:T(8,128)(2,1)} %get-tuple-element.107), channel_id=1, source_target_pairs={{0,4},{4,0},{8,12},{12,8},{16,20},{20,16},{24,28},{28,24},{1,5},{5... | collective-permute-start | bytes 2359304 | tf_op jit(solution)/shard_map/ppermute | solution.py:768
  137.8 9.4 %copy-start.11 = (bf16[9,128,128]{2,1,0:T(8,128)(2,1)}, bf16[9,128,128]{2,1,0:T(8,128)(2,1)S(1)}, u32[]{:S(2)}) copy-start(bf16[9,128,128]{2,1,0:T(8,128)(2,1)S(1)} %collective-permute-done.20.refs_2_) | copy-start | bytes 884740
  137.8 9.4 %copy-start.12 = (bf16[9,128,128]{2,1,0:T(8,128)(2,1)}, bf16[9,128,128]{2,1,0:T(8,128)(2,1)S(1)}, u32[]{:S(2)}) copy-start(bf16[9,128,128]{2,1,0:T(8,128)(2,1)S(1)} %collective-permute-done.19.refs_1_) | copy-start | bytes 884740
  155.1 3.4 %collective-permute-start.25 = (bf16[2,8,72,256]{3,2,1,0:T(8,128)(2,1)}, bf16[2,8,72,256]{3,2,1,0:T(8,128)(2,1)S(1)}, u32[]{:S(2)}, u32[]{:S(2)}) collective-permute-start(bf16[2,8,72,256]{3,2,1,0:T(8,128)(2,1)} %get-tuple-element.106), channel_id=1, source_target_pairs={{0,1},{1,0},{2,3},{3,2},{4,5},{5,4},{6,7},{7,6},{8,9},{9,8},{10,11... | collective-permute-start | bytes 1769480 | tf_op jit(solution)/shard_map/ppermute | solution.py:768
  162.5 29.5 %collective-permute-start.27 = (bf16[8,72,256]{2,1,0:T(8,128)(2,1)}, bf16[8,72,256]{2,1,0:T(8,128)(2,1)S(1)}, u32[]{:S(2)}, u32[]{:S(2)}) collective-permute-start(bf16[8,72,256]{2,1,0:T(8,128)(2,1)} %shard_map.228.refs_5_), channel_id=1, source_target_pairs={{0,2},{1,3},{2,0},{3,1},{4,6},{5,7},{6,4},{7,5},{8,10},{9,11},{10,... | collective-permute-start | bytes 884744 | tf_op jit(solution)/shard_map/ppermute | solution.py:768
  164.1 9.9 %collective-permute-start.28 = (bf16[256,384]{1,0:T(8,128)(2,1)}, bf16[256,384]{1,0:T(8,128)(2,1)S(1)}, u32[]{:S(2)}, u32[]{:S(2)}) collective-permute-start(bf16[256,384]{1,0:T(8,128)(2,1)} %get-tuple-element.109), channel_id=1, source_target_pairs={{0,8},{4,12},{8,0},{12,4},{16,24},{20,28},{24,16},{28,20},{1,9},{5... | collective-permute-start | bytes 589832 | tf_op jit(solution)/shard_map/ppermute | solution.py:768
  167.6 16.4 %collective-permute-start.29 = (bf16[256,384]{1,0:T(8,128)(2,1)}, bf16[256,384]{1,0:T(8,128)(2,1)S(1)}, u32[]{:S(2)}, u32[]{:S(2)}) collective-permute-start(bf16[256,384]{1,0:T(8,128)(2,1)} %get-tuple-element.110), channel_id=1, source_target_pairs={{0,16},{4,20},{8,24},{12,28},{16,0},{20,4},{24,8},{28,12},{1,17},{... | collective-permute-start | bytes 589832 | tf_op jit(solution)/shard_map/ppermute | solution.py:768
  169.0 15.0 %collective-permute-start.30 = (bf16[256,384]{1,0:T(8,128)(2,1)}, bf16[256,384]{1,0:T(8,128)(2,1)S(1)}, u32[]{:S(2)}, u32[]{:S(2)}) collective-permute-start(bf16[256,384]{1,0:T(8,128)(2,1)} %get-tuple-element.111), channel_id=1, source_target_pairs={{0,24},{4,28},{8,16},{12,20},{16,8},{20,12},{24,0},{28,4},{1,25},{... | collective-permute-start | bytes 589832 | tf_op jit(solution)/shard_map/ppermute | solution.py:768
  174.0 10.0 %copy-start.14 = (bf16[256,384]{1,0:T(8,128)(2,1)}, bf16[256,384]{1,0:T(8,128)(2,1)S(1)}, u32[]{:S(2)}) copy-start(bf16[256,384]{1,0:T(8,128)(2,1)S(1)} %collective-permute-done.28.refs_2_) | copy-start | bytes 589828
  187.3 15.4 %collective-permute-start.37 = (bf16[256,384]{1,0:T(8,128)(2,1)}, bf16[256,384]{1,0:T(8,128)(2,1)S(1)}, u32[]{:S(2)}, u32[]{:S(2)}) collective-permute-start(bf16[256,384]{1,0:T(8,128)(2,1)} %shard_map.229.refs_4_.refs_1_), channel_id=1, source_target_pairs={{0,24},{4,28},{8,16},{12,20},{16,8},{20,12},{24,0},{28,4},{1,25},{... | collective-permute-start | bytes 589832 | tf_op jit(solution)/shard_map/ppermute | solution.py:768
  189.8 17.3 %collective-permute-start.36 = (bf16[256,384]{1,0:T(8,128)(2,1)}, bf16[256,384]{1,0:T(8,128)(2,1)S(1)}, u32[]{:S(2)}, u32[]{:S(2)}) collective-permute-start(bf16[256,384]{1,0:T(8,128)(2,1)} %shard_map.229.refs_4_.refs_1_), channel_id=1, source_target_pairs={{0,16},{4,20},{8,24},{12,28},{16,0},{20,4},{24,8},{28,12},{1,17},{... | collective-permute-start | bytes 589832 | tf_op jit(solution)/shard_map/ppermute | solution.py:768
  192.0 15.1 %collective-permute-start.35 = (bf16[256,384]{1,0:T(8,128)(2,1)}, bf16[256,384]{1,0:T(8,128)(2,1)S(1)}, u32[]{:S(2)}, u32[]{:S(2)}) collective-permute-start(bf16[256,384]{1,0:T(8,128)(2,1)} %shard_map.229.refs_4_.refs_1_), channel_id=1, source_target_pairs={{0,8},{4,12},{8,0},{12,4},{16,24},{20,28},{24,16},{28,20},{1,9},{5... | collective-permute-start | bytes 589832 | tf_op jit(solution)/shard_map/ppermute | solution.py:768
  194.7 5.8 %collective-permute-start.31 = (bf16[4,72,256]{2,1,0:T(8,128)(2,1)}, bf16[4,72,256]{2,1,0:T(8,128)(2,1)S(1)}, u32[]{:S(2)}, u32[]{:S(2)}) collective-permute-start(bf16[4,72,256]{2,1,0:T(8,128)(2,1)} %get-tuple-element.113), channel_id=1, source_target_pairs={{0,4},{4,0},{8,12},{12,8},{16,20},{20,16},{24,28},{28,24},{1,5},{5... | collective-permute-start | bytes 442376 | tf_op jit(solution)/shard_map/ppermute | solution.py:768
  210.0 22.3 %collective-permute-start.42 = (bf16[4,256,384]{2,1,0:T(8,128)(2,1)}, bf16[4,256,384]{2,1,0:T(8,128)(2,1)S(1)}, u32[]{:S(2)}, u32[]{:S(2)}) collective-permute-start(bf16[4,256,384]{2,1,0:T(8,128)(2,1)} %shard_map.232.refs_5_.refs_0_), channel_id=1, source_target_pairs={{0,4},{4,0},{8,12},{12,8},{16,20},{20,16},{24,28},{28,24},{1,5},{5... | collective-permute-start | bytes 2359304 | tf_op jit(solution)/shard_map/ppermute | solution.py:768
  210.0 4.4 %collective-permute-start.32 = (bf16[72,256]{1,0:T(8,128)(2,1)}, bf16[72,256]{1,0:T(8,128)(2,1)S(1)}, u32[]{:S(2)}, u32[]{:S(2)}) collective-permute-start(bf16[72,256]{1,0:T(8,128)(2,1)} %get-tuple-element.115), channel_id=1, source_target_pairs={{0,8},{4,12},{8,0},{12,4},{16,24},{20,28},{24,16},{28,20},{1,9},{5... | collective-permute-start | bytes 110600 | tf_op jit(solution)/shard_map/ppermute | solution.py:768
  210.0 5.5 %collective-permute-start.33 = (bf16[72,256]{1,0:T(8,128)(2,1)}, bf16[72,256]{1,0:T(8,128)(2,1)S(1)}, u32[]{:S(2)}, u32[]{:S(2)}) collective-permute-start(bf16[72,256]{1,0:T(8,128)(2,1)} %get-tuple-element.116), channel_id=1, source_target_pairs={{0,16},{4,20},{8,24},{12,28},{16,0},{20,4},{24,8},{28,12},{1,17},{... | collective-permute-start | bytes 110600 | tf_op jit(solution)/shard_map/ppermute | solution.py:768
  211.4 6.0 %collective-permute-start.34 = (bf16[72,256]{1,0:T(8,128)(2,1)}, bf16[72,256]{1,0:T(8,128)(2,1)S(1)}, u32[]{:S(2)}, u32[]{:S(2)}) collective-permute-start(bf16[72,256]{1,0:T(8,128)(2,1)} %get-tuple-element.117), channel_id=1, source_target_pairs={{0,24},{4,28},{8,16},{12,20},{16,8},{20,12},{24,0},{28,4},{1,25},{... | collective-permute-start | bytes 110600 | tf_op jit(solution)/shard_map/ppermute | solution.py:768
  219.5 6.2 %collective-permute-start.40 = (bf16[72,256]{1,0:T(8,128)(2,1)}, bf16[72,256]{1,0:T(8,128)(2,1)S(1)}, u32[]{:S(2)}, u32[]{:S(2)}) collective-permute-start(bf16[72,256]{1,0:T(8,128)(2,1)} %shard_map.233.refs_1_.refs_5_), channel_id=1, source_target_pairs={{0,24},{4,28},{8,16},{12,20},{16,8},{20,12},{24,0},{28,4},{1,25},{... | collective-permute-start | bytes 110600 | tf_op jit(solution)/shard_map/ppermute | solution.py:768
  222.4 5.1 %collective-permute-start.39 = (bf16[72,256]{1,0:T(8,128)(2,1)}, bf16[72,256]{1,0:T(8,128)(2,1)S(1)}, u32[]{:S(2)}, u32[]{:S(2)}) collective-permute-start(bf16[72,256]{1,0:T(8,128)(2,1)} %shard_map.233.refs_1_.refs_5_), channel_id=1, source_target_pairs={{0,16},{4,20},{8,24},{12,28},{16,0},{20,4},{24,8},{28,12},{1,17},{... | collective-permute-start | bytes 110600 | tf_op jit(solution)/shard_map/ppermute | solution.py:768
  222.4 5.1 %collective-permute-start.38 = (bf16[72,256]{1,0:T(8,128)(2,1)}, bf16[72,256]{1,0:T(8,128)(2,1)S(1)}, u32[]{:S(2)}, u32[]{:S(2)}) collective-permute-start(bf16[72,256]{1,0:T(8,128)(2,1)} %shard_map.233.refs_1_.refs_5_), channel_id=1, source_target_pairs={{0,8},{4,12},{8,0},{12,4},{16,24},{20,28},{24,16},{28,20},{1,9},{5... | collective-permute-start | bytes 110600 | tf_op jit(solution)/shard_map/ppermute | solution.py:768
  230.2 6.4 %collective-permute-start.41 = (bf16[4,72,256]{2,1,0:T(8,128)(2,1)}, bf16[4,72,256]{2,1,0:T(8,128)(2,1)S(1)}, u32[]{:S(2)}, u32[]{:S(2)}) collective-permute-start(bf16[4,72,256]{2,1,0:T(8,128)(2,1)} %shard_map.234.refs_0_), channel_id=1, source_target_pairs={{0,4},{4,0},{8,12},{12,8},{16,20},{20,16},{24,28},{28,24},{1,5},{5... | collective-permute-start | bytes 442376 | tf_op jit(solution)/shard_map/ppermute | solution.py:768
  (29 other events, 50.6 us)

commit v2 on v1

--- a/solution.py
+++ b/solution.py
@@ -27,7 +27,7 @@
 NN = (((1,), (0,)), ((), ()))
 NT = (((1,), (1,)), ((), ()))
 TN = (((0,), (0,)), ((), ()))
-VMEM_LIMIT = 63 * 1024 * 1024
+VMEM_LIMIT = 64 * 1024 * 1024 - 65536
 PER_US = 1.0e9
 
 
@@ -788,8 +788,37 @@
     refs[-1][...] = total_of(*(ref[...] for ref in refs[:-1]))
 
 
-def core_kernel(place_ref, keep, got, out):
-    out[...] = total_of(keep[0], got[0])
+def core_kernel(place_ref, keep, got, *refs):
+    out, keep_all, got_all, out_all, sems = refs[-5:]
+    loads = []
+    for c in range(CHUNKS):
+        for i, (source, target) in enumerate(((keep, keep_all), (got, got_all))):
+            copy = pltpu.make_async_copy(source.at[1, c], target.at[c], sems.at[i, c])
+            copy.start()
+            loads.append(copy)
+    stores = []
+    for c in range(CHUNKS):
+        loads[2 * c].wait()
+        loads[2 * c + 1].wait()
+        out_all[c] = total_of(keep_all[c], got_all[c])
+        copy = pltpu.make_async_copy(out_all.at[c], out.at[c], sems.at[2, c])
+        copy.start()
+        stores.append(copy)
+    for copy in stores:
+        copy.wait()
+
+
+def core_sum(place, keep, got, after):
+    hbm = pl.BlockSpec(memory_space=pl.ANY)
+    shape = keep.shape[1:]
+    return call(
+        core_kernel,
+        sds(shape, BF16),
+        [pl.BlockSpec(memory_space=pltpu.SMEM)] + [hbm] * (2 + len(after)),
+        cost=0.05,
+        out_specs=hbm,
+        scratch_shapes=[pltpu.VMEM(shape, BF16)] * 3 + [pltpu.SemaphoreType.DMA((3, CHUNKS))],
+    )(place, keep, got, *after)
 
 
 def y_kernel(place_ref, keep, got, far, mine, away):
@@ -837,19 +866,7 @@
 
     def core(self, *after):
         keep, got = self.parts
-        two = (2,) + self.shape
-        source = pl.BlockSpec((1,) + two, lambda i: (1, i, 0, 0))
-        target = pl.BlockSpec(two, lambda i: (i, 0, 0))
-        (away,) = fuse(
-            core_kernel,
-            self.place,
-            [(CHUNKS,) + self.shape],
-            self.parts,
-            after,
-            [source, source],
-            (target,),
-            (CHUNKS // 2,),
-        )
+        away = core_sum(self.place, keep, got, after)
         self.parts = (keep, got, flip(away, "fsdp", 2))
         return away
 

time: 240 us -> 233 us (0.971)
  local copies, waits for them, and re-layouts: 12.1 us -> 0.02 us
  other arithmetic: 4.09 us -> 7.9 us
    unnamed x68 -> x0, local copies, waits for them, and re-layouts: 12 us -> none
    pallas_call x11 -> x9, Pallas kernels: 26.1 us -> 19 us  [fuse(): call(body, tuple((sds(shape, BF16) for shape in outs)), [pl.BlockSpec(mem...]
    pallas_call x0 -> x2, Pallas kernels: none -> 6.06 us  [core_sum(): call(core_kernel, sds(shape, BF16), [pl.BlockSpec(memory_space=pltpu.SMEM...]
    ppermute x37, waiting for transfers between devices: 44.9 us -> 49.8 us  [flip(): return lax.ppermute(x, axis, [(i, i ^ mask) for i in range(n)])]
  transfers between devices with their start and end apart: 43 -> 43, of which waited for: 18 -> 19; matrix products, arithmetic and copies ran while one was open for 2% -> 3% of each run, Pallas kernels for 28% -> 29%
where the time goes in v2:
time: 233 us
  Pallas kernels  102 us (44%)
  starting transfers between devices  61.1 us (26%)
  waiting for transfers between devices  61.1 us (26%)
  other arithmetic  7.9 us (3%)
    ppermute x37, waiting for transfers between devices, flip(): return lax.ppermute(x, axis, [(i, i ^ mask) for i in range(n)])  49.8 us
    ppermute x37, starting transfers between devices, flip(): return lax.ppermute(x, axis, [(i, i ^ mask) for i in range(n)])  42.8 us
    pallas_call x1, Pallas kernels, middle(): call(functools.partial(middle_kernel, fused), (sds((tiles // KV_HEADS, di...  21.3 us
    pallas_call x4, Pallas kernels, attend_back(): call(functools.partial(attend_back_kernel, steps, diagonal, carry is None...  19.3 us
    pallas_call x9, Pallas kernels, fuse(): call(body, tuple((sds(shape, BF16) for shape in outs)), [pl.BlockSpec(mem...  19 us
    pallas_call x3, Pallas kernels, attend(): call(functools.partial(attend_kernel, steps, diagonal, carry is None), (s...  14.5 us
    ppermute x3, starting transfers between devices, local(): piece = lax.ppermute(piece, 'ctx', up)  14.2 us
    ppermute x3, waiting for transfers between devices, send_down(): lax.ppermute(x, 'ctx', [(i, i - 2 * levels) for i in range(2 * levels, n)])  7.89 us
  transfers between devices with their start and end apart: 43, of which 19 were waited for; matrix products, arithmetic and copies ran while one was open for 3% of the time, Pallas kernels for 29%

profile of v2, /device:TPU:0, one launch (start us, length us, event | category | flops | bytes accessed | tf_op | source)
XLA Modules:
  0.0 232.6 jit_solution(15403322876985145294)
XLA Ops:
  0.6 1.9 shard_map.212.w0
  2.6 3.0 %collective-permute-start.1 = (bf16[144,1024]{1,0:T(8,128)(2,1)}, bf16[144,1024]{1,0:T(8,128)(2,1)}, u32[]{:S(2)}, u32[]{:S(2)}) collective-permute-start(bf16[144,1024]{1,0:T(8,128)(2,1)} %shard_map.212.w0), channel_id=1, source_target_pairs={{0,2},{1,3},{2,0},{3,1},{4,6},{5,7},{6,4},{7,5},{8,10},{9,11},{10,... | collective-permute-start | bytes 884744 | tf_op jit(solution)/shard_map/ppermute | solution.py:768
  5.5 2.7 %shard_map.217 = (bf16[144,3072]{1,0:T(8,128)(2,1)}, bf16[528,576]{1,0:T(8,128)(2,1)}) custom-call(bf16[144,1536]{1,0:T(8,128)(2,1)} %gate_ref.1, bf16[144,1536]{1,0:T(8,128)(2,1)} %up_ref.1, bf16[576,384]{1,0:T(8,128)(2,1)} %bitcast.50, bf16[144,576]{1,0:T(8,128)(2,1)} %w_ref.1), custom_call_target="tpu_custom_call" | custom-call | flops 3000000000 | tf_op jit(solution)/shard_map/pallas_call | solution.py:967
  8.7 1.7 collective-permute-start.11
  11.2 2.5 %collective-permute-done.1.w2 = bf16[144,1024]{1,0:T(8,128)(2,1)} collective-permute-done((bf16[144,1024]{1,0:T(8,128)(2,1)}, bf16[144,1024]{1,0:T(8,128)(2,1)}, u32[]{:S(2)}, u32[]{:S(2)}) %collective-permute-start.1) | collective-permute-done | bytes 294944 | tf_op jit(solution)/shard_map/ppermute | solution.py:768
  17.5 4.2 %shard_map.213 = (bf16[576,1024]{1,0:T(8,128)(2,1)}, bf16[384,576]{1,0:T(8,128)(2,1)}, bf16[9,384,128]{2,1,0:T(8,128)(2,1)}, bf16[9,128,128]{2,1,0:T(8,128)(2,1)...) custom-call(s32[1]{0:T(128)} %bitcast.index_ref, bf16[3,576,128]{2,1,0:T(8,128)(2,1)} %bitcast.51, ...), custom_call_target="tpu_custom_call" | custom-call | flops 4000000000 | tf_op jit(solution)/shard_map/pallas_call | solution.py:952
  21.7 2.0 collective-permute-start.7
  23.7 4.2 %collective-permute-start.3 = (bf16[9,128,128]{2,1,0:T(8,128)(2,1)}, bf16[9,128,128]{2,1,0:T(8,128)(2,1)}, u32[]{:S(2)}, u32[]{:S(2)}) collective-permute-start(bf16[9,128,128]{2,1,0:T(8,128)(2,1)} %get-tuple-element.72), channel_id=1, source_target_pairs={{0,8},{4,12},{8,16},{12,20},{16,24},{20,28},{1,9},{5,13},{9,17},{1... | collective-permute-start | bytes 884744 | tf_op jit(solution)/shard_map/ppermute | solution.py:996
  30.6 3.5 %collective-permute-done.3 = bf16[9,128,128]{2,1,0:T(8,128)(2,1)} collective-permute-done((bf16[9,128,128]{2,1,0:T(8,128)(2,1)}, bf16[9,128,128]{2,1,0:T(8,128)(2,1)}, u32[]{:S(2)}, u32[]{:S(2)}) %collective-permute-start.3) | collective-permute-done | bytes 294944 | tf_op jit(solution)/shard_map/ppermute | solution.py:996
  34.7 5.1 %collective-permute-start.4 = (bf16[9,128,128]{2,1,0:T(8,128)(2,1)}, bf16[9,128,128]{2,1,0:T(8,128)(2,1)}, u32[]{:S(2)}, u32[]{:S(2)}) collective-permute-start(bf16[9,128,128]{2,1,0:T(8,128)(2,1)} %collective-permute-done.3), channel_id=1, source_target_pairs={{0,8},{4,12},{8,16},{12,20},{16,24},{20,28},{1,9},{5,13},{9,17},{1... | collective-permute-start | bytes 884744 | tf_op jit(solution)/shard_map/ppermute | solution.py:996
  39.8 5.4 %shard_map.214 = (f32[9,384,128]{2,1,0:T(8,128)}, f32[9,384,128]{2,1,0:T(8,128)}) custom-call(s32[9]{0:T(128)} %get-tuple-element.130.info_ref, bf16[9,384,128]{2,1,0:T(8,128)(2,1)} %get-tuple-element.71.q_ref, bf16[1,9,128,128]{3,2,1,0:T(8,128)(2,1)} %bitcast.42, bf16[1,9,128,128]{3,2,1,0:T(8,128)(2,1)} %bitcast.18.b_ref), custom_call_target="tpu_custom_call" | custom-call | flops 10000000000 | tf_op jit(solution)/shard_map/pallas_call | solution.py:224
  45.2 4.9 %collective-permute-start.8 = (bf16[9,128,128]{2,1,0:T(8,128)(2,1)}, bf16[9,128,128]{2,1,0:T(8,128)(2,1)}, u32[]{:S(2)}, u32[]{:S(2)}) collective-permute-start(bf16[9,128,128]{2,1,0:T(8,128)(2,1)} %collective-permute-done.4), channel_id=1, source_target_pairs={{0,8},{4,12},{8,16},{12,20},{16,24},{20,28},{1,9},{5,13},{9,17},{1... | collective-permute-start | bytes 884744 | tf_op jit(solution)/shard_map/ppermute | solution.py:996
  51.5 4.6 %shard_map.215 = (f32[9,384,128]{2,1,0:T(8,128)}, f32[9,384,128]{2,1,0:T(8,128)}) custom-call(s32[9]{0:T(128)} %get-tuple-element.132.info_ref, bf16[9,384,128]{2,1,0:T(8,128)(2,1)} %get-tuple-element.71.q_ref, bf16[1,9,128,128]{3,2,1,0:T(8,128)(2,1)} %bitcast.13.a_ref, bf16[1,9,128,128]{3,2,1,0:T(8,128)(2,1)} %bitcast.14.b_ref, ...), custom_call_target="tpu_custom_call" | custom-call | flops 10000000000 | tf_op jit(solution)/shard_map/pallas_call | solution.py:224
  58.7 4.6 %shard_map.216 = (f32[9,384,128]{2,1,0:T(8,128)}, f32[9,384,128]{2,1,0:T(8,128)}) custom-call(s32[9]{0:T(128)} %get-tuple-element.131.info_ref, bf16[9,384,128]{2,1,0:T(8,128)(2,1)} %get-tuple-element.71.q_ref, bf16[1,9,128,128]{3,2,1,0:T(8,128)(2,1)} %bitcast.9.a_ref, bf16[1,9,128,128]{3,2,1,0:T(8,128)(2,1)} %bitcast.10.b_ref, ...), custom_call_target="tpu_custom_call" | custom-call | flops 10000000000 | tf_op jit(solution)/shard_map/pallas_call | solution.py:224
  63.3 3.1 %collective-permute-done.9 = bf16[9,128,128]{2,1,0:T(8,128)(2,1)} collective-permute-done((bf16[9,128,128]{2,1,0:T(8,128)(2,1)}, bf16[9,128,128]{2,1,0:T(8,128)(2,1)}, u32[]{:S(2)}, u32[]{:S(2)}) %collective-permute-start.9) | collective-permute-done | bytes 294944 | tf_op jit(solution)/shard_map/ppermute | solution.py:768
  66.3 21.3 %shard_map.218 = (f32[3,576,128]{2,1,0:T(8,128)}, f32[384,576]{1,0:T(8,128)}, bf16[9,384,128]{2,1,0:T(8,128)(2,1)}, f32[9,8,384]{2,1,0:T(8,128)}, bf16[2,8,256,3...) custom-call(s32[1]{0:T(128)} %bitcast.index_ref, s32[9]{0:T(128)} %get-tuple-element.133.info_ref, ...), custom_call_target="tpu_custom_call" | custom-call | flops 20000000000 | tf_op jit(solution)/shard_map/pallas_call | solution.py:531
  88.4 3.5 %shard_map.219 = (f32[9,384,128]{2,1,0:T(8,128)}, bf16[1,9,128,128]{3,2,1,0:T(8,128)(2,1)}, bf16[1,9,128,128]{3,2,1,0:T(8,128)(2,1)}) custom-call(s32[9]{0:T(128)} %get-tuple-element.133.info_ref, bf16[9,384,128]{2,1,0:T(8,128)(2,1)} %get-tuple-element.71.q_ref, bf16[9,384,128]{2,1,0:T(8,128)(2,1)} %get-tuple-element.84.d_ref, ...), custom_call_target="tpu_custom_call" | custom-call | flops 50000000 | tf_op jit(solution)/shard_map/pallas_call | solution.py:305
  91.9 1.8 collective-permute-done.16.got.refs_2_
  93.7 3.5 %shard_map.220.refs_1_ = bf16[8,256,384]{2,1,0:T(8,128)(2,1)} custom-call(s32[3]{0:T(128)} %pad_add_fusion.place_ref.refs_0_, bf16[2,8,256,384]{3,2,1,0:T(8,128)(2,1)} %get-tuple-element.87.keep.refs_1_, bf16[2,8,256,384]{3,2,1,0:T(8,128)(2,1)} %collective-permute-done.16.got.refs_2_, f32[9,384,128]{2,1,0:T(8,128)} %get-tuple-element.86.refs_0_), custom_call_target="tpu_custom_call" | custom-call | flops 50000000 | tf_op jit(solution)/shard_map/pallas_call | solution.py:814
  99.4 3.9 %shard_map.221 = (f32[9,384,128]{2,1,0:T(8,128)}, bf16[1,9,128,128]{3,2,1,0:T(8,128)(2,1)}, bf16[1,9,128,128]{3,2,1,0:T(8,128)(2,1)}) custom-call(s32[9]{0:T(128)} %get-tuple-element.131.info_ref, bf16[9,384,128]{2,1,0:T(8,128)(2,1)} %get-tuple-element.71.q_ref, bf16[9,384,128]{2,1,0:T(8,128)(2,1)} %get-tuple-element.84.d_ref, ...), custom_call_target="tpu_custom_call" | custom-call | flops 50000000 | tf_op jit(solution)/shard_map/pallas_call | solution.py:305
  104.8 4.3 %collective-permute-done.17.refs_2_ = bf16[9,128,128]{2,1,0:T(8,128)(2,1)} collective-permute-done((bf16[9,128,128]{2,1,0:T(8,128)(2,1)}, bf16[9,128,128]{2,1,0:T(8,128)(2,1)}, u32[]{:S(2)}, u32[]{:S(2)}) %collective-permute-start.17) | collective-permute-done | bytes 294944 | tf_op jit(solution)/shard_map/ppermute | solution.py:768
  109.1 4.1 %shard_map.222 = (f32[9,384,128]{2,1,0:T(8,128)}, bf16[1,9,128,128]{3,2,1,0:T(8,128)(2,1)}, bf16[1,9,128,128]{3,2,1,0:T(8,128)(2,1)}, bf16[9,128,128]{2,1,0:T(8,128)(2,1)}) custom-call(s32[9]{0:T(128)} %get-tuple-element.132.info_ref, bf16[9,384,128]{2,1,0:T(8,128)(2,1)} %get-tuple-element.71.q_ref, bf16[9,384,128]{2,1,0:T(8,128)(2,1)} %get-tuple-element.84.d_ref, ...), custom_call_target="tpu_custom_call" | custom-call | flops 50000000 | tf_op jit(solution)/shard_map/pallas_call | solution.py:305
  115.0 7.7 %shard_map.223 = (f32[9,384,128]{2,1,0:T(8,128)}, bf16[1,9,128,128]{3,2,1,0:T(8,128)(2,1)}, bf16[1,9,128,128]{3,2,1,0:T(8,128)(2,1)}, bf16[9,128,128]{2,1,0:T(8,128)(2,1)}) custom-call(s32[9]{0:T(128)} %get-tuple-element.130.info_ref, bf16[9,384,128]{2,1,0:T(8,128)(2,1)} %get-tuple-element.71.q_ref, bf16[9,384,128]{2,1,0:T(8,128)(2,1)} %get-tuple-element.84.d_ref, ...), custom_call_target="tpu_custom_call" | custom-call | flops 50000000 | tf_op jit(solution)/shard_map/pallas_call | solution.py:305
  125.5 1.8 shard_map.224.refs_4_
  128.9 5.1 %collective-permute-done.24.refs_3_ = bf16[8,256,384]{2,1,0:T(8,128)(2,1)} collective-permute-done((bf16[8,256,384]{2,1,0:T(8,128)(2,1)}, bf16[8,256,384]{2,1,0:T(8,128)(2,1)}, u32[]{:S(2)}, u32[]{:S(2)}) %collective-permute-start.24) | collective-permute-done | bytes 1572896 | tf_op jit(solution)/shard_map/ppermute | solution.py:768
  134.1 4.0 %shard_map.225 = (bf16[4,256,384]{2,1,0:T(8,128)(2,1)}, bf16[4,256,384]{2,1,0:T(8,128)(2,1)}) custom-call(s32[3]{0:T(128)} %pad_add_fusion.place_ref.refs_0_, bf16[2,8,256,384]{3,2,1,0:T(8,128)(2,1)} %get-tuple-element.87.keep.refs_1_, bf16[2,8,256,384]{3,2,1,0:T(8,128)(2,1)} %collective-permute-done.16.got.refs_2_, ...), custom_call_target="tpu_custom_call" | custom-call | flops 50000000 | tf_op jit(solution)/shard_map/pallas_call | solution.py:850
  138.6 7.0 %collective-permute-done.21.refs_3_ = bf16[9,128,128]{2,1,0:T(8,128)(2,1)} collective-permute-done((bf16[9,128,128]{2,1,0:T(8,128)(2,1)}, bf16[9,128,128]{2,1,0:T(8,128)(2,1)}, u32[]{:S(2)}, u32[]{:S(2)}) %collective-permute-start.21) | collective-permute-done | bytes 294944 | tf_op jit(solution)/shard_map/ppermute | solution.py:908
  146.5 7.2 %shard_map.226 = (f32[3,576,128]{2,1,0:T(8,128)}, bf16[2,8,72,256]{3,2,1,0:T(8,128)(2,1)}, bf16[2,8,72,256]{3,2,1,0:T(8,128)(2,1)}) custom-call(s32[1]{0:T(128)} %bitcast.index_ref, bf16[384,576]{1,0:T(8,128)(2,1)} %get-tuple-element.69.x_ref, bf16[384,576]{1,0:T(8,128)(2,1)} %get-tuple-element.82.normed_ref, bf16[576,1024]{1,0:T(8,128)(2,1)} %get-tuple-element.83.w_ref, ...), custom_call_target="tpu_custom_call" | custom-call | flops 50000000 | tf_op jit(solution)/shard_map/pallas_call | solution.py:652
  153.8 3.4 %collective-permute-done.26.refs_2_ = bf16[4,256,384]{2,1,0:T(8,128)(2,1)} collective-permute-done((bf16[4,256,384]{2,1,0:T(8,128)(2,1)}, bf16[4,256,384]{2,1,0:T(8,128)(2,1)}, u32[]{:S(2)}, u32[]{:S(2)}) %collective-permute-start.26) | collective-permute-done | bytes 786464 | tf_op jit(solution)/shard_map/ppermute | solution.py:768
  157.2 2.3 shard_map.227
  159.5 2.5 %shard_map.228.refs_5_ = bf16[8,72,256]{2,1,0:T(8,128)(2,1)} custom-call(s32[3]{0:T(128)} %pad_add_fusion.place_ref.refs_0_, bf16[2,8,72,256]{3,2,1,0:T(8,128)(2,1)} %get-tuple-element.105.refs_3_.keep.refs_1_, bf16[2,8,72,256]{3,2,1,0:T(8,128)(2,1)} %collective-permute-done.25.got.refs_2_, bf16[256,384]{1,0:T(8,128)(2,1)} %get-tuple-element.108.refs_0_.refs_1_), custom_call_target="tpu_custom_call" | custom-call | flops 50000000 | tf_op jit(solution)/shard_map/pallas_call | solution.py:814
  163.6 2.4 %collective-permute-start.28 = (bf16[256,384]{1,0:T(8,128)(2,1)}, bf16[256,384]{1,0:T(8,128)(2,1)}, u32[]{:S(2)}, u32[]{:S(2)}) collective-permute-start(bf16[256,384]{1,0:T(8,128)(2,1)} %get-tuple-element.109), channel_id=1, source_target_pairs={{0,8},{4,12},{8,0},{12,4},{16,24},{20,28},{24,16},{28,20},{1,9},{5... | collective-permute-start | bytes 589832 | tf_op jit(solution)/shard_map/ppermute | solution.py:768
  169.2 3.9 %collective-permute-done.28.refs_2_ = bf16[256,384]{1,0:T(8,128)(2,1)} collective-permute-done((bf16[256,384]{1,0:T(8,128)(2,1)}, bf16[256,384]{1,0:T(8,128)(2,1)}, u32[]{:S(2)}, u32[]{:S(2)}) %collective-permute-start.28) | collective-permute-done | bytes 196640 | tf_op jit(solution)/shard_map/ppermute | solution.py:768
  173.1 10.0 %collective-permute-done.29.refs_3_ = bf16[256,384]{1,0:T(8,128)(2,1)} collective-permute-done((bf16[256,384]{1,0:T(8,128)(2,1)}, bf16[256,384]{1,0:T(8,128)(2,1)}, u32[]{:S(2)}, u32[]{:S(2)}) %collective-permute-start.29) | collective-permute-done | bytes 196640 | tf_op jit(solution)/shard_map/ppermute | solution.py:768
  183.1 2.0 shard_map.229.refs_4_.refs_1_
  185.1 2.5 %collective-permute-start.37 = (bf16[256,384]{1,0:T(8,128)(2,1)}, bf16[256,384]{1,0:T(8,128)(2,1)}, u32[]{:S(2)}, u32[]{:S(2)}) collective-permute-start(bf16[256,384]{1,0:T(8,128)(2,1)} %shard_map.229.refs_4_.refs_1_), channel_id=1, source_target_pairs={{0,24},{4,28},{8,16},{12,20},{16,8},{20,12},{24,0},{28,4},{1,25},{... | collective-permute-start | bytes 589832 | tf_op jit(solution)/shard_map/ppermute | solution.py:768
  187.6 4.2 %collective-permute-start.36 = (bf16[256,384]{1,0:T(8,128)(2,1)}, bf16[256,384]{1,0:T(8,128)(2,1)}, u32[]{:S(2)}, u32[]{:S(2)}) collective-permute-start(bf16[256,384]{1,0:T(8,128)(2,1)} %shard_map.229.refs_4_.refs_1_), channel_id=1, source_target_pairs={{0,16},{4,20},{8,24},{12,28},{16,0},{20,4},{24,8},{28,12},{1,17},{... | collective-permute-start | bytes 589832 | tf_op jit(solution)/shard_map/ppermute | solution.py:768
  191.8 2.0 shard_map.230
  194.3 4.9 %collective-permute-done.31.refs_2_ = bf16[4,72,256]{2,1,0:T(8,128)(2,1)} collective-permute-done((bf16[4,72,256]{2,1,0:T(8,128)(2,1)}, bf16[4,72,256]{2,1,0:T(8,128)(2,1)}, u32[]{:S(2)}, u32[]{:S(2)}) %collective-permute-start.31) | collective-permute-done | bytes 147488 | tf_op jit(solution)/shard_map/ppermute | solution.py:768
  200.9 2.9 %collective-permute-done.36.refs_3_ = bf16[256,384]{1,0:T(8,128)(2,1)} collective-permute-done((bf16[256,384]{1,0:T(8,128)(2,1)}, bf16[256,384]{1,0:T(8,128)(2,1)}, u32[]{:S(2)}, u32[]{:S(2)}) %collective-permute-start.36) | collective-permute-done | bytes 196640 | tf_op jit(solution)/shard_map/ppermute | solution.py:768
  203.8 2.2 shard_map.232.refs_5_.refs_0_
  206.4 2.1 collective-permute-start.33
  208.5 2.3 collective-permute-start.34
  211.6 3.0 %collective-permute-done.34.refs_4_ = bf16[72,256]{1,0:T(8,128)(2,1)} collective-permute-done((bf16[72,256]{1,0:T(8,128)(2,1)}, bf16[72,256]{1,0:T(8,128)(2,1)}, u32[]{:S(2)}, u32[]{:S(2)}) %collective-permute-start.34) | collective-permute-done | bytes 36896 | tf_op jit(solution)/shard_map/ppermute | solution.py:768
  216.1 2.4 %collective-permute-start.40 = (bf16[72,256]{1,0:T(8,128)(2,1)}, bf16[72,256]{1,0:T(8,128)(2,1)}, u32[]{:S(2)}, u32[]{:S(2)}) collective-permute-start(bf16[72,256]{1,0:T(8,128)(2,1)} %shard_map.233.refs_1_.refs_5_), channel_id=1, source_target_pairs={{0,24},{4,28},{8,16},{12,20},{16,8},{20,12},{24,0},{28,4},{1,25},{... | collective-permute-start | bytes 110600 | tf_op jit(solution)/shard_map/ppermute | solution.py:768
  218.5 2.0 collective-permute-start.38
  226.8 3.5 %shard_map.235 = (f32[144,1536]{1,0:T(8,128)}, f32[144,1536]{1,0:T(8,128)}, f32[576,384]{1,0:T(8,128)}, f32[144,576]{1,0:T(8,128)}, f32[1,144]{1,0:T(1,128)}) custom-call(s32[3]{0:T(128)} %pad_add_fusion.place_ref.refs_0_, bf16[4,256,384]{2,1,0:T(8,128)(2,1)} %shard_map.232.refs_5_.refs_0_, bf16[4,256,384]{2,1,0:T(8,128)(2,1)} %collective-permute-done.42.refs_1_), custom_call_target="tpu_custom_call" | custom-call | flops 50000000 | tf_op jit(solution)/shard_map/pallas_call | solution.py:730
  230.6 2.0 shard_map.236
  (75 shorter events, 40.5 us)
Async XLA Ops:
  2.6 11.1 %collective-permute-start.1 = (bf16[144,1024]{1,0:T(8,128)(2,1)}, bf16[144,1024]{1,0:T(8,128)(2,1)}, u32[]{:S(2)}, u32[]{:S(2)}) collective-permute-start(bf16[144,1024]{1,0:T(8,128)(2,1)} %shard_map.212.w0), channel_id=1, source_target_pairs={{0,2},{1,3},{2,0},{3,1},{4,6},{5,7},{6,4},{7,5},{8,10},{9,11},{10,... | collective-permute-start | bytes 884744 | tf_op jit(solution)/shard_map/ppermute | solution.py:768
  5.5 11.9 %collective-permute-start = (bf16[144,1024]{1,0:T(8,128)(2,1)}, bf16[144,1024]{1,0:T(8,128)(2,1)}, u32[]{:S(2)}, u32[]{:S(2)}) collective-permute-start(bf16[144,1024]{1,0:T(8,128)(2,1)} %shard_map.212.w0), channel_id=1, source_target_pairs={{0,1},{1,0},{2,3},{3,2},{4,5},{5,4},{6,7},{7,6},{8,9},{9,8},{10,11... | collective-permute-start | bytes 884744 | tf_op jit(solution)/shard_map/ppermute | solution.py:768
  8.2 47.9 %collective-permute-start.14 = (bf16[528,576]{1,0:T(8,128)(2,1)}, bf16[528,576]{1,0:T(8,128)(2,1)}, u32[]{:S(2)}, u32[]{:S(2)}) collective-permute-start(bf16[528,576]{1,0:T(8,128)(2,1)} %get-tuple-element.80.do0), channel_id=1, source_target_pairs={{0,2},{1,3},{2,0},{3,1},{4,6},{5,7},{6,4},{7,5},{8,10},{9,11},{10,... | collective-permute-start | bytes 1824776 | tf_op jit(solution)/shard_map/ppermute | solution.py:768
  8.2 55.0 %collective-permute-start.13 = (bf16[528,576]{1,0:T(8,128)(2,1)}, bf16[528,576]{1,0:T(8,128)(2,1)}, u32[]{:S(2)}, u32[]{:S(2)}) collective-permute-start(bf16[528,576]{1,0:T(8,128)(2,1)} %get-tuple-element.80.do0), channel_id=1, source_target_pairs={{0,1},{1,0},{2,3},{3,2},{4,5},{5,4},{6,7},{7,6},{8,9},{9,8},{10,11... | collective-permute-start | bytes 1824776 | tf_op jit(solution)/shard_map/ppermute | solution.py:768
  8.7 47.4 %collective-permute-start.11 = (bf16[144,3072]{1,0:T(8,128)(2,1)}, bf16[144,3072]{1,0:T(8,128)(2,1)}, u32[]{:S(2)}, u32[]{:S(2)}) collective-permute-start(bf16[144,3072]{1,0:T(8,128)(2,1)} %get-tuple-element.79.gu0), channel_id=1, source_target_pairs={{0,2},{1,3},{2,0},{3,1},{4,6},{5,7},{6,4},{7,5},{8,10},{9,11},{10,... | collective-permute-start | bytes 2654216 | tf_op jit(solution)/shard_map/ppermute | solution.py:768
  13.7 3.8 %collective-permute-start.2 = (bf16[144,1024]{1,0:T(8,128)(2,1)}, bf16[144,1024]{1,0:T(8,128)(2,1)}, u32[]{:S(2)}, u32[]{:S(2)}) collective-permute-start(bf16[144,1024]{1,0:T(8,128)(2,1)} %collective-permute-done.1.w2), channel_id=1, source_target_pairs={{0,1},{1,0},{2,3},{3,2},{4,5},{5,4},{6,7},{7,6},{8,9},{9,8},{10,11... | collective-permute-start | bytes 884744 | tf_op jit(solution)/shard_map/ppermute | solution.py:768
  21.7 13.0 %collective-permute-start.7 = (bf16[9,128,128]{2,1,0:T(8,128)(2,1)}, bf16[9,128,128]{2,1,0:T(8,128)(2,1)}, u32[]{:S(2)}, u32[]{:S(2)}) collective-permute-start(bf16[9,128,128]{2,1,0:T(8,128)(2,1)} %get-tuple-element.72), channel_id=1, source_target_pairs={{0,4},{4,0},{8,12},{12,8},{16,20},{20,16},{24,28},{28,24},{1,5},{5... | collective-permute-start | bytes 884744 | tf_op jit(solution)/shard_map/ppermute | solution.py:768
  23.7 10.4 %collective-permute-start.3 = (bf16[9,128,128]{2,1,0:T(8,128)(2,1)}, bf16[9,128,128]{2,1,0:T(8,128)(2,1)}, u32[]{:S(2)}, u32[]{:S(2)}) collective-permute-start(bf16[9,128,128]{2,1,0:T(8,128)(2,1)} %get-tuple-element.72), channel_id=1, source_target_pairs={{0,8},{4,12},{8,16},{12,20},{16,24},{20,28},{1,9},{5,13},{9,17},{1... | collective-permute-start | bytes 884744 | tf_op jit(solution)/shard_map/ppermute | solution.py:996
  34.1 15.9 %collective-permute-start.6 = (bf16[9,128,128]{2,1,0:T(8,128)(2,1)}, bf16[9,128,128]{2,1,0:T(8,128)(2,1)}, u32[]{:S(2)}, u32[]{:S(2)}) collective-permute-start(bf16[9,128,128]{2,1,0:T(8,128)(2,1)} %collective-permute-done.3), channel_id=1, source_target_pairs={{0,4},{4,0},{8,12},{12,8},{16,20},{20,16},{24,28},{28,24},{1,5},{5... | collective-permute-start | bytes 884744 | tf_op jit(solution)/shard_map/ppermute | solution.py:768
  34.7 10.5 %collective-permute-start.4 = (bf16[9,128,128]{2,1,0:T(8,128)(2,1)}, bf16[9,128,128]{2,1,0:T(8,128)(2,1)}, u32[]{:S(2)}, u32[]{:S(2)}) collective-permute-start(bf16[9,128,128]{2,1,0:T(8,128)(2,1)} %collective-permute-done.3), channel_id=1, source_target_pairs={{0,8},{4,12},{8,16},{12,20},{16,24},{20,28},{1,9},{5,13},{9,17},{1... | collective-permute-start | bytes 884744 | tf_op jit(solution)/shard_map/ppermute | solution.py:996
  45.2 11.4 %collective-permute-start.8 = (bf16[9,128,128]{2,1,0:T(8,128)(2,1)}, bf16[9,128,128]{2,1,0:T(8,128)(2,1)}, u32[]{:S(2)}, u32[]{:S(2)}) collective-permute-start(bf16[9,128,128]{2,1,0:T(8,128)(2,1)} %collective-permute-done.4), channel_id=1, source_target_pairs={{0,8},{4,12},{8,16},{12,20},{16,24},{20,28},{1,9},{5,13},{9,17},{1... | collective-permute-start | bytes 884744 | tf_op jit(solution)/shard_map/ppermute | solution.py:996
  50.0 7.2 %collective-permute-start.5 = (bf16[9,128,128]{2,1,0:T(8,128)(2,1)}, bf16[9,128,128]{2,1,0:T(8,128)(2,1)}, u32[]{:S(2)}, u32[]{:S(2)}) collective-permute-start(bf16[9,128,128]{2,1,0:T(8,128)(2,1)} %collective-permute-done.4), channel_id=1, source_target_pairs={{0,4},{4,0},{8,12},{12,8},{16,20},{20,16},{24,28},{28,24},{1,5},{5... | collective-permute-start | bytes 884744 | tf_op jit(solution)/shard_map/ppermute | solution.py:768
  56.1 7.2 %collective-permute-start.10 = (bf16[144,3072]{1,0:T(8,128)(2,1)}, bf16[144,3072]{1,0:T(8,128)(2,1)}, u32[]{:S(2)}, u32[]{:S(2)}) collective-permute-start(bf16[144,3072]{1,0:T(8,128)(2,1)} %get-tuple-element.79.gu0), channel_id=1, source_target_pairs={{0,1},{1,0},{2,3},{3,2},{4,5},{5,4},{6,7},{7,6},{8,9},{9,8},{10,11... | collective-permute-start | bytes 2654216 | tf_op jit(solution)/shard_map/ppermute | solution.py:768
  56.1 7.1 %collective-permute-start.15 = (bf16[528,576]{1,0:T(8,128)(2,1)}, bf16[528,576]{1,0:T(8,128)(2,1)}, u32[]{:S(2)}, u32[]{:S(2)}) collective-permute-start(bf16[528,576]{1,0:T(8,128)(2,1)} %collective-permute-done.14.do2), channel_id=1, source_target_pairs={{0,1},{1,0},{2,3},{3,2},{4,5},{5,4},{6,7},{7,6},{8,9},{9,8},{10,11... | collective-permute-start | bytes 1824776 | tf_op jit(solution)/shard_map/ppermute | solution.py:768
  56.6 6.7 %collective-permute-start.12 = (bf16[144,3072]{1,0:T(8,128)(2,1)}, bf16[144,3072]{1,0:T(8,128)(2,1)}, u32[]{:S(2)}, u32[]{:S(2)}) collective-permute-start(bf16[144,3072]{1,0:T(8,128)(2,1)} %collective-permute-done.11.gu2), channel_id=1, source_target_pairs={{0,1},{1,0},{2,3},{3,2},{4,5},{5,4},{6,7},{7,6},{8,9},{9,8},{10,11... | collective-permute-start | bytes 2654216 | tf_op jit(solution)/shard_map/ppermute | solution.py:768
  57.2 9.2 %collective-permute-start.9 = (bf16[9,128,128]{2,1,0:T(8,128)(2,1)}, bf16[9,128,128]{2,1,0:T(8,128)(2,1)}, u32[]{:S(2)}, u32[]{:S(2)}) collective-permute-start(bf16[9,128,128]{2,1,0:T(8,128)(2,1)} %collective-permute-done.8), channel_id=1, source_target_pairs={{0,4},{4,0},{8,12},{12,8},{16,20},{20,16},{24,28},{28,24},{1,5},{5... | collective-permute-start | bytes 884744 | tf_op jit(solution)/shard_map/ppermute | solution.py:768
  87.7 6.1 %collective-permute-start.16 = (bf16[2,8,256,384]{3,2,1,0:T(8,128)(2,1)}, bf16[2,8,256,384]{3,2,1,0:T(8,128)(2,1)}, u32[]{:S(2)}, u32[]{:S(2)}) collective-permute-start(bf16[2,8,256,384]{3,2,1,0:T(8,128)(2,1)} %get-tuple-element.88), channel_id=1, source_target_pairs={{0,1},{1,0},{2,3},{3,2},{4,5},{5,4},{6,7},{7,6},{8,9},{9,8},{10,11... | collective-permute-start | bytes 9437192 | tf_op jit(solution)/shard_map/ppermute | solution.py:768
  97.3 36.8 %collective-permute-start.24 = (bf16[8,256,384]{2,1,0:T(8,128)(2,1)}, bf16[8,256,384]{2,1,0:T(8,128)(2,1)}, u32[]{:S(2)}, u32[]{:S(2)}) collective-permute-start(bf16[8,256,384]{2,1,0:T(8,128)(2,1)} %shard_map.220.refs_1_), channel_id=1, source_target_pairs={{0,2},{1,3},{2,0},{3,1},{4,6},{5,7},{6,4},{7,5},{8,10},{9,11},{10,... | collective-permute-start | bytes 4718600 | tf_op jit(solution)/shard_map/ppermute | solution.py:768
  98.9 10.2 %collective-permute-start.17 = (bf16[9,128,128]{2,1,0:T(8,128)(2,1)}, bf16[9,128,128]{2,1,0:T(8,128)(2,1)}, u32[]{:S(2)}, u32[]{:S(2)}) collective-permute-start(bf16[9,128,128]{2,1,0:T(8,128)(2,1)} %bitcast.56), channel_id=1, source_target_pairs={{0,4},{4,0},{8,12},{12,8},{16,20},{20,16},{24,28},{28,24},{1,5},{5... | collective-permute-start | bytes 884744 | tf_op jit(solution)/shard_map/ppermute | solution.py:768
  103.3 11.7 %collective-permute-start.18 = (bf16[9,128,128]{2,1,0:T(8,128)(2,1)}, bf16[9,128,128]{2,1,0:T(8,128)(2,1)}, u32[]{:S(2)}, u32[]{:S(2)}) collective-permute-start(bf16[9,128,128]{2,1,0:T(8,128)(2,1)} %bitcast.55), channel_id=1, source_target_pairs={{0,4},{4,0},{8,12},{12,8},{16,20},{20,16},{24,28},{28,24},{1,5},{5... | collective-permute-start | bytes 884744 | tf_op jit(solution)/shard_map/ppermute | solution.py:768
  113.2 12.3 %collective-permute-start.22 = (bf16[9,128,128]{2,1,0:T(8,128)(2,1)}, bf16[9,128,128]{2,1,0:T(8,128)(2,1)}, u32[]{:S(2)}, u32[]{:S(2)}) collective-permute-start(bf16[9,128,128]{2,1,0:T(8,128)(2,1)} %bitcast.54), channel_id=1, source_target_pairs={{0,4},{4,0},{8,12},{12,8},{16,20},{20,16},{24,28},{28,24},{1,5},{5... | collective-permute-start | bytes 884744 | tf_op jit(solution)/shard_map/ppermute | solution.py:768
  113.7 24.9 %collective-permute-start.20 = (bf16[9,128,128]{2,1,0:T(8,128)(2,1)}, bf16[9,128,128]{2,1,0:T(8,128)(2,1)}, u32[]{:S(2)}, u32[]{:S(2)}) collective-permute-start(bf16[9,128,128]{2,1,0:T(8,128)(2,1)} %get-tuple-element.99), channel_id=1, source_target_pairs={{24,0},{28,4},{25,1},{29,5},{26,2},{30,6},{27,3},{31,7}} | collective-permute-start | bytes 884744 | tf_op jit(solution)/shard_map/ppermute | solution.py:908
  122.8 15.9 %collective-permute-start.19 = (bf16[9,128,128]{2,1,0:T(8,128)(2,1)}, bf16[9,128,128]{2,1,0:T(8,128)(2,1)}, u32[]{:S(2)}, u32[]{:S(2)}) collective-permute-start(bf16[9,128,128]{2,1,0:T(8,128)(2,1)} %bitcast.53), channel_id=1, source_target_pairs={{0,4},{4,0},{8,12},{12,8},{16,20},{20,16},{24,28},{28,24},{1,5},{5... | collective-permute-start | bytes 884744 | tf_op jit(solution)/shard_map/ppermute | solution.py:768
  124.2 21.4 %collective-permute-start.21 = (bf16[9,128,128]{2,1,0:T(8,128)(2,1)}, bf16[9,128,128]{2,1,0:T(8,128)(2,1)}, u32[]{:S(2)}, u32[]{:S(2)}) collective-permute-start(bf16[9,128,128]{2,1,0:T(8,128)(2,1)} %get-tuple-element.100), channel_id=1, source_target_pairs={{16,0},{20,4},{24,8},{28,12},{17,1},{21,5},{25,9},{29,13},{18,2},{... | collective-permute-start | bytes 884744 | tf_op jit(solution)/shard_map/ppermute | solution.py:908
  127.4 19.1 %collective-permute-start.23 = (bf16[9,128,128]{2,1,0:T(8,128)(2,1)}, bf16[9,128,128]{2,1,0:T(8,128)(2,1)}, u32[]{:S(2)}, u32[]{:S(2)}) collective-permute-start(bf16[9,128,128]{2,1,0:T(8,128)(2,1)} %shard_map.224.refs_4_), channel_id=1, source_target_pairs={{8,0},{12,4},{16,8},{20,12},{24,16},{28,20},{9,1},{13,5},{17,9},{2... | collective-permute-start | bytes 884744 | tf_op jit(solution)/shard_map/ppermute | solution.py:908
  138.1 19.1 %collective-permute-start.26 = (bf16[4,256,384]{2,1,0:T(8,128)(2,1)}, bf16[4,256,384]{2,1,0:T(8,128)(2,1)}, u32[]{:S(2)}, u32[]{:S(2)}) collective-permute-start(bf16[4,256,384]{2,1,0:T(8,128)(2,1)} %get-tuple-element.107), channel_id=1, source_target_pairs={{0,4},{4,0},{8,12},{12,8},{16,20},{20,16},{24,28},{28,24},{1,5},{5... | collective-permute-start | bytes 2359304 | tf_op jit(solution)/shard_map/ppermute | solution.py:768
  153.8 5.7 %collective-permute-start.25 = (bf16[2,8,72,256]{3,2,1,0:T(8,128)(2,1)}, bf16[2,8,72,256]{3,2,1,0:T(8,128)(2,1)}, u32[]{:S(2)}, u32[]{:S(2)}) collective-permute-start(bf16[2,8,72,256]{3,2,1,0:T(8,128)(2,1)} %get-tuple-element.106), channel_id=1, source_target_pairs={{0,1},{1,0},{2,3},{3,2},{4,5},{5,4},{6,7},{7,6},{8,9},{9,8},{10,11... | collective-permute-start | bytes 1769480 | tf_op jit(solution)/shard_map/ppermute | solution.py:768
  162.0 29.8 %collective-permute-start.27 = (bf16[8,72,256]{2,1,0:T(8,128)(2,1)}, bf16[8,72,256]{2,1,0:T(8,128)(2,1)}, u32[]{:S(2)}, u32[]{:S(2)}) collective-permute-start(bf16[8,72,256]{2,1,0:T(8,128)(2,1)} %shard_map.228.refs_5_), channel_id=1, source_target_pairs={{0,2},{1,3},{2,0},{3,1},{4,6},{5,7},{6,4},{7,5},{8,10},{9,11},{10,... | collective-permute-start | bytes 884744 | tf_op jit(solution)/shard_map/ppermute | solution.py:768
  163.6 9.5 %collective-permute-start.28 = (bf16[256,384]{1,0:T(8,128)(2,1)}, bf16[256,384]{1,0:T(8,128)(2,1)}, u32[]{:S(2)}, u32[]{:S(2)}) collective-permute-start(bf16[256,384]{1,0:T(8,128)(2,1)} %get-tuple-element.109), channel_id=1, source_target_pairs={{0,8},{4,12},{8,0},{12,4},{16,24},{20,28},{24,16},{28,20},{1,9},{5... | collective-permute-start | bytes 589832 | tf_op jit(solution)/shard_map/ppermute | solution.py:768
  166.1 17.1 %collective-permute-start.29 = (bf16[256,384]{1,0:T(8,128)(2,1)}, bf16[256,384]{1,0:T(8,128)(2,1)}, u32[]{:S(2)}, u32[]{:S(2)}) collective-permute-start(bf16[256,384]{1,0:T(8,128)(2,1)} %get-tuple-element.110), channel_id=1, source_target_pairs={{0,16},{4,20},{8,24},{12,28},{16,0},{20,4},{24,8},{28,12},{1,17},{... | collective-permute-start | bytes 589832 | tf_op jit(solution)/shard_map/ppermute | solution.py:768
  167.7 15.4 %collective-permute-start.30 = (bf16[256,384]{1,0:T(8,128)(2,1)}, bf16[256,384]{1,0:T(8,128)(2,1)}, u32[]{:S(2)}, u32[]{:S(2)}) collective-permute-start(bf16[256,384]{1,0:T(8,128)(2,1)} %get-tuple-element.111), channel_id=1, source_target_pairs={{0,24},{4,28},{8,16},{12,20},{16,8},{20,12},{24,0},{28,4},{1,25},{... | collective-permute-start | bytes 589832 | tf_op jit(solution)/shard_map/ppermute | solution.py:768
  185.1 15.8 %collective-permute-start.37 = (bf16[256,384]{1,0:T(8,128)(2,1)}, bf16[256,384]{1,0:T(8,128)(2,1)}, u32[]{:S(2)}, u32[]{:S(2)}) collective-permute-start(bf16[256,384]{1,0:T(8,128)(2,1)} %shard_map.229.refs_4_.refs_1_), channel_id=1, source_target_pairs={{0,24},{4,28},{8,16},{12,20},{16,8},{20,12},{24,0},{28,4},{1,25},{... | collective-permute-start | bytes 589832 | tf_op jit(solution)/shard_map/ppermute | solution.py:768
  187.6 16.2 %collective-permute-start.36 = (bf16[256,384]{1,0:T(8,128)(2,1)}, bf16[256,384]{1,0:T(8,128)(2,1)}, u32[]{:S(2)}, u32[]{:S(2)}) collective-permute-start(bf16[256,384]{1,0:T(8,128)(2,1)} %shard_map.229.refs_4_.refs_1_), channel_id=1, source_target_pairs={{0,16},{4,20},{8,24},{12,28},{16,0},{20,4},{24,8},{28,12},{1,17},{... | collective-permute-start | bytes 589832 | tf_op jit(solution)/shard_map/ppermute | solution.py:768
  191.8 12.0 %collective-permute-start.35 = (bf16[256,384]{1,0:T(8,128)(2,1)}, bf16[256,384]{1,0:T(8,128)(2,1)}, u32[]{:S(2)}, u32[]{:S(2)}) collective-permute-start(bf16[256,384]{1,0:T(8,128)(2,1)} %shard_map.229.refs_4_.refs_1_), channel_id=1, source_target_pairs={{0,8},{4,12},{8,0},{12,4},{16,24},{20,28},{24,16},{28,20},{1,9},{5... | collective-permute-start | bytes 589832 | tf_op jit(solution)/shard_map/ppermute | solution.py:768
  193.8 5.5 %collective-permute-start.31 = (bf16[4,72,256]{2,1,0:T(8,128)(2,1)}, bf16[4,72,256]{2,1,0:T(8,128)(2,1)}, u32[]{:S(2)}, u32[]{:S(2)}) collective-permute-start(bf16[4,72,256]{2,1,0:T(8,128)(2,1)} %get-tuple-element.113), channel_id=1, source_target_pairs={{0,4},{4,0},{8,12},{12,8},{16,20},{20,16},{24,28},{28,24},{1,5},{5... | collective-permute-start | bytes 442376 | tf_op jit(solution)/shard_map/ppermute | solution.py:768
  206.0 20.7 %collective-permute-start.42 = (bf16[4,256,384]{2,1,0:T(8,128)(2,1)}, bf16[4,256,384]{2,1,0:T(8,128)(2,1)}, u32[]{:S(2)}, u32[]{:S(2)}) collective-permute-start(bf16[4,256,384]{2,1,0:T(8,128)(2,1)} %shard_map.232.refs_5_.refs_0_), channel_id=1, source_target_pairs={{0,4},{4,0},{8,12},{12,8},{16,20},{20,16},{24,28},{28,24},{1,5},{5... | collective-permute-start | bytes 2359304 | tf_op jit(solution)/shard_map/ppermute | solution.py:768
  206.4 4.4 %collective-permute-start.32 = (bf16[72,256]{1,0:T(8,128)(2,1)}, bf16[72,256]{1,0:T(8,128)(2,1)}, u32[]{:S(2)}, u32[]{:S(2)}) collective-permute-start(bf16[72,256]{1,0:T(8,128)(2,1)} %get-tuple-element.115), channel_id=1, source_target_pairs={{0,8},{4,12},{8,0},{12,4},{16,24},{20,28},{24,16},{28,20},{1,9},{5... | collective-permute-start | bytes 110600 | tf_op jit(solution)/shard_map/ppermute | solution.py:768
  206.4 5.2 %collective-permute-start.33 = (bf16[72,256]{1,0:T(8,128)(2,1)}, bf16[72,256]{1,0:T(8,128)(2,1)}, u32[]{:S(2)}, u32[]{:S(2)}) collective-permute-start(bf16[72,256]{1,0:T(8,128)(2,1)} %get-tuple-element.116), channel_id=1, source_target_pairs={{0,16},{4,20},{8,24},{12,28},{16,0},{20,4},{24,8},{28,12},{1,17},{... | collective-permute-start | bytes 110600 | tf_op jit(solution)/shard_map/ppermute | solution.py:768
  208.5 6.1 %collective-permute-start.34 = (bf16[72,256]{1,0:T(8,128)(2,1)}, bf16[72,256]{1,0:T(8,128)(2,1)}, u32[]{:S(2)}, u32[]{:S(2)}) collective-permute-start(bf16[72,256]{1,0:T(8,128)(2,1)} %get-tuple-element.117), channel_id=1, source_target_pairs={{0,24},{4,28},{8,16},{12,20},{16,8},{20,12},{24,0},{28,4},{1,25},{... | collective-permute-start | bytes 110600 | tf_op jit(solution)/shard_map/ppermute | solution.py:768
  216.1 6.1 %collective-permute-start.40 = (bf16[72,256]{1,0:T(8,128)(2,1)}, bf16[72,256]{1,0:T(8,128)(2,1)}, u32[]{:S(2)}, u32[]{:S(2)}) collective-permute-start(bf16[72,256]{1,0:T(8,128)(2,1)} %shard_map.233.refs_1_.refs_5_), channel_id=1, source_target_pairs={{0,24},{4,28},{8,16},{12,20},{16,8},{20,12},{24,0},{28,4},{1,25},{... | collective-permute-start | bytes 110600 | tf_op jit(solution)/shard_map/ppermute | solution.py:768
  218.5 5.2 %collective-permute-start.39 = (bf16[72,256]{1,0:T(8,128)(2,1)}, bf16[72,256]{1,0:T(8,128)(2,1)}, u32[]{:S(2)}, u32[]{:S(2)}) collective-permute-start(bf16[72,256]{1,0:T(8,128)(2,1)} %shard_map.233.refs_1_.refs_5_), channel_id=1, source_target_pairs={{0,16},{4,20},{8,24},{12,28},{16,0},{20,4},{24,8},{28,12},{1,17},{... | collective-permute-start | bytes 110600 | tf_op jit(solution)/shard_map/ppermute | solution.py:768
  218.5 5.2 %collective-permute-start.38 = (bf16[72,256]{1,0:T(8,128)(2,1)}, bf16[72,256]{1,0:T(8,128)(2,1)}, u32[]{:S(2)}, u32[]{:S(2)}) collective-permute-start(bf16[72,256]{1,0:T(8,128)(2,1)} %shard_map.233.refs_1_.refs_5_), channel_id=1, source_target_pairs={{0,8},{4,12},{8,0},{12,4},{16,24},{20,28},{24,16},{28,20},{1,9},{5... | collective-permute-start | bytes 110600 | tf_op jit(solution)/shard_map/ppermute | solution.py:768
  225.1 5.5 %collective-permute-start.41 = (bf16[4,72,256]{2,1,0:T(8,128)(2,1)}, bf16[4,72,256]{2,1,0:T(8,128)(2,1)}, u32[]{:S(2)}, u32[]{:S(2)}) collective-permute-start(bf16[4,72,256]{2,1,0:T(8,128)(2,1)} %shard_map.234.refs_0_), channel_id=1, source_target_pairs={{0,4},{4,0},{8,12},{12,8},{16,20},{20,16},{24,28},{28,24},{1,5},{5... | collective-permute-start | bytes 442376 | tf_op jit(solution)/shard_map/ppermute | solution.py:768

commit v3 on v2

--- a/solution.py
+++ b/solution.py
@@ -427,8 +427,8 @@
     width = ff // 2
 
     def ff_step(i, carry):
-        at = pl.multiple_of(i * width, width)
-        cols, cols_up = pl.ds(at, width), pl.ds(pl.multiple_of(at + ff, width), width)
+        at = i * width
+        cols, cols_up = pl.ds(at, width), pl.ds(at + ff, width)
         n2 = n2_ref[...]
         w_g, w_u, w_d = w_gu[:, cols], w_gu[:, cols_up], w_down[cols, :]
         gate = dot(n2, w_g)
@@ -446,7 +446,8 @@
         dn2_ref[...] += dot(d_gate, w_g, NT) + dot(d_up, w_u, NT)
         return carry
 
-    lax.fori_loop(0, 2, ff_step, 0)
+    ff_step(0, 0)
+    ff_step(1, 0)
     part = dim // CHUNKS
     quarter = 2 * ff // CHUNKS
     stores = []
@@ -625,21 +626,17 @@
     dim = x.shape[1]
     fs = dim // 4
     for slot in range(4):
-        start = (index ^ SLOTS[slot]) * fs
+        at = pl.ds(pl.multiple_of((index ^ SLOTS[slot]) * fs, 16), fs)
         to = keep if slot < 2 else send
         for c in range(CHUNKS):
-            half, quarter = divmod(c, 4)
-            size, cols = fs // 2, width // 4
-            at = pl.ds(pl.multiple_of(start + half * size, 8), size)
-            tile = g_ref[at, quarter * cols : (quarter + 1) * cols]
-            if c == 3:
+            tile = g_ref[at, c * LANES : (c + 1) * LANES]
+            if c == CHUNKS - 1:
                 pad = jnp.concatenate(
                     [gain_grad[:, k * HEAD_DIM : (k + 1) * HEAD_DIM] for k in range(HEADS)]
-                    + [jnp.zeros((size - HEADS, HEAD_DIM), F32)],
+                    + [jnp.zeros((fs - HEADS, HEAD_DIM), F32)],
                     axis=0,
                 )
-                pad = jnp.concatenate([tile[:, : cols - HEAD_DIM], pad], axis=1)
-                tile = pad
+                tile = jnp.concatenate([tile[:, :HEAD_DIM], pad], axis=1)
             to[slot % 2, c] = tile.astype(BF16)
 
 
@@ -647,7 +644,7 @@
     n, dim = x.shape
     width = w.shape[1]
     vm = pl.BlockSpec(memory_space=pltpu.VMEM)
-    pair = sds((2, CHUNKS, dim // 8, width // 4), BF16)
+    pair = sds((2, CHUNKS, dim // 4, width // CHUNKS), BF16)
     tiles = dkv[0].shape[0]
     return call(
         functools.partial(end_kernel, parts=len(dkv)),
@@ -708,12 +705,10 @@
 def own_q_kernel(place_ref, *refs):
     parts = refs[:2]
     query_ref, key_ref, value_ref, gain_ref, all_ref = refs[-5:]
-    part, cols = parts[0].shape[1:]
     for d in range(4):
         quarter, first, second = both_halves(place_ref, parts, d)
-        at = pl.ds(pl.multiple_of(quarter * cols, LANES), cols)
-        all_ref[:part, at] = first
-        all_ref[part:, at] = second
+        all_ref[:, pl.ds(pl.multiple_of(quarter * LANES, LANES), LANES)] = first
+        all_ref[:, pl.ds(pl.multiple_of((4 + quarter) * LANES, LANES), LANES)] = second
     first = KV_HEADS * LANES
     for g in range(KV_HEADS):
         to = slice(g * HEAD_DIM, (g + 1) * HEAD_DIM)

time: 233 us -> 234 us (level)
  waiting for transfers between devices: 61.1 us -> 63.5 us
    ppermute x37, waiting for transfers between devices: 49.8 us -> 53.3 us  [flip(): return lax.ppermute(x, axis, [(i, i ^ mask) for i in range(n)])]
  transfers between devices with their start and end apart: 43 -> 43, of which waited for: 19 -> 20; matrix products, arithmetic and copies ran while one was open for 3% -> 3% of each run, Pallas kernels for 29% -> 29%
where the time goes in v3:
time: 234 us
  Pallas kernels  101 us (43%)
  waiting for transfers between devices  63.5 us (27%)
  starting transfers between devices  60.5 us (26%)
  other arithmetic  7.9 us (3%)
    ppermute x37, waiting for transfers between devices, flip(): return lax.ppermute(x, axis, [(i, i ^ mask) for i in range(n)])  53.3 us
    ppermute x37, starting transfers between devices, flip(): return lax.ppermute(x, axis, [(i, i ^ mask) for i in range(n)])  42.3 us
    pallas_call x1, Pallas kernels, middle(): call(functools.partial(middle_kernel, fused), (sds((tiles // KV_HEADS, di...  20.7 us
    pallas_call x4, Pallas kernels, attend_back(): call(functools.partial(attend_back_kernel, steps, diagonal, carry is None...  19.1 us
    pallas_call x9, Pallas kernels, fuse(): call(body, tuple((sds(shape, BF16) for shape in outs)), [pl.BlockSpec(mem...  19 us
    pallas_call x3, Pallas kernels, attend(): call(functools.partial(attend_kernel, steps, diagonal, carry is None), (s...  14.5 us
    ppermute x3, starting transfers between devices, local(): piece = lax.ppermute(piece, 'ctx', up)  14.2 us
    pallas_call x1, Pallas kernels, finish(): call(functools.partial(end_kernel, parts=len(dkv)), (sds((tiles // KV_HEA...  7.25 us
  transfers between devices with their start and end apart: 43, of which 20 were waited for; matrix products, arithmetic and copies ran while one was open for 3% of the time, Pallas kernels for 29%

profile of v3, /device:TPU:0, one launch (start us, length us, event | category | flops | bytes accessed | tf_op | source)
XLA Modules:
  0.0 233.7 jit_solution(7481798543025655757)
XLA Ops:
  0.6 1.9 shard_map.212.w0
  2.6 3.0 %collective-permute-start.1 = (bf16[144,1024]{1,0:T(8,128)(2,1)}, bf16[144,1024]{1,0:T(8,128)(2,1)}, u32[]{:S(2)}, u32[]{:S(2)}) collective-permute-start(bf16[144,1024]{1,0:T(8,128)(2,1)} %shard_map.212.w0), channel_id=1, source_target_pairs={{0,2},{1,3},{2,0},{3,1},{4,6},{5,7},{6,4},{7,5},{8,10},{9,11},{10,... | collective-permute-start | bytes 884744 | tf_op jit(solution)/shard_map/ppermute | solution.py:763
  5.5 2.7 %shard_map.217 = (bf16[144,3072]{1,0:T(8,128)(2,1)}, bf16[528,576]{1,0:T(8,128)(2,1)}) custom-call(bf16[144,1536]{1,0:T(8,128)(2,1)} %gate_ref.1, bf16[144,1536]{1,0:T(8,128)(2,1)} %up_ref.1, bf16[576,384]{1,0:T(8,128)(2,1)} %bitcast.50, bf16[144,576]{1,0:T(8,128)(2,1)} %w_ref.1), custom_call_target="tpu_custom_call" | custom-call | flops 3000000000 | tf_op jit(solution)/shard_map/pallas_call | solution.py:962
  8.7 1.7 collective-permute-start.11
  11.2 2.5 %collective-permute-done.1.w2 = bf16[144,1024]{1,0:T(8,128)(2,1)} collective-permute-done((bf16[144,1024]{1,0:T(8,128)(2,1)}, bf16[144,1024]{1,0:T(8,128)(2,1)}, u32[]{:S(2)}, u32[]{:S(2)}) %collective-permute-start.1) | collective-permute-done | bytes 294944 | tf_op jit(solution)/shard_map/ppermute | solution.py:763
  17.5 4.2 %shard_map.213 = (bf16[576,1024]{1,0:T(8,128)(2,1)}, bf16[384,576]{1,0:T(8,128)(2,1)}, bf16[9,384,128]{2,1,0:T(8,128)(2,1)}, bf16[9,128,128]{2,1,0:T(8,128)(2,1)...) custom-call(s32[1]{0:T(128)} %bitcast.index_ref, bf16[3,576,128]{2,1,0:T(8,128)(2,1)} %bitcast.51, ...), custom_call_target="tpu_custom_call" | custom-call | flops 4000000000 | tf_op jit(solution)/shard_map/pallas_call | solution.py:947
  21.7 2.0 collective-permute-start.7
  23.7 4.2 %collective-permute-start.3 = (bf16[9,128,128]{2,1,0:T(8,128)(2,1)}, bf16[9,128,128]{2,1,0:T(8,128)(2,1)}, u32[]{:S(2)}, u32[]{:S(2)}) collective-permute-start(bf16[9,128,128]{2,1,0:T(8,128)(2,1)} %get-tuple-element.72), channel_id=1, source_target_pairs={{0,8},{4,12},{8,16},{12,20},{16,24},{20,28},{1,9},{5,13},{9,17},{1... | collective-permute-start | bytes 884744 | tf_op jit(solution)/shard_map/ppermute | solution.py:991
  30.6 3.5 %collective-permute-done.3 = bf16[9,128,128]{2,1,0:T(8,128)(2,1)} collective-permute-done((bf16[9,128,128]{2,1,0:T(8,128)(2,1)}, bf16[9,128,128]{2,1,0:T(8,128)(2,1)}, u32[]{:S(2)}, u32[]{:S(2)}) %collective-permute-start.3) | collective-permute-done | bytes 294944 | tf_op jit(solution)/shard_map/ppermute | solution.py:991
  34.7 5.1 %collective-permute-start.4 = (bf16[9,128,128]{2,1,0:T(8,128)(2,1)}, bf16[9,128,128]{2,1,0:T(8,128)(2,1)}, u32[]{:S(2)}, u32[]{:S(2)}) collective-permute-start(bf16[9,128,128]{2,1,0:T(8,128)(2,1)} %collective-permute-done.3), channel_id=1, source_target_pairs={{0,8},{4,12},{8,16},{12,20},{16,24},{20,28},{1,9},{5,13},{9,17},{1... | collective-permute-start | bytes 884744 | tf_op jit(solution)/shard_map/ppermute | solution.py:991
  39.8 5.4 %shard_map.214 = (f32[9,384,128]{2,1,0:T(8,128)}, f32[9,384,128]{2,1,0:T(8,128)}) custom-call(s32[9]{0:T(128)} %get-tuple-element.130.info_ref, bf16[9,384,128]{2,1,0:T(8,128)(2,1)} %get-tuple-element.71.q_ref, bf16[1,9,128,128]{3,2,1,0:T(8,128)(2,1)} %bitcast.42, bf16[1,9,128,128]{3,2,1,0:T(8,128)(2,1)} %bitcast.18.b_ref), custom_call_target="tpu_custom_call" | custom-call | flops 10000000000 | tf_op jit(solution)/shard_map/pallas_call | solution.py:224
  45.2 4.9 %collective-permute-start.8 = (bf16[9,128,128]{2,1,0:T(8,128)(2,1)}, bf16[9,128,128]{2,1,0:T(8,128)(2,1)}, u32[]{:S(2)}, u32[]{:S(2)}) collective-permute-start(bf16[9,128,128]{2,1,0:T(8,128)(2,1)} %collective-permute-done.4), channel_id=1, source_target_pairs={{0,8},{4,12},{8,16},{12,20},{16,24},{20,28},{1,9},{5,13},{9,17},{1... | collective-permute-start | bytes 884744 | tf_op jit(solution)/shard_map/ppermute | solution.py:991
  51.5 4.6 %shard_map.215 = (f32[9,384,128]{2,1,0:T(8,128)}, f32[9,384,128]{2,1,0:T(8,128)}) custom-call(s32[9]{0:T(128)} %get-tuple-element.132.info_ref, bf16[9,384,128]{2,1,0:T(8,128)(2,1)} %get-tuple-element.71.q_ref, bf16[1,9,128,128]{3,2,1,0:T(8,128)(2,1)} %bitcast.13.a_ref, bf16[1,9,128,128]{3,2,1,0:T(8,128)(2,1)} %bitcast.14.b_ref, ...), custom_call_target="tpu_custom_call" | custom-call | flops 10000000000 | tf_op jit(solution)/shard_map/pallas_call | solution.py:224
  58.7 4.6 %shard_map.216 = (f32[9,384,128]{2,1,0:T(8,128)}, f32[9,384,128]{2,1,0:T(8,128)}) custom-call(s32[9]{0:T(128)} %get-tuple-element.131.info_ref, bf16[9,384,128]{2,1,0:T(8,128)(2,1)} %get-tuple-element.71.q_ref, bf16[1,9,128,128]{3,2,1,0:T(8,128)(2,1)} %bitcast.9.a_ref, bf16[1,9,128,128]{3,2,1,0:T(8,128)(2,1)} %bitcast.10.b_ref, ...), custom_call_target="tpu_custom_call" | custom-call | flops 10000000000 | tf_op jit(solution)/shard_map/pallas_call | solution.py:224
  63.3 3.1 %collective-permute-done.9 = bf16[9,128,128]{2,1,0:T(8,128)(2,1)} collective-permute-done((bf16[9,128,128]{2,1,0:T(8,128)(2,1)}, bf16[9,128,128]{2,1,0:T(8,128)(2,1)}, u32[]{:S(2)}, u32[]{:S(2)}) %collective-permute-start.9) | collective-permute-done | bytes 294944 | tf_op jit(solution)/shard_map/ppermute | solution.py:763
  66.3 20.7 %shard_map.218 = (f32[3,576,128]{2,1,0:T(8,128)}, f32[384,576]{1,0:T(8,128)}, bf16[9,384,128]{2,1,0:T(8,128)(2,1)}, f32[9,8,384]{2,1,0:T(8,128)}, bf16[2,8,256,3...) custom-call(s32[1]{0:T(128)} %bitcast.index_ref, s32[9]{0:T(128)} %get-tuple-element.133.info_ref, ...), custom_call_target="tpu_custom_call" | custom-call | flops 20000000000 | tf_op jit(solution)/shard_map/pallas_call | solution.py:532
  87.8 3.3 %shard_map.219 = (f32[9,384,128]{2,1,0:T(8,128)}, bf16[1,9,128,128]{3,2,1,0:T(8,128)(2,1)}, bf16[1,9,128,128]{3,2,1,0:T(8,128)(2,1)}) custom-call(s32[9]{0:T(128)} %get-tuple-element.133.info_ref, bf16[9,384,128]{2,1,0:T(8,128)(2,1)} %get-tuple-element.71.q_ref, bf16[9,384,128]{2,1,0:T(8,128)(2,1)} %get-tuple-element.84.d_ref, ...), custom_call_target="tpu_custom_call" | custom-call | flops 50000000 | tf_op jit(solution)/shard_map/pallas_call | solution.py:305
  91.1 2.0 collective-permute-done.16.got.refs_2_
  93.2 3.5 %shard_map.220.refs_1_ = bf16[8,256,384]{2,1,0:T(8,128)(2,1)} custom-call(s32[3]{0:T(128)} %pad_add_fusion.place_ref.refs_0_, bf16[2,8,256,384]{3,2,1,0:T(8,128)(2,1)} %get-tuple-element.87.keep.refs_1_, bf16[2,8,256,384]{3,2,1,0:T(8,128)(2,1)} %collective-permute-done.16.got.refs_2_, f32[9,384,128]{2,1,0:T(8,128)} %get-tuple-element.86.refs_0_), custom_call_target="tpu_custom_call" | custom-call | flops 50000000 | tf_op jit(solution)/shard_map/pallas_call | solution.py:809
  98.8 3.9 %shard_map.221 = (f32[9,384,128]{2,1,0:T(8,128)}, bf16[1,9,128,128]{3,2,1,0:T(8,128)(2,1)}, bf16[1,9,128,128]{3,2,1,0:T(8,128)(2,1)}) custom-call(s32[9]{0:T(128)} %get-tuple-element.131.info_ref, bf16[9,384,128]{2,1,0:T(8,128)(2,1)} %get-tuple-element.71.q_ref, bf16[9,384,128]{2,1,0:T(8,128)(2,1)} %get-tuple-element.84.d_ref, ...), custom_call_target="tpu_custom_call" | custom-call | flops 50000000 | tf_op jit(solution)/shard_map/pallas_call | solution.py:305
  104.2 4.3 %collective-permute-done.17.refs_2_ = bf16[9,128,128]{2,1,0:T(8,128)(2,1)} collective-permute-done((bf16[9,128,128]{2,1,0:T(8,128)(2,1)}, bf16[9,128,128]{2,1,0:T(8,128)(2,1)}, u32[]{:S(2)}, u32[]{:S(2)}) %collective-permute-start.17) | collective-permute-done | bytes 294944 | tf_op jit(solution)/shard_map/ppermute | solution.py:763
  108.5 4.1 %shard_map.222 = (f32[9,384,128]{2,1,0:T(8,128)}, bf16[1,9,128,128]{3,2,1,0:T(8,128)(2,1)}, bf16[1,9,128,128]{3,2,1,0:T(8,128)(2,1)}, bf16[9,128,128]{2,1,0:T(8,128)(2,1)}) custom-call(s32[9]{0:T(128)} %get-tuple-element.132.info_ref, bf16[9,384,128]{2,1,0:T(8,128)(2,1)} %get-tuple-element.71.q_ref, bf16[9,384,128]{2,1,0:T(8,128)(2,1)} %get-tuple-element.84.d_ref, ...), custom_call_target="tpu_custom_call" | custom-call | flops 50000000 | tf_op jit(solution)/shard_map/pallas_call | solution.py:305
  114.5 7.7 %shard_map.223 = (f32[9,384,128]{2,1,0:T(8,128)}, bf16[1,9,128,128]{3,2,1,0:T(8,128)(2,1)}, bf16[1,9,128,128]{3,2,1,0:T(8,128)(2,1)}, bf16[9,128,128]{2,1,0:T(8,128)(2,1)}) custom-call(s32[9]{0:T(128)} %get-tuple-element.130.info_ref, bf16[9,384,128]{2,1,0:T(8,128)(2,1)} %get-tuple-element.71.q_ref, bf16[9,384,128]{2,1,0:T(8,128)(2,1)} %get-tuple-element.84.d_ref, ...), custom_call_target="tpu_custom_call" | custom-call | flops 50000000 | tf_op jit(solution)/shard_map/pallas_call | solution.py:305
  125.0 1.8 shard_map.224.refs_4_
  128.4 5.1 %collective-permute-done.24.refs_3_ = bf16[8,256,384]{2,1,0:T(8,128)(2,1)} collective-permute-done((bf16[8,256,384]{2,1,0:T(8,128)(2,1)}, bf16[8,256,384]{2,1,0:T(8,128)(2,1)}, u32[]{:S(2)}, u32[]{:S(2)}) %collective-permute-start.24) | collective-permute-done | bytes 1572896 | tf_op jit(solution)/shard_map/ppermute | solution.py:763
  133.5 4.0 %shard_map.225 = (bf16[4,256,384]{2,1,0:T(8,128)(2,1)}, bf16[4,256,384]{2,1,0:T(8,128)(2,1)}) custom-call(s32[3]{0:T(128)} %pad_add_fusion.place_ref.refs_0_, bf16[2,8,256,384]{3,2,1,0:T(8,128)(2,1)} %get-tuple-element.87.keep.refs_1_, bf16[2,8,256,384]{3,2,1,0:T(8,128)(2,1)} %collective-permute-done.16.got.refs_2_, ...), custom_call_target="tpu_custom_call" | custom-call | flops 50000000 | tf_op jit(solution)/shard_map/pallas_call | solution.py:845
  138.0 6.4 %collective-permute-done.21.refs_3_ = bf16[9,128,128]{2,1,0:T(8,128)(2,1)} collective-permute-done((bf16[9,128,128]{2,1,0:T(8,128)(2,1)}, bf16[9,128,128]{2,1,0:T(8,128)(2,1)}, u32[]{:S(2)}, u32[]{:S(2)}) %collective-permute-start.21) | collective-permute-done | bytes 294944 | tf_op jit(solution)/shard_map/ppermute | solution.py:903
  144.8 7.3 %shard_map.226 = (f32[3,576,128]{2,1,0:T(8,128)}, bf16[2,8,144,128]{3,2,1,0:T(8,128)(2,1)}, bf16[2,8,144,128]{3,2,1,0:T(8,128)(2,1)}) custom-call(s32[1]{0:T(128)} %bitcast.index_ref, bf16[384,576]{1,0:T(8,128)(2,1)} %get-tuple-element.69.x_ref, bf16[384,576]{1,0:T(8,128)(2,1)} %get-tuple-element.82.normed_ref, bf16[576,1024]{1,0:T(8,128)(2,1)} %get-tuple-element.83.w_ref, ...), custom_call_target="tpu_custom_call" | custom-call | flops 50000000 | tf_op jit(solution)/shard_map/pallas_call | solution.py:649
  152.1 4.5 %collective-permute-done.26.refs_2_ = bf16[4,256,384]{2,1,0:T(8,128)(2,1)} collective-permute-done((bf16[4,256,384]{2,1,0:T(8,128)(2,1)}, bf16[4,256,384]{2,1,0:T(8,128)(2,1)}, u32[]{:S(2)}, u32[]{:S(2)}) %collective-permute-start.26) | collective-permute-done | bytes 786464 | tf_op jit(solution)/shard_map/ppermute | solution.py:763
  156.6 2.3 shard_map.227
  158.9 2.5 %shard_map.228.refs_5_ = bf16[8,144,128]{2,1,0:T(8,128)(2,1)} custom-call(s32[3]{0:T(128)} %pad_add_fusion.place_ref.refs_0_, bf16[2,8,144,128]{3,2,1,0:T(8,128)(2,1)} %get-tuple-element.105.refs_3_.keep.refs_1_, bf16[2,8,144,128]{3,2,1,0:T(8,128)(2,1)} %collective-permute-done.25.got.refs_2_, bf16[256,384]{1,0:T(8,128)(2,1)} %get-tuple-element.108.refs_0_.refs_1_), custom_call_target="tpu_custom_call" | custom-call | flops 50000000 | tf_op jit(solution)/shard_map/pallas_call | solution.py:809
  163.0 2.9 %collective-permute-start.28 = (bf16[256,384]{1,0:T(8,128)(2,1)}, bf16[256,384]{1,0:T(8,128)(2,1)}, u32[]{:S(2)}, u32[]{:S(2)}) collective-permute-start(bf16[256,384]{1,0:T(8,128)(2,1)} %get-tuple-element.109), channel_id=1, source_target_pairs={{0,8},{4,12},{8,0},{12,4},{16,24},{20,28},{24,16},{28,20},{1,9},{5... | collective-permute-start | bytes 589832 | tf_op jit(solution)/shard_map/ppermute | solution.py:763
  168.4 3.7 %collective-permute-done.28.refs_2_ = bf16[256,384]{1,0:T(8,128)(2,1)} collective-permute-done((bf16[256,384]{1,0:T(8,128)(2,1)}, bf16[256,384]{1,0:T(8,128)(2,1)}, u32[]{:S(2)}, u32[]{:S(2)}) %collective-permute-start.28) | collective-permute-done | bytes 196640 | tf_op jit(solution)/shard_map/ppermute | solution.py:763
  172.1 10.2 %collective-permute-done.29.refs_3_ = bf16[256,384]{1,0:T(8,128)(2,1)} collective-permute-done((bf16[256,384]{1,0:T(8,128)(2,1)}, bf16[256,384]{1,0:T(8,128)(2,1)}, u32[]{:S(2)}, u32[]{:S(2)}) %collective-permute-start.29) | collective-permute-done | bytes 196640 | tf_op jit(solution)/shard_map/ppermute | solution.py:763
  182.4 2.0 shard_map.229.refs_4_.refs_1_
  184.4 2.0 collective-permute-start.37
  186.3 4.3 %collective-permute-start.36 = (bf16[256,384]{1,0:T(8,128)(2,1)}, bf16[256,384]{1,0:T(8,128)(2,1)}, u32[]{:S(2)}, u32[]{:S(2)}) collective-permute-start(bf16[256,384]{1,0:T(8,128)(2,1)} %shard_map.229.refs_4_.refs_1_), channel_id=1, source_target_pairs={{0,16},{4,20},{8,24},{12,28},{16,0},{20,4},{24,8},{28,12},{1,17},{... | collective-permute-start | bytes 589832 | tf_op jit(solution)/shard_map/ppermute | solution.py:763
  190.7 2.0 shard_map.230
  193.2 4.9 %collective-permute-done.31.refs_2_ = bf16[4,144,128]{2,1,0:T(8,128)(2,1)} collective-permute-done((bf16[4,144,128]{2,1,0:T(8,128)(2,1)}, bf16[4,144,128]{2,1,0:T(8,128)(2,1)}, u32[]{:S(2)}, u32[]{:S(2)}) %collective-permute-start.31) | collective-permute-done | bytes 147488 | tf_op jit(solution)/shard_map/ppermute | solution.py:763
  198.1 1.7 shard_map.231
  199.8 4.7 %collective-permute-done.36.refs_3_ = bf16[256,384]{1,0:T(8,128)(2,1)} collective-permute-done((bf16[256,384]{1,0:T(8,128)(2,1)}, bf16[256,384]{1,0:T(8,128)(2,1)}, u32[]{:S(2)}, u32[]{:S(2)}) %collective-permute-start.36) | collective-permute-done | bytes 196640 | tf_op jit(solution)/shard_map/ppermute | solution.py:763
  204.5 2.2 shard_map.232.refs_5_.refs_0_
  207.3 2.8 %collective-permute-start.33 = (bf16[144,128]{1,0:T(8,128)(2,1)}, bf16[144,128]{1,0:T(8,128)(2,1)}, u32[]{:S(2)}, u32[]{:S(2)}) collective-permute-start(bf16[144,128]{1,0:T(8,128)(2,1)} %get-tuple-element.116), channel_id=1, source_target_pairs={{0,16},{4,20},{8,24},{12,28},{16,0},{20,4},{24,8},{28,12},{1,17},{... | collective-permute-start | bytes 110600 | tf_op jit(solution)/shard_map/ppermute | solution.py:763
  213.0 3.2 %collective-permute-done.34.refs_4_ = bf16[144,128]{1,0:T(8,128)(2,1)} collective-permute-done((bf16[144,128]{1,0:T(8,128)(2,1)}, bf16[144,128]{1,0:T(8,128)(2,1)}, u32[]{:S(2)}, u32[]{:S(2)}) %collective-permute-start.34) | collective-permute-done | bytes 36896 | tf_op jit(solution)/shard_map/ppermute | solution.py:763
  219.2 2.8 %collective-permute-start.38 = (bf16[144,128]{1,0:T(8,128)(2,1)}, bf16[144,128]{1,0:T(8,128)(2,1)}, u32[]{:S(2)}, u32[]{:S(2)}) collective-permute-start(bf16[144,128]{1,0:T(8,128)(2,1)} %shard_map.233.refs_1_.refs_5_), channel_id=1, source_target_pairs={{0,8},{4,12},{8,0},{12,4},{16,24},{20,28},{24,16},{28,20},{1,9},{5... | collective-permute-start | bytes 110600 | tf_op jit(solution)/shard_map/ppermute | solution.py:763
  222.0 1.7 collective-permute-done.40.refs_4_
  227.7 3.5 %shard_map.235 = (f32[144,1536]{1,0:T(8,128)}, f32[144,1536]{1,0:T(8,128)}, f32[576,384]{1,0:T(8,128)}, f32[144,576]{1,0:T(8,128)}, f32[1,144]{1,0:T(1,128)}) custom-call(s32[3]{0:T(128)} %pad_add_fusion.place_ref.refs_0_, bf16[4,256,384]{2,1,0:T(8,128)(2,1)} %shard_map.232.refs_5_.refs_0_, bf16[4,256,384]{2,1,0:T(8,128)(2,1)} %collective-permute-done.42.refs_1_), custom_call_target="tpu_custom_call" | custom-call | flops 50000000 | tf_op jit(solution)/shard_map/pallas_call | solution.py:725
  231.6 2.0 shard_map.236
  (75 shorter events, 39.4 us)
Async XLA Ops:
  2.6 11.1 %collective-permute-start.1 = (bf16[144,1024]{1,0:T(8,128)(2,1)}, bf16[144,1024]{1,0:T(8,128)(2,1)}, u32[]{:S(2)}, u32[]{:S(2)}) collective-permute-start(bf16[144,1024]{1,0:T(8,128)(2,1)} %shard_map.212.w0), channel_id=1, source_target_pairs={{0,2},{1,3},{2,0},{3,1},{4,6},{5,7},{6,4},{7,5},{8,10},{9,11},{10,... | collective-permute-start | bytes 884744 | tf_op jit(solution)/shard_map/ppermute | solution.py:763
  5.5 11.9 %collective-permute-start = (bf16[144,1024]{1,0:T(8,128)(2,1)}, bf16[144,1024]{1,0:T(8,128)(2,1)}, u32[]{:S(2)}, u32[]{:S(2)}) collective-permute-start(bf16[144,1024]{1,0:T(8,128)(2,1)} %shard_map.212.w0), channel_id=1, source_target_pairs={{0,1},{1,0},{2,3},{3,2},{4,5},{5,4},{6,7},{7,6},{8,9},{9,8},{10,11... | collective-permute-start | bytes 884744 | tf_op jit(solution)/shard_map/ppermute | solution.py:763
  8.2 47.9 %collective-permute-start.14 = (bf16[528,576]{1,0:T(8,128)(2,1)}, bf16[528,576]{1,0:T(8,128)(2,1)}, u32[]{:S(2)}, u32[]{:S(2)}) collective-permute-start(bf16[528,576]{1,0:T(8,128)(2,1)} %get-tuple-element.80.do0), channel_id=1, source_target_pairs={{0,2},{1,3},{2,0},{3,1},{4,6},{5,7},{6,4},{7,5},{8,10},{9,11},{10,... | collective-permute-start | bytes 1824776 | tf_op jit(solution)/shard_map/ppermute | solution.py:763
  8.2 55.0 %collective-permute-start.13 = (bf16[528,576]{1,0:T(8,128)(2,1)}, bf16[528,576]{1,0:T(8,128)(2,1)}, u32[]{:S(2)}, u32[]{:S(2)}) collective-permute-start(bf16[528,576]{1,0:T(8,128)(2,1)} %get-tuple-element.80.do0), channel_id=1, source_target_pairs={{0,1},{1,0},{2,3},{3,2},{4,5},{5,4},{6,7},{7,6},{8,9},{9,8},{10,11... | collective-permute-start | bytes 1824776 | tf_op jit(solution)/shard_map/ppermute | solution.py:763
  8.7 47.4 %collective-permute-start.11 = (bf16[144,3072]{1,0:T(8,128)(2,1)}, bf16[144,3072]{1,0:T(8,128)(2,1)}, u32[]{:S(2)}, u32[]{:S(2)}) collective-permute-start(bf16[144,3072]{1,0:T(8,128)(2,1)} %get-tuple-element.79.gu0), channel_id=1, source_target_pairs={{0,2},{1,3},{2,0},{3,1},{4,6},{5,7},{6,4},{7,5},{8,10},{9,11},{10,... | collective-permute-start | bytes 2654216 | tf_op jit(solution)/shard_map/ppermute | solution.py:763
  13.7 3.8 %collective-permute-start.2 = (bf16[144,1024]{1,0:T(8,128)(2,1)}, bf16[144,1024]{1,0:T(8,128)(2,1)}, u32[]{:S(2)}, u32[]{:S(2)}) collective-permute-start(bf16[144,1024]{1,0:T(8,128)(2,1)} %collective-permute-done.1.w2), channel_id=1, source_target_pairs={{0,1},{1,0},{2,3},{3,2},{4,5},{5,4},{6,7},{7,6},{8,9},{9,8},{10,11... | collective-permute-start | bytes 884744 | tf_op jit(solution)/shard_map/ppermute | solution.py:763
  21.7 13.0 %collective-permute-start.7 = (bf16[9,128,128]{2,1,0:T(8,128)(2,1)}, bf16[9,128,128]{2,1,0:T(8,128)(2,1)}, u32[]{:S(2)}, u32[]{:S(2)}) collective-permute-start(bf16[9,128,128]{2,1,0:T(8,128)(2,1)} %get-tuple-element.72), channel_id=1, source_target_pairs={{0,4},{4,0},{8,12},{12,8},{16,20},{20,16},{24,28},{28,24},{1,5},{5... | collective-permute-start | bytes 884744 | tf_op jit(solution)/shard_map/ppermute | solution.py:763
  23.7 10.4 %collective-permute-start.3 = (bf16[9,128,128]{2,1,0:T(8,128)(2,1)}, bf16[9,128,128]{2,1,0:T(8,128)(2,1)}, u32[]{:S(2)}, u32[]{:S(2)}) collective-permute-start(bf16[9,128,128]{2,1,0:T(8,128)(2,1)} %get-tuple-element.72), channel_id=1, source_target_pairs={{0,8},{4,12},{8,16},{12,20},{16,24},{20,28},{1,9},{5,13},{9,17},{1... | collective-permute-start | bytes 884744 | tf_op jit(solution)/shard_map/ppermute | solution.py:991
  34.1 15.9 %collective-permute-start.6 = (bf16[9,128,128]{2,1,0:T(8,128)(2,1)}, bf16[9,128,128]{2,1,0:T(8,128)(2,1)}, u32[]{:S(2)}, u32[]{:S(2)}) collective-permute-start(bf16[9,128,128]{2,1,0:T(8,128)(2,1)} %collective-permute-done.3), channel_id=1, source_target_pairs={{0,4},{4,0},{8,12},{12,8},{16,20},{20,16},{24,28},{28,24},{1,5},{5... | collective-permute-start | bytes 884744 | tf_op jit(solution)/shard_map/ppermute | solution.py:763
  34.7 10.5 %collective-permute-start.4 = (bf16[9,128,128]{2,1,0:T(8,128)(2,1)}, bf16[9,128,128]{2,1,0:T(8,128)(2,1)}, u32[]{:S(2)}, u32[]{:S(2)}) collective-permute-start(bf16[9,128,128]{2,1,0:T(8,128)(2,1)} %collective-permute-done.3), channel_id=1, source_target_pairs={{0,8},{4,12},{8,16},{12,20},{16,24},{20,28},{1,9},{5,13},{9,17},{1... | collective-permute-start | bytes 884744 | tf_op jit(solution)/shard_map/ppermute | solution.py:991
  45.2 11.4 %collective-permute-start.8 = (bf16[9,128,128]{2,1,0:T(8,128)(2,1)}, bf16[9,128,128]{2,1,0:T(8,128)(2,1)}, u32[]{:S(2)}, u32[]{:S(2)}) collective-permute-start(bf16[9,128,128]{2,1,0:T(8,128)(2,1)} %collective-permute-done.4), channel_id=1, source_target_pairs={{0,8},{4,12},{8,16},{12,20},{16,24},{20,28},{1,9},{5,13},{9,17},{1... | collective-permute-start | bytes 884744 | tf_op jit(solution)/shard_map/ppermute | solution.py:991
  50.0 7.2 %collective-permute-start.5 = (bf16[9,128,128]{2,1,0:T(8,128)(2,1)}, bf16[9,128,128]{2,1,0:T(8,128)(2,1)}, u32[]{:S(2)}, u32[]{:S(2)}) collective-permute-start(bf16[9,128,128]{2,1,0:T(8,128)(2,1)} %collective-permute-done.4), channel_id=1, source_target_pairs={{0,4},{4,0},{8,12},{12,8},{16,20},{20,16},{24,28},{28,24},{1,5},{5... | collective-permute-start | bytes 884744 | tf_op jit(solution)/shard_map/ppermute | solution.py:763
  56.1 7.2 %collective-permute-start.10 = (bf16[144,3072]{1,0:T(8,128)(2,1)}, bf16[144,3072]{1,0:T(8,128)(2,1)}, u32[]{:S(2)}, u32[]{:S(2)}) collective-permute-start(bf16[144,3072]{1,0:T(8,128)(2,1)} %get-tuple-element.79.gu0), channel_id=1, source_target_pairs={{0,1},{1,0},{2,3},{3,2},{4,5},{5,4},{6,7},{7,6},{8,9},{9,8},{10,11... | collective-permute-start | bytes 2654216 | tf_op jit(solution)/shard_map/ppermute | solution.py:763
  56.1 7.1 %collective-permute-start.15 = (bf16[528,576]{1,0:T(8,128)(2,1)}, bf16[528,576]{1,0:T(8,128)(2,1)}, u32[]{:S(2)}, u32[]{:S(2)}) collective-permute-start(bf16[528,576]{1,0:T(8,128)(2,1)} %collective-permute-done.14.do2), channel_id=1, source_target_pairs={{0,1},{1,0},{2,3},{3,2},{4,5},{5,4},{6,7},{7,6},{8,9},{9,8},{10,11... | collective-permute-start | bytes 1824776 | tf_op jit(solution)/shard_map/ppermute | solution.py:763
  56.6 6.7 %collective-permute-start.12 = (bf16[144,3072]{1,0:T(8,128)(2,1)}, bf16[144,3072]{1,0:T(8,128)(2,1)}, u32[]{:S(2)}, u32[]{:S(2)}) collective-permute-start(bf16[144,3072]{1,0:T(8,128)(2,1)} %collective-permute-done.11.gu2), channel_id=1, source_target_pairs={{0,1},{1,0},{2,3},{3,2},{4,5},{5,4},{6,7},{7,6},{8,9},{9,8},{10,11... | collective-permute-start | bytes 2654216 | tf_op jit(solution)/shard_map/ppermute | solution.py:763
  57.2 9.2 %collective-permute-start.9 = (bf16[9,128,128]{2,1,0:T(8,128)(2,1)}, bf16[9,128,128]{2,1,0:T(8,128)(2,1)}, u32[]{:S(2)}, u32[]{:S(2)}) collective-permute-start(bf16[9,128,128]{2,1,0:T(8,128)(2,1)} %collective-permute-done.8), channel_id=1, source_target_pairs={{0,4},{4,0},{8,12},{12,8},{16,20},{20,16},{24,28},{28,24},{1,5},{5... | collective-permute-start | bytes 884744 | tf_op jit(solution)/shard_map/ppermute | solution.py:763
  87.1 6.1 %collective-permute-start.16 = (bf16[2,8,256,384]{3,2,1,0:T(8,128)(2,1)}, bf16[2,8,256,384]{3,2,1,0:T(8,128)(2,1)}, u32[]{:S(2)}, u32[]{:S(2)}) collective-permute-start(bf16[2,8,256,384]{3,2,1,0:T(8,128)(2,1)} %get-tuple-element.88), channel_id=1, source_target_pairs={{0,1},{1,0},{2,3},{3,2},{4,5},{5,4},{6,7},{7,6},{8,9},{9,8},{10,11... | collective-permute-start | bytes 9437192 | tf_op jit(solution)/shard_map/ppermute | solution.py:763
  96.7 36.8 %collective-permute-start.24 = (bf16[8,256,384]{2,1,0:T(8,128)(2,1)}, bf16[8,256,384]{2,1,0:T(8,128)(2,1)}, u32[]{:S(2)}, u32[]{:S(2)}) collective-permute-start(bf16[8,256,384]{2,1,0:T(8,128)(2,1)} %shard_map.220.refs_1_), channel_id=1, source_target_pairs={{0,2},{1,3},{2,0},{3,1},{4,6},{5,7},{6,4},{7,5},{8,10},{9,11},{10,... | collective-permute-start | bytes 4718600 | tf_op jit(solution)/shard_map/ppermute | solution.py:763
  98.3 10.2 %collective-permute-start.17 = (bf16[9,128,128]{2,1,0:T(8,128)(2,1)}, bf16[9,128,128]{2,1,0:T(8,128)(2,1)}, u32[]{:S(2)}, u32[]{:S(2)}) collective-permute-start(bf16[9,128,128]{2,1,0:T(8,128)(2,1)} %bitcast.56), channel_id=1, source_target_pairs={{0,4},{4,0},{8,12},{12,8},{16,20},{20,16},{24,28},{28,24},{1,5},{5... | collective-permute-start | bytes 884744 | tf_op jit(solution)/shard_map/ppermute | solution.py:763
  102.7 11.7 %collective-permute-start.18 = (bf16[9,128,128]{2,1,0:T(8,128)(2,1)}, bf16[9,128,128]{2,1,0:T(8,128)(2,1)}, u32[]{:S(2)}, u32[]{:S(2)}) collective-permute-start(bf16[9,128,128]{2,1,0:T(8,128)(2,1)} %bitcast.55), channel_id=1, source_target_pairs={{0,4},{4,0},{8,12},{12,8},{16,20},{20,16},{24,28},{28,24},{1,5},{5... | collective-permute-start | bytes 884744 | tf_op jit(solution)/shard_map/ppermute | solution.py:763
  112.6 12.3 %collective-permute-start.22 = (bf16[9,128,128]{2,1,0:T(8,128)(2,1)}, bf16[9,128,128]{2,1,0:T(8,128)(2,1)}, u32[]{:S(2)}, u32[]{:S(2)}) collective-permute-start(bf16[9,128,128]{2,1,0:T(8,128)(2,1)} %bitcast.54), channel_id=1, source_target_pairs={{0,4},{4,0},{8,12},{12,8},{16,20},{20,16},{24,28},{28,24},{1,5},{5... | collective-permute-start | bytes 884744 | tf_op jit(solution)/shard_map/ppermute | solution.py:763
  113.2 24.9 %collective-permute-start.20 = (bf16[9,128,128]{2,1,0:T(8,128)(2,1)}, bf16[9,128,128]{2,1,0:T(8,128)(2,1)}, u32[]{:S(2)}, u32[]{:S(2)}) collective-permute-start(bf16[9,128,128]{2,1,0:T(8,128)(2,1)} %get-tuple-element.99), channel_id=1, source_target_pairs={{24,0},{28,4},{25,1},{29,5},{26,2},{30,6},{27,3},{31,7}} | collective-permute-start | bytes 884744 | tf_op jit(solution)/shard_map/ppermute | solution.py:903
  122.2 15.9 %collective-permute-start.19 = (bf16[9,128,128]{2,1,0:T(8,128)(2,1)}, bf16[9,128,128]{2,1,0:T(8,128)(2,1)}, u32[]{:S(2)}, u32[]{:S(2)}) collective-permute-start(bf16[9,128,128]{2,1,0:T(8,128)(2,1)} %bitcast.53), channel_id=1, source_target_pairs={{0,4},{4,0},{8,12},{12,8},{16,20},{20,16},{24,28},{28,24},{1,5},{5... | collective-permute-start | bytes 884744 | tf_op jit(solution)/shard_map/ppermute | solution.py:763
  123.7 20.7 %collective-permute-start.21 = (bf16[9,128,128]{2,1,0:T(8,128)(2,1)}, bf16[9,128,128]{2,1,0:T(8,128)(2,1)}, u32[]{:S(2)}, u32[]{:S(2)}) collective-permute-start(bf16[9,128,128]{2,1,0:T(8,128)(2,1)} %get-tuple-element.100), channel_id=1, source_target_pairs={{16,0},{20,4},{24,8},{28,12},{17,1},{21,5},{25,9},{29,13},{18,2},{... | collective-permute-start | bytes 884744 | tf_op jit(solution)/shard_map/ppermute | solution.py:903
  126.8 18.0 %collective-permute-start.23 = (bf16[9,128,128]{2,1,0:T(8,128)(2,1)}, bf16[9,128,128]{2,1,0:T(8,128)(2,1)}, u32[]{:S(2)}, u32[]{:S(2)}) collective-permute-start(bf16[9,128,128]{2,1,0:T(8,128)(2,1)} %shard_map.224.refs_4_), channel_id=1, source_target_pairs={{8,0},{12,4},{16,8},{20,12},{24,16},{28,20},{9,1},{13,5},{17,9},{2... | collective-permute-start | bytes 884744 | tf_op jit(solution)/shard_map/ppermute | solution.py:903
  137.5 19.1 %collective-permute-start.26 = (bf16[4,256,384]{2,1,0:T(8,128)(2,1)}, bf16[4,256,384]{2,1,0:T(8,128)(2,1)}, u32[]{:S(2)}, u32[]{:S(2)}) collective-permute-start(bf16[4,256,384]{2,1,0:T(8,128)(2,1)} %get-tuple-element.107), channel_id=1, source_target_pairs={{0,4},{4,0},{8,12},{12,8},{16,20},{20,16},{24,28},{28,24},{1,5},{5... | collective-permute-start | bytes 2359304 | tf_op jit(solution)/shard_map/ppermute | solution.py:763
  152.1 6.8 %collective-permute-start.25 = (bf16[2,8,144,128]{3,2,1,0:T(8,128)(2,1)}, bf16[2,8,144,128]{3,2,1,0:T(8,128)(2,1)}, u32[]{:S(2)}, u32[]{:S(2)}) collective-permute-start(bf16[2,8,144,128]{3,2,1,0:T(8,128)(2,1)} %get-tuple-element.106), channel_id=1, source_target_pairs={{0,1},{1,0},{2,3},{3,2},{4,5},{5,4},{6,7},{7,6},{8,9},{9,8},{10,11... | collective-permute-start | bytes 1769480 | tf_op jit(solution)/shard_map/ppermute | solution.py:763
  161.4 29.3 %collective-permute-start.27 = (bf16[8,144,128]{2,1,0:T(8,128)(2,1)}, bf16[8,144,128]{2,1,0:T(8,128)(2,1)}, u32[]{:S(2)}, u32[]{:S(2)}) collective-permute-start(bf16[8,144,128]{2,1,0:T(8,128)(2,1)} %shard_map.228.refs_5_), channel_id=1, source_target_pairs={{0,2},{1,3},{2,0},{3,1},{4,6},{5,7},{6,4},{7,5},{8,10},{9,11},{10,... | collective-permute-start | bytes 884744 | tf_op jit(solution)/shard_map/ppermute | solution.py:763
  163.0 9.1 %collective-permute-start.28 = (bf16[256,384]{1,0:T(8,128)(2,1)}, bf16[256,384]{1,0:T(8,128)(2,1)}, u32[]{:S(2)}, u32[]{:S(2)}) collective-permute-start(bf16[256,384]{1,0:T(8,128)(2,1)} %get-tuple-element.109), channel_id=1, source_target_pairs={{0,8},{4,12},{8,0},{12,4},{16,24},{20,28},{24,16},{28,20},{1,9},{5... | collective-permute-start | bytes 589832 | tf_op jit(solution)/shard_map/ppermute | solution.py:763
  166.0 16.4 %collective-permute-start.29 = (bf16[256,384]{1,0:T(8,128)(2,1)}, bf16[256,384]{1,0:T(8,128)(2,1)}, u32[]{:S(2)}, u32[]{:S(2)}) collective-permute-start(bf16[256,384]{1,0:T(8,128)(2,1)} %get-tuple-element.110), channel_id=1, source_target_pairs={{0,16},{4,20},{8,24},{12,28},{16,0},{20,4},{24,8},{28,12},{1,17},{... | collective-permute-start | bytes 589832 | tf_op jit(solution)/shard_map/ppermute | solution.py:763
  167.3 15.0 %collective-permute-start.30 = (bf16[256,384]{1,0:T(8,128)(2,1)}, bf16[256,384]{1,0:T(8,128)(2,1)}, u32[]{:S(2)}, u32[]{:S(2)}) collective-permute-start(bf16[256,384]{1,0:T(8,128)(2,1)} %get-tuple-element.111), channel_id=1, source_target_pairs={{0,24},{4,28},{8,16},{12,20},{16,8},{20,12},{24,0},{28,4},{1,25},{... | collective-permute-start | bytes 589832 | tf_op jit(solution)/shard_map/ppermute | solution.py:763
  184.4 15.4 %collective-permute-start.37 = (bf16[256,384]{1,0:T(8,128)(2,1)}, bf16[256,384]{1,0:T(8,128)(2,1)}, u32[]{:S(2)}, u32[]{:S(2)}) collective-permute-start(bf16[256,384]{1,0:T(8,128)(2,1)} %shard_map.229.refs_4_.refs_1_), channel_id=1, source_target_pairs={{0,24},{4,28},{8,16},{12,20},{16,8},{20,12},{24,0},{28,4},{1,25},{... | collective-permute-start | bytes 589832 | tf_op jit(solution)/shard_map/ppermute | solution.py:763
  186.3 18.2 %collective-permute-start.36 = (bf16[256,384]{1,0:T(8,128)(2,1)}, bf16[256,384]{1,0:T(8,128)(2,1)}, u32[]{:S(2)}, u32[]{:S(2)}) collective-permute-start(bf16[256,384]{1,0:T(8,128)(2,1)} %shard_map.229.refs_4_.refs_1_), channel_id=1, source_target_pairs={{0,16},{4,20},{8,24},{12,28},{16,0},{20,4},{24,8},{28,12},{1,17},{... | collective-permute-start | bytes 589832 | tf_op jit(solution)/shard_map/ppermute | solution.py:763
  190.6 13.9 %collective-permute-start.35 = (bf16[256,384]{1,0:T(8,128)(2,1)}, bf16[256,384]{1,0:T(8,128)(2,1)}, u32[]{:S(2)}, u32[]{:S(2)}) collective-permute-start(bf16[256,384]{1,0:T(8,128)(2,1)} %shard_map.229.refs_4_.refs_1_), channel_id=1, source_target_pairs={{0,8},{4,12},{8,0},{12,4},{16,24},{20,28},{24,16},{28,20},{1,9},{5... | collective-permute-start | bytes 589832 | tf_op jit(solution)/shard_map/ppermute | solution.py:763
  192.7 5.5 %collective-permute-start.31 = (bf16[4,144,128]{2,1,0:T(8,128)(2,1)}, bf16[4,144,128]{2,1,0:T(8,128)(2,1)}, u32[]{:S(2)}, u32[]{:S(2)}) collective-permute-start(bf16[4,144,128]{2,1,0:T(8,128)(2,1)} %get-tuple-element.113), channel_id=1, source_target_pairs={{0,4},{4,0},{8,12},{12,8},{16,20},{20,16},{24,28},{28,24},{1,5},{5... | collective-permute-start | bytes 442376 | tf_op jit(solution)/shard_map/ppermute | solution.py:763
  206.7 20.9 %collective-permute-start.42 = (bf16[4,256,384]{2,1,0:T(8,128)(2,1)}, bf16[4,256,384]{2,1,0:T(8,128)(2,1)}, u32[]{:S(2)}, u32[]{:S(2)}) collective-permute-start(bf16[4,256,384]{2,1,0:T(8,128)(2,1)} %shard_map.232.refs_5_.refs_0_), channel_id=1, source_target_pairs={{0,4},{4,0},{8,12},{12,8},{16,20},{20,16},{24,28},{28,24},{1,5},{5... | collective-permute-start | bytes 2359304 | tf_op jit(solution)/shard_map/ppermute | solution.py:763
  207.3 4.4 %collective-permute-start.32 = (bf16[144,128]{1,0:T(8,128)(2,1)}, bf16[144,128]{1,0:T(8,128)(2,1)}, u32[]{:S(2)}, u32[]{:S(2)}) collective-permute-start(bf16[144,128]{1,0:T(8,128)(2,1)} %get-tuple-element.115), channel_id=1, source_target_pairs={{0,8},{4,12},{8,0},{12,4},{16,24},{20,28},{24,16},{28,20},{1,9},{5... | collective-permute-start | bytes 110600 | tf_op jit(solution)/shard_map/ppermute | solution.py:763
  207.3 5.7 %collective-permute-start.33 = (bf16[144,128]{1,0:T(8,128)(2,1)}, bf16[144,128]{1,0:T(8,128)(2,1)}, u32[]{:S(2)}, u32[]{:S(2)}) collective-permute-start(bf16[144,128]{1,0:T(8,128)(2,1)} %get-tuple-element.116), channel_id=1, source_target_pairs={{0,16},{4,20},{8,24},{12,28},{16,0},{20,4},{24,8},{28,12},{1,17},{... | collective-permute-start | bytes 110600 | tf_op jit(solution)/shard_map/ppermute | solution.py:763
  210.1 6.1 %collective-permute-start.34 = (bf16[144,128]{1,0:T(8,128)(2,1)}, bf16[144,128]{1,0:T(8,128)(2,1)}, u32[]{:S(2)}, u32[]{:S(2)}) collective-permute-start(bf16[144,128]{1,0:T(8,128)(2,1)} %get-tuple-element.117), channel_id=1, source_target_pairs={{0,24},{4,28},{8,16},{12,20},{16,8},{20,12},{24,0},{28,4},{1,25},{... | collective-permute-start | bytes 110600 | tf_op jit(solution)/shard_map/ppermute | solution.py:763
  217.6 6.1 %collective-permute-start.40 = (bf16[144,128]{1,0:T(8,128)(2,1)}, bf16[144,128]{1,0:T(8,128)(2,1)}, u32[]{:S(2)}, u32[]{:S(2)}) collective-permute-start(bf16[144,128]{1,0:T(8,128)(2,1)} %shard_map.233.refs_1_.refs_5_), channel_id=1, source_target_pairs={{0,24},{4,28},{8,16},{12,20},{16,8},{20,12},{24,0},{28,4},{1,25},{... | collective-permute-start | bytes 110600 | tf_op jit(solution)/shard_map/ppermute | solution.py:763
  219.2 5.4 %collective-permute-start.39 = (bf16[144,128]{1,0:T(8,128)(2,1)}, bf16[144,128]{1,0:T(8,128)(2,1)}, u32[]{:S(2)}, u32[]{:S(2)}) collective-permute-start(bf16[144,128]{1,0:T(8,128)(2,1)} %shard_map.233.refs_1_.refs_5_), channel_id=1, source_target_pairs={{0,16},{4,20},{8,24},{12,28},{16,0},{20,4},{24,8},{28,12},{1,17},{... | collective-permute-start | bytes 110600 | tf_op jit(solution)/shard_map/ppermute | solution.py:763
  219.2 5.5 %collective-permute-start.38 = (bf16[144,128]{1,0:T(8,128)(2,1)}, bf16[144,128]{1,0:T(8,128)(2,1)}, u32[]{:S(2)}, u32[]{:S(2)}) collective-permute-start(bf16[144,128]{1,0:T(8,128)(2,1)} %shard_map.233.refs_1_.refs_5_), channel_id=1, source_target_pairs={{0,8},{4,12},{8,0},{12,4},{16,24},{20,28},{24,16},{28,20},{1,9},{5... | collective-permute-start | bytes 110600 | tf_op jit(solution)/shard_map/ppermute | solution.py:763
  226.2 5.5 %collective-permute-start.41 = (bf16[4,144,128]{2,1,0:T(8,128)(2,1)}, bf16[4,144,128]{2,1,0:T(8,128)(2,1)}, u32[]{:S(2)}, u32[]{:S(2)}) collective-permute-start(bf16[4,144,128]{2,1,0:T(8,128)(2,1)} %shard_map.234.refs_0_), channel_id=1, source_target_pairs={{0,4},{4,0},{8,12},{12,8},{16,20},{20,16},{24,28},{28,24},{1,5},{5... | collective-permute-start | bytes 442376 | tf_op jit(solution)/shard_map/ppermute | solution.py:763

commit v4 on v3

--- a/solution.py
+++ b/solution.py
@@ -816,12 +816,43 @@
     )(place, keep, got, *after)
 
 
-def y_kernel(place_ref, keep, got, far, mine, away):
+def y_kernel(place_ref, keep, got, far, *refs):
+    mine, away, keep_all, got_all, far_all, mine_all, away_all, sems = refs[-8:]
     x_bit = place_ref[0]
-    for c in range(4):
-        here, there = 4 * x_bit + c, 4 * (1 - x_bit) + c
-        mine[c] = total_of(keep[0, here], got[0, here], far[here])
-        away[c] = total_of(keep[0, there], got[0, there], far[there])
+    plan = [(4 * (1 - x_bit) + c, away_all, away, c) for c in range(4)]
+    plan += [(4 * x_bit + c, mine_all, mine, c) for c in range(4)]
+    loads = []
+    for at, (chunk, *_) in enumerate(plan):
+        sources = ((keep.at[0], keep_all), (got.at[0], got_all), (far, far_all))
+        for i, (source, target) in enumerate(sources):
+            copy = pltpu.make_async_copy(source.at[chunk], target.at[at], sems.at[i, at])
+            copy.start()
+            loads.append(copy)
+    stores = []
+    for at, (chunk, held, target, c) in enumerate(plan):
+        for copy in loads[3 * at : 3 * at + 3]:
+            copy.wait()
+        held[c] = total_of(keep_all[at], got_all[at], far_all[at])
+        copy = pltpu.make_async_copy(held.at[c], target.at[c], sems.at[3, at])
+        copy.start()
+        stores.append(copy)
+    for copy in stores:
+        copy.wait()
+
+
+def y_sum(place, keep, got, far, after):
+    hbm = pl.BlockSpec(memory_space=pl.ANY)
+    whole, half = far.shape, (4,) + far.shape[1:]
+    return call(
+        y_kernel,
+        (sds(half, BF16), sds(half, BF16)),
+        [pl.BlockSpec(memory_space=pltpu.SMEM)] + [hbm] * (3 + len(after)),
+        cost=0.05,
+        out_specs=(hbm, hbm),
+        scratch_shapes=[pltpu.VMEM(whole, BF16)] * 3
+        + [pltpu.VMEM(half, BF16)] * 2
+        + [pltpu.SemaphoreType.DMA((4, CHUNKS))],
+    )(place, keep, got, far, *after)
 
 
 def x_kernel(place_ref, keep, got, *outs):
@@ -865,15 +896,8 @@
         self.parts = (keep, got, flip(away, "fsdp", 2))
         return away
 
-    def y_specs(self):
-        first = pl.BlockSpec((1, CHUNKS) + self.shape, lambda i: (0, 0, 0, 0))
-        return [first, first, pl.BlockSpec(memory_space=pltpu.VMEM)]
-
     def y(self, *after):
-        shape = (4,) + self.shape
-        keep, send = fuse(
-            y_kernel, self.place, [shape] * 2, self.parts, after, self.y_specs(), None, (1,)
-        )
+        keep, send = y_sum(self.place, *self.parts, after)
         self.parts = (keep, flip(send, "ctx", 1))
         return keep
 

time: 234 us -> 234 us (level)
    pallas_call x0 -> x2, Pallas kernels: none -> 7.02 us  [y_sum(): call(y_kernel, (sds(half, BF16), sds(half, BF16)), [pl.BlockSpec(memory_s...]
    pallas_call x9 -> x7, Pallas kernels: 19 us -> 13 us  [fuse(): call(body, tuple((sds(shape, BF16) for shape in outs)), [pl.BlockSpec(mem...]
  transfers between devices with their start and end apart: 43 -> 43, of which waited for: 20 -> 20; matrix products, arithmetic and copies ran while one was open for 3% -> 3% of each run, Pallas kernels for 29% -> 30%
where the time goes in v4:
time: 234 us; the launch traced here: 233 us
  Pallas kernels  102 us (44%)
  waiting for transfers between devices  62.9 us (27%)
  starting transfers between devices  59.2 us (25%)
  other arithmetic  7.9 us (3%)
    ppermute x37, waiting for transfers between devices, flip(): return lax.ppermute(x, axis, [(i, i ^ mask) for i in range(n)])  52.7 us
    ppermute x37, starting transfers between devices, flip(): return lax.ppermute(x, axis, [(i, i ^ mask) for i in range(n)])  41 us
    pallas_call x1, Pallas kernels, middle(): call(functools.partial(middle_kernel, fused), (sds((tiles // KV_HEADS, di...  20.7 us
    pallas_call x4, Pallas kernels, attend_back(): call(functools.partial(attend_back_kernel, steps, diagonal, carry is None...  19.1 us
    pallas_call x3, Pallas kernels, attend(): call(functools.partial(attend_kernel, steps, diagonal, carry is None), (s...  14.5 us
    ppermute x3, starting transfers between devices, local(): piece = lax.ppermute(piece, 'ctx', up)  14.2 us
    pallas_call x7, Pallas kernels, fuse(): call(body, tuple((sds(shape, BF16) for shape in outs)), [pl.BlockSpec(mem...  13 us
    pallas_call x1, Pallas kernels, finish(): call(functools.partial(end_kernel, parts=len(dkv)), (sds((tiles // KV_HEA...  7.26 us
  transfers between devices with their start and end apart: 43, of which 20 were waited for; matrix products, arithmetic and copies ran while one was open for 3% of the time, Pallas kernels for 30%

profile of v4, /device:TPU:0, one launch (start us, length us, event | category | flops | bytes accessed | tf_op | source)
XLA Modules:
  0.0 232.8 jit_solution(12445919865730498513)
XLA Ops:
  0.6 1.9 shard_map.212.w0
  2.6 3.0 %collective-permute-start.1 = (bf16[144,1024]{1,0:T(8,128)(2,1)}, bf16[144,1024]{1,0:T(8,128)(2,1)}, u32[]{:S(2)}, u32[]{:S(2)}) collective-permute-start(bf16[144,1024]{1,0:T(8,128)(2,1)} %shard_map.212.w0), channel_id=1, source_target_pairs={{0,2},{1,3},{2,0},{3,1},{4,6},{5,7},{6,4},{7,5},{8,10},{9,11},{10,... | collective-permute-start | bytes 884744 | tf_op jit(solution)/shard_map/ppermute | solution.py:763
  5.5 2.7 %shard_map.217 = (bf16[144,3072]{1,0:T(8,128)(2,1)}, bf16[528,576]{1,0:T(8,128)(2,1)}) custom-call(bf16[144,1536]{1,0:T(8,128)(2,1)} %gate_ref.1, bf16[144,1536]{1,0:T(8,128)(2,1)} %up_ref.1, bf16[576,384]{1,0:T(8,128)(2,1)} %bitcast.50, bf16[144,576]{1,0:T(8,128)(2,1)} %w_ref.1), custom_call_target="tpu_custom_call" | custom-call | flops 3000000000 | tf_op jit(solution)/shard_map/pallas_call | solution.py:986
  8.7 1.7 collective-permute-start.11
  11.2 2.5 %collective-permute-done.1.w2 = bf16[144,1024]{1,0:T(8,128)(2,1)} collective-permute-done((bf16[144,1024]{1,0:T(8,128)(2,1)}, bf16[144,1024]{1,0:T(8,128)(2,1)}, u32[]{:S(2)}, u32[]{:S(2)}) %collective-permute-start.1) | collective-permute-done | bytes 294944 | tf_op jit(solution)/shard_map/ppermute | solution.py:763
  17.5 4.2 %shard_map.213 = (bf16[576,1024]{1,0:T(8,128)(2,1)}, bf16[384,576]{1,0:T(8,128)(2,1)}, bf16[9,384,128]{2,1,0:T(8,128)(2,1)}, bf16[9,128,128]{2,1,0:T(8,128)(2,1)...) custom-call(s32[1]{0:T(128)} %bitcast.index_ref, bf16[3,576,128]{2,1,0:T(8,128)(2,1)} %bitcast.51, ...), custom_call_target="tpu_custom_call" | custom-call | flops 4000000000 | tf_op jit(solution)/shard_map/pallas_call | solution.py:971
  21.7 2.0 collective-permute-start.7
  23.7 4.2 %collective-permute-start.3 = (bf16[9,128,128]{2,1,0:T(8,128)(2,1)}, bf16[9,128,128]{2,1,0:T(8,128)(2,1)}, u32[]{:S(2)}, u32[]{:S(2)}) collective-permute-start(bf16[9,128,128]{2,1,0:T(8,128)(2,1)} %get-tuple-element.72), channel_id=1, source_target_pairs={{0,8},{4,12},{8,16},{12,20},{16,24},{20,28},{1,9},{5,13},{9,17},{1... | collective-permute-start | bytes 884744 | tf_op jit(solution)/shard_map/ppermute | solution.py:1015
  30.6 3.5 %collective-permute-done.3 = bf16[9,128,128]{2,1,0:T(8,128)(2,1)} collective-permute-done((bf16[9,128,128]{2,1,0:T(8,128)(2,1)}, bf16[9,128,128]{2,1,0:T(8,128)(2,1)}, u32[]{:S(2)}, u32[]{:S(2)}) %collective-permute-start.3) | collective-permute-done | bytes 294944 | tf_op jit(solution)/shard_map/ppermute | solution.py:1015
  34.7 5.1 %collective-permute-start.4 = (bf16[9,128,128]{2,1,0:T(8,128)(2,1)}, bf16[9,128,128]{2,1,0:T(8,128)(2,1)}, u32[]{:S(2)}, u32[]{:S(2)}) collective-permute-start(bf16[9,128,128]{2,1,0:T(8,128)(2,1)} %collective-permute-done.3), channel_id=1, source_target_pairs={{0,8},{4,12},{8,16},{12,20},{16,24},{20,28},{1,9},{5,13},{9,17},{1... | collective-permute-start | bytes 884744 | tf_op jit(solution)/shard_map/ppermute | solution.py:1015
  39.8 5.4 %shard_map.214 = (f32[9,384,128]{2,1,0:T(8,128)}, f32[9,384,128]{2,1,0:T(8,128)}) custom-call(s32[9]{0:T(128)} %get-tuple-element.130.info_ref, bf16[9,384,128]{2,1,0:T(8,128)(2,1)} %get-tuple-element.71.q_ref, bf16[1,9,128,128]{3,2,1,0:T(8,128)(2,1)} %bitcast.42, bf16[1,9,128,128]{3,2,1,0:T(8,128)(2,1)} %bitcast.18.b_ref), custom_call_target="tpu_custom_call" | custom-call | flops 10000000000 | tf_op jit(solution)/shard_map/pallas_call | solution.py:224
  45.2 4.9 %collective-permute-start.8 = (bf16[9,128,128]{2,1,0:T(8,128)(2,1)}, bf16[9,128,128]{2,1,0:T(8,128)(2,1)}, u32[]{:S(2)}, u32[]{:S(2)}) collective-permute-start(bf16[9,128,128]{2,1,0:T(8,128)(2,1)} %collective-permute-done.4), channel_id=1, source_target_pairs={{0,8},{4,12},{8,16},{12,20},{16,24},{20,28},{1,9},{5,13},{9,17},{1... | collective-permute-start | bytes 884744 | tf_op jit(solution)/shard_map/ppermute | solution.py:1015
  51.5 4.6 %shard_map.215 = (f32[9,384,128]{2,1,0:T(8,128)}, f32[9,384,128]{2,1,0:T(8,128)}) custom-call(s32[9]{0:T(128)} %get-tuple-element.132.info_ref, bf16[9,384,128]{2,1,0:T(8,128)(2,1)} %get-tuple-element.71.q_ref, bf16[1,9,128,128]{3,2,1,0:T(8,128)(2,1)} %bitcast.13.a_ref, bf16[1,9,128,128]{3,2,1,0:T(8,128)(2,1)} %bitcast.14.b_ref, ...), custom_call_target="tpu_custom_call" | custom-call | flops 10000000000 | tf_op jit(solution)/shard_map/pallas_call | solution.py:224
  58.7 4.6 %shard_map.216 = (f32[9,384,128]{2,1,0:T(8,128)}, f32[9,384,128]{2,1,0:T(8,128)}) custom-call(s32[9]{0:T(128)} %get-tuple-element.131.info_ref, bf16[9,384,128]{2,1,0:T(8,128)(2,1)} %get-tuple-element.71.q_ref, bf16[1,9,128,128]{3,2,1,0:T(8,128)(2,1)} %bitcast.9.a_ref, bf16[1,9,128,128]{3,2,1,0:T(8,128)(2,1)} %bitcast.10.b_ref, ...), custom_call_target="tpu_custom_call" | custom-call | flops 10000000000 | tf_op jit(solution)/shard_map/pallas_call | solution.py:224
  63.3 3.1 %collective-permute-done.9 = bf16[9,128,128]{2,1,0:T(8,128)(2,1)} collective-permute-done((bf16[9,128,128]{2,1,0:T(8,128)(2,1)}, bf16[9,128,128]{2,1,0:T(8,128)(2,1)}, u32[]{:S(2)}, u32[]{:S(2)}) %collective-permute-start.9) | collective-permute-done | bytes 294944 | tf_op jit(solution)/shard_map/ppermute | solution.py:763
  66.3 20.7 %shard_map.218 = (f32[3,576,128]{2,1,0:T(8,128)}, f32[384,576]{1,0:T(8,128)}, bf16[9,384,128]{2,1,0:T(8,128)(2,1)}, f32[9,8,384]{2,1,0:T(8,128)}, bf16[2,8,256,3...) custom-call(s32[1]{0:T(128)} %bitcast.index_ref, s32[9]{0:T(128)} %get-tuple-element.133.info_ref, ...), custom_call_target="tpu_custom_call" | custom-call | flops 20000000000 | tf_op jit(solution)/shard_map/pallas_call | solution.py:532
  87.8 3.3 %shard_map.219 = (f32[9,384,128]{2,1,0:T(8,128)}, bf16[1,9,128,128]{3,2,1,0:T(8,128)(2,1)}, bf16[1,9,128,128]{3,2,1,0:T(8,128)(2,1)}) custom-call(s32[9]{0:T(128)} %get-tuple-element.133.info_ref, bf16[9,384,128]{2,1,0:T(8,128)(2,1)} %get-tuple-element.71.q_ref, bf16[9,384,128]{2,1,0:T(8,128)(2,1)} %get-tuple-element.84.d_ref, ...), custom_call_target="tpu_custom_call" | custom-call | flops 50000000 | tf_op jit(solution)/shard_map/pallas_call | solution.py:305
  91.1 2.0 collective-permute-done.16.got
  93.2 3.5 %shard_map.220.refs_1_ = bf16[8,256,384]{2,1,0:T(8,128)(2,1)} custom-call(s32[3]{0:T(128)} %pad_add_fusion.place_ref.refs_0_, bf16[2,8,256,384]{3,2,1,0:T(8,128)(2,1)} %get-tuple-element.87.keep, bf16[2,8,256,384]{3,2,1,0:T(8,128)(2,1)} %collective-permute-done.16.got, f32[9,384,128]{2,1,0:T(8,128)} %get-tuple-element.86.refs_0_), custom_call_target="tpu_custom_call" | custom-call | flops 50000000 | tf_op jit(solution)/shard_map/pallas_call | solution.py:809
  98.8 3.9 %shard_map.221 = (f32[9,384,128]{2,1,0:T(8,128)}, bf16[1,9,128,128]{3,2,1,0:T(8,128)(2,1)}, bf16[1,9,128,128]{3,2,1,0:T(8,128)(2,1)}) custom-call(s32[9]{0:T(128)} %get-tuple-element.131.info_ref, bf16[9,384,128]{2,1,0:T(8,128)(2,1)} %get-tuple-element.71.q_ref, bf16[9,384,128]{2,1,0:T(8,128)(2,1)} %get-tuple-element.84.d_ref, ...), custom_call_target="tpu_custom_call" | custom-call | flops 50000000 | tf_op jit(solution)/shard_map/pallas_call | solution.py:305
  104.2 4.3 %collective-permute-done.17.refs_2_ = bf16[9,128,128]{2,1,0:T(8,128)(2,1)} collective-permute-done((bf16[9,128,128]{2,1,0:T(8,128)(2,1)}, bf16[9,128,128]{2,1,0:T(8,128)(2,1)}, u32[]{:S(2)}, u32[]{:S(2)}) %collective-permute-start.17) | collective-permute-done | bytes 294944 | tf_op jit(solution)/shard_map/ppermute | solution.py:763
  108.5 4.1 %shard_map.222 = (f32[9,384,128]{2,1,0:T(8,128)}, bf16[1,9,128,128]{3,2,1,0:T(8,128)(2,1)}, bf16[1,9,128,128]{3,2,1,0:T(8,128)(2,1)}, bf16[9,128,128]{2,1,0:T(8,128)(2,1)}) custom-call(s32[9]{0:T(128)} %get-tuple-element.132.info_ref, bf16[9,384,128]{2,1,0:T(8,128)(2,1)} %get-tuple-element.71.q_ref, bf16[9,384,128]{2,1,0:T(8,128)(2,1)} %get-tuple-element.84.d_ref, ...), custom_call_target="tpu_custom_call" | custom-call | flops 50000000 | tf_op jit(solution)/shard_map/pallas_call | solution.py:305
  114.5 7.7 %shard_map.223 = (f32[9,384,128]{2,1,0:T(8,128)}, bf16[1,9,128,128]{3,2,1,0:T(8,128)(2,1)}, bf16[1,9,128,128]{3,2,1,0:T(8,128)(2,1)}, bf16[9,128,128]{2,1,0:T(8,128)(2,1)}) custom-call(s32[9]{0:T(128)} %get-tuple-element.130.info_ref, bf16[9,384,128]{2,1,0:T(8,128)(2,1)} %get-tuple-element.71.q_ref, bf16[9,384,128]{2,1,0:T(8,128)(2,1)} %get-tuple-element.84.d_ref, ...), custom_call_target="tpu_custom_call" | custom-call | flops 50000000 | tf_op jit(solution)/shard_map/pallas_call | solution.py:305
  125.0 1.8 shard_map.224.refs_0_
  128.4 5.1 %collective-permute-done.24.far = bf16[8,256,384]{2,1,0:T(8,128)(2,1)} collective-permute-done((bf16[8,256,384]{2,1,0:T(8,128)(2,1)}, bf16[8,256,384]{2,1,0:T(8,128)(2,1)}, u32[]{:S(2)}, u32[]{:S(2)}) %collective-permute-start.24) | collective-permute-done | bytes 1572896 | tf_op jit(solution)/shard_map/ppermute | solution.py:763
  133.5 4.3 %shard_map.225 = (bf16[4,256,384]{2,1,0:T(8,128)(2,1)}, bf16[4,256,384]{2,1,0:T(8,128)(2,1)}) custom-call(s32[3]{0:T(128)} %pad_add_fusion.place_ref.refs_0_, bf16[2,8,256,384]{3,2,1,0:T(8,128)(2,1)} %get-tuple-element.87.keep, bf16[2,8,256,384]{3,2,1,0:T(8,128)(2,1)} %collective-permute-done.16.got, bf16[8,256,384]{2,1,0:T(8,128)(2,1)} %collective-permute-done.24.far, ...), custom_call_target="tpu_custom_call" | custom-call | flops 50000000 | tf_op jit(solution)/shard_map/pallas_call | solution.py:846
  138.4 5.8 %collective-permute-done.21.refs_3_ = bf16[9,128,128]{2,1,0:T(8,128)(2,1)} collective-permute-done((bf16[9,128,128]{2,1,0:T(8,128)(2,1)}, bf16[9,128,128]{2,1,0:T(8,128)(2,1)}, u32[]{:S(2)}, u32[]{:S(2)}) %collective-permute-start.21) | collective-permute-done | bytes 294944 | tf_op jit(solution)/shard_map/ppermute | solution.py:927
  145.1 7.3 %shard_map.226 = (f32[3,576,128]{2,1,0:T(8,128)}, bf16[2,8,144,128]{3,2,1,0:T(8,128)(2,1)}, bf16[2,8,144,128]{3,2,1,0:T(8,128)(2,1)}) custom-call(s32[1]{0:T(128)} %bitcast.index_ref, bf16[384,576]{1,0:T(8,128)(2,1)} %get-tuple-element.69.x_ref, bf16[384,576]{1,0:T(8,128)(2,1)} %get-tuple-element.82.normed_ref, bf16[576,1024]{1,0:T(8,128)(2,1)} %get-tuple-element.83.w_ref, ...), custom_call_target="tpu_custom_call" | custom-call | flops 50000000 | tf_op jit(solution)/shard_map/pallas_call | solution.py:649
  152.4 4.6 %collective-permute-done.26.refs_2_ = bf16[4,256,384]{2,1,0:T(8,128)(2,1)} collective-permute-done((bf16[4,256,384]{2,1,0:T(8,128)(2,1)}, bf16[4,256,384]{2,1,0:T(8,128)(2,1)}, u32[]{:S(2)}, u32[]{:S(2)}) %collective-permute-start.26) | collective-permute-done | bytes 786464 | tf_op jit(solution)/shard_map/ppermute | solution.py:763
  157.0 2.3 shard_map.227
  159.3 2.5 %shard_map.228.refs_5_ = bf16[8,144,128]{2,1,0:T(8,128)(2,1)} custom-call(s32[3]{0:T(128)} %pad_add_fusion.place_ref.refs_0_, bf16[2,8,144,128]{3,2,1,0:T(8,128)(2,1)} %get-tuple-element.105.refs_3_.keep, bf16[2,8,144,128]{3,2,1,0:T(8,128)(2,1)} %collective-permute-done.25.got, bf16[256,384]{1,0:T(8,128)(2,1)} %get-tuple-element.108.refs_0_.refs_1_), custom_call_target="tpu_custom_call" | custom-call | flops 50000000 | tf_op jit(solution)/shard_map/pallas_call | solution.py:809
  163.4 2.3 collective-permute-start.28
  165.7 2.0 collective-permute-start.29
  168.2 4.0 %collective-permute-done.28.refs_2_ = bf16[256,384]{1,0:T(8,128)(2,1)} collective-permute-done((bf16[256,384]{1,0:T(8,128)(2,1)}, bf16[256,384]{1,0:T(8,128)(2,1)}, u32[]{:S(2)}, u32[]{:S(2)}) %collective-permute-start.28) | collective-permute-done | bytes 196640 | tf_op jit(solution)/shard_map/ppermute | solution.py:763
  172.1 10.1 %collective-permute-done.29.refs_3_ = bf16[256,384]{1,0:T(8,128)(2,1)} collective-permute-done((bf16[256,384]{1,0:T(8,128)(2,1)}, bf16[256,384]{1,0:T(8,128)(2,1)}, u32[]{:S(2)}, u32[]{:S(2)}) %collective-permute-start.29) | collective-permute-done | bytes 196640 | tf_op jit(solution)/shard_map/ppermute | solution.py:763
  182.2 2.0 shard_map.229.refs_0_.refs_1_
  184.2 2.3 collective-permute-start.37
  186.6 4.0 %collective-permute-start.36 = (bf16[256,384]{1,0:T(8,128)(2,1)}, bf16[256,384]{1,0:T(8,128)(2,1)}, u32[]{:S(2)}, u32[]{:S(2)}) collective-permute-start(bf16[256,384]{1,0:T(8,128)(2,1)} %shard_map.229.refs_0_.refs_1_), channel_id=1, source_target_pairs={{0,16},{4,20},{8,24},{12,28},{16,0},{20,4},{24,8},{28,12},{1,17},{... | collective-permute-start | bytes 589832 | tf_op jit(solution)/shard_map/ppermute | solution.py:763
  190.6 2.7 %shard_map.230 = (bf16[4,144,128]{2,1,0:T(8,128)(2,1)}, bf16[4,144,128]{2,1,0:T(8,128)(2,1)}) custom-call(s32[3]{0:T(128)} %pad_add_fusion.place_ref.refs_0_, bf16[2,8,144,128]{3,2,1,0:T(8,128)(2,1)} %get-tuple-element.105.refs_3_.keep, bf16[2,8,144,128]{3,2,1,0:T(8,128)(2,1)} %collective-permute-done.25.got, ...), custom_call_target="tpu_custom_call" | custom-call | flops 50000000 | tf_op jit(solution)/shard_map/pallas_call | solution.py:846
  193.4 5.4 %collective-permute-done.31.refs_2_ = bf16[4,144,128]{2,1,0:T(8,128)(2,1)} collective-permute-done((bf16[4,144,128]{2,1,0:T(8,128)(2,1)}, bf16[4,144,128]{2,1,0:T(8,128)(2,1)}, u32[]{:S(2)}, u32[]{:S(2)}) %collective-permute-start.31) | collective-permute-done | bytes 147488 | tf_op jit(solution)/shard_map/ppermute | solution.py:763
  202.1 2.2 shard_map.232.refs_5_.refs_0_
  206.0 3.2 %collective-permute-start.33 = (bf16[144,128]{1,0:T(8,128)(2,1)}, bf16[144,128]{1,0:T(8,128)(2,1)}, u32[]{:S(2)}, u32[]{:S(2)}) collective-permute-start(bf16[144,128]{1,0:T(8,128)(2,1)} %get-tuple-element.116), channel_id=1, source_target_pairs={{0,16},{4,20},{8,24},{12,28},{16,0},{20,4},{24,8},{28,12},{1,17},{... | collective-permute-start | bytes 110600 | tf_op jit(solution)/shard_map/ppermute | solution.py:763
  211.5 3.9 %collective-permute-done.34.refs_4_ = bf16[144,128]{1,0:T(8,128)(2,1)} collective-permute-done((bf16[144,128]{1,0:T(8,128)(2,1)}, bf16[144,128]{1,0:T(8,128)(2,1)}, u32[]{:S(2)}, u32[]{:S(2)}) %collective-permute-start.34) | collective-permute-done | bytes 36896 | tf_op jit(solution)/shard_map/ppermute | solution.py:763
  218.0 3.2 %collective-permute-start.38 = (bf16[144,128]{1,0:T(8,128)(2,1)}, bf16[144,128]{1,0:T(8,128)(2,1)}, u32[]{:S(2)}, u32[]{:S(2)}) collective-permute-start(bf16[144,128]{1,0:T(8,128)(2,1)} %shard_map.233.refs_1_.refs_5_), channel_id=1, source_target_pairs={{0,8},{4,12},{8,0},{12,4},{16,24},{20,28},{24,16},{28,20},{1,9},{5... | collective-permute-start | bytes 110600 | tf_op jit(solution)/shard_map/ppermute | solution.py:763
  221.2 1.7 collective-permute-done.40.refs_4_
  225.5 3.5 %shard_map.235 = (f32[144,1536]{1,0:T(8,128)}, f32[144,1536]{1,0:T(8,128)}, f32[576,384]{1,0:T(8,128)}, f32[144,576]{1,0:T(8,128)}, f32[1,144]{1,0:T(1,128)}) custom-call(s32[3]{0:T(128)} %pad_add_fusion.place_ref.refs_0_, bf16[4,256,384]{2,1,0:T(8,128)(2,1)} %shard_map.232.refs_5_.refs_0_, bf16[4,256,384]{2,1,0:T(8,128)(2,1)} %collective-permute-done.42.refs_1_), custom_call_target="tpu_custom_call" | custom-call | flops 50000000 | tf_op jit(solution)/shard_map/pallas_call | solution.py:725
  229.0 1.8 collective-permute-done.41.refs_1_
  230.8 2.0 shard_map.236
  (75 shorter events, 39.0 us)
Async XLA Ops:
  2.6 11.1 %collective-permute-start.1 = (bf16[144,1024]{1,0:T(8,128)(2,1)}, bf16[144,1024]{1,0:T(8,128)(2,1)}, u32[]{:S(2)}, u32[]{:S(2)}) collective-permute-start(bf16[144,1024]{1,0:T(8,128)(2,1)} %shard_map.212.w0), channel_id=1, source_target_pairs={{0,2},{1,3},{2,0},{3,1},{4,6},{5,7},{6,4},{7,5},{8,10},{9,11},{10,... | collective-permute-start | bytes 884744 | tf_op jit(solution)/shard_map/ppermute | solution.py:763
  5.5 11.9 %collective-permute-start = (bf16[144,1024]{1,0:T(8,128)(2,1)}, bf16[144,1024]{1,0:T(8,128)(2,1)}, u32[]{:S(2)}, u32[]{:S(2)}) collective-permute-start(bf16[144,1024]{1,0:T(8,128)(2,1)} %shard_map.212.w0), channel_id=1, source_target_pairs={{0,1},{1,0},{2,3},{3,2},{4,5},{5,4},{6,7},{7,6},{8,9},{9,8},{10,11... | collective-permute-start | bytes 884744 | tf_op jit(solution)/shard_map/ppermute | solution.py:763
  8.2 47.9 %collective-permute-start.14 = (bf16[528,576]{1,0:T(8,128)(2,1)}, bf16[528,576]{1,0:T(8,128)(2,1)}, u32[]{:S(2)}, u32[]{:S(2)}) collective-permute-start(bf16[528,576]{1,0:T(8,128)(2,1)} %get-tuple-element.80.do0), channel_id=1, source_target_pairs={{0,2},{1,3},{2,0},{3,1},{4,6},{5,7},{6,4},{7,5},{8,10},{9,11},{10,... | collective-permute-start | bytes 1824776 | tf_op jit(solution)/shard_map/ppermute | solution.py:763
  8.2 55.0 %collective-permute-start.13 = (bf16[528,576]{1,0:T(8,128)(2,1)}, bf16[528,576]{1,0:T(8,128)(2,1)}, u32[]{:S(2)}, u32[]{:S(2)}) collective-permute-start(bf16[528,576]{1,0:T(8,128)(2,1)} %get-tuple-element.80.do0), channel_id=1, source_target_pairs={{0,1},{1,0},{2,3},{3,2},{4,5},{5,4},{6,7},{7,6},{8,9},{9,8},{10,11... | collective-permute-start | bytes 1824776 | tf_op jit(solution)/shard_map/ppermute | solution.py:763
  8.7 47.4 %collective-permute-start.11 = (bf16[144,3072]{1,0:T(8,128)(2,1)}, bf16[144,3072]{1,0:T(8,128)(2,1)}, u32[]{:S(2)}, u32[]{:S(2)}) collective-permute-start(bf16[144,3072]{1,0:T(8,128)(2,1)} %get-tuple-element.79.gu0), channel_id=1, source_target_pairs={{0,2},{1,3},{2,0},{3,1},{4,6},{5,7},{6,4},{7,5},{8,10},{9,11},{10,... | collective-permute-start | bytes 2654216 | tf_op jit(solution)/shard_map/ppermute | solution.py:763
  13.7 3.8 %collective-permute-start.2 = (bf16[144,1024]{1,0:T(8,128)(2,1)}, bf16[144,1024]{1,0:T(8,128)(2,1)}, u32[]{:S(2)}, u32[]{:S(2)}) collective-permute-start(bf16[144,1024]{1,0:T(8,128)(2,1)} %collective-permute-done.1.w2), channel_id=1, source_target_pairs={{0,1},{1,0},{2,3},{3,2},{4,5},{5,4},{6,7},{7,6},{8,9},{9,8},{10,11... | collective-permute-start | bytes 884744 | tf_op jit(solution)/shard_map/ppermute | solution.py:763
  21.7 13.0 %collective-permute-start.7 = (bf16[9,128,128]{2,1,0:T(8,128)(2,1)}, bf16[9,128,128]{2,1,0:T(8,128)(2,1)}, u32[]{:S(2)}, u32[]{:S(2)}) collective-permute-start(bf16[9,128,128]{2,1,0:T(8,128)(2,1)} %get-tuple-element.72), channel_id=1, source_target_pairs={{0,4},{4,0},{8,12},{12,8},{16,20},{20,16},{24,28},{28,24},{1,5},{5... | collective-permute-start | bytes 884744 | tf_op jit(solution)/shard_map/ppermute | solution.py:763
  23.7 10.4 %collective-permute-start.3 = (bf16[9,128,128]{2,1,0:T(8,128)(2,1)}, bf16[9,128,128]{2,1,0:T(8,128)(2,1)}, u32[]{:S(2)}, u32[]{:S(2)}) collective-permute-start(bf16[9,128,128]{2,1,0:T(8,128)(2,1)} %get-tuple-element.72), channel_id=1, source_target_pairs={{0,8},{4,12},{8,16},{12,20},{16,24},{20,28},{1,9},{5,13},{9,17},{1... | collective-permute-start | bytes 884744 | tf_op jit(solution)/shard_map/ppermute | solution.py:1015
  34.1 15.9 %collective-permute-start.6 = (bf16[9,128,128]{2,1,0:T(8,128)(2,1)}, bf16[9,128,128]{2,1,0:T(8,128)(2,1)}, u32[]{:S(2)}, u32[]{:S(2)}) collective-permute-start(bf16[9,128,128]{2,1,0:T(8,128)(2,1)} %collective-permute-done.3), channel_id=1, source_target_pairs={{0,4},{4,0},{8,12},{12,8},{16,20},{20,16},{24,28},{28,24},{1,5},{5... | collective-permute-start | bytes 884744 | tf_op jit(solution)/shard_map/ppermute | solution.py:763
  34.7 10.5 %collective-permute-start.4 = (bf16[9,128,128]{2,1,0:T(8,128)(2,1)}, bf16[9,128,128]{2,1,0:T(8,128)(2,1)}, u32[]{:S(2)}, u32[]{:S(2)}) collective-permute-start(bf16[9,128,128]{2,1,0:T(8,128)(2,1)} %collective-permute-done.3), channel_id=1, source_target_pairs={{0,8},{4,12},{8,16},{12,20},{16,24},{20,28},{1,9},{5,13},{9,17},{1... | collective-permute-start | bytes 884744 | tf_op jit(solution)/shard_map/ppermute | solution.py:1015
  45.2 11.4 %collective-permute-start.8 = (bf16[9,128,128]{2,1,0:T(8,128)(2,1)}, bf16[9,128,128]{2,1,0:T(8,128)(2,1)}, u32[]{:S(2)}, u32[]{:S(2)}) collective-permute-start(bf16[9,128,128]{2,1,0:T(8,128)(2,1)} %collective-permute-done.4), channel_id=1, source_target_pairs={{0,8},{4,12},{8,16},{12,20},{16,24},{20,28},{1,9},{5,13},{9,17},{1... | collective-permute-start | bytes 884744 | tf_op jit(solution)/shard_map/ppermute | solution.py:1015
  50.0 7.2 %collective-permute-start.5 = (bf16[9,128,128]{2,1,0:T(8,128)(2,1)}, bf16[9,128,128]{2,1,0:T(8,128)(2,1)}, u32[]{:S(2)}, u32[]{:S(2)}) collective-permute-start(bf16[9,128,128]{2,1,0:T(8,128)(2,1)} %collective-permute-done.4), channel_id=1, source_target_pairs={{0,4},{4,0},{8,12},{12,8},{16,20},{20,16},{24,28},{28,24},{1,5},{5... | collective-permute-start | bytes 884744 | tf_op jit(solution)/shard_map/ppermute | solution.py:763
  56.1 7.2 %collective-permute-start.10 = (bf16[144,3072]{1,0:T(8,128)(2,1)}, bf16[144,3072]{1,0:T(8,128)(2,1)}, u32[]{:S(2)}, u32[]{:S(2)}) collective-permute-start(bf16[144,3072]{1,0:T(8,128)(2,1)} %get-tuple-element.79.gu0), channel_id=1, source_target_pairs={{0,1},{1,0},{2,3},{3,2},{4,5},{5,4},{6,7},{7,6},{8,9},{9,8},{10,11... | collective-permute-start | bytes 2654216 | tf_op jit(solution)/shard_map/ppermute | solution.py:763
  56.1 7.1 %collective-permute-start.15 = (bf16[528,576]{1,0:T(8,128)(2,1)}, bf16[528,576]{1,0:T(8,128)(2,1)}, u32[]{:S(2)}, u32[]{:S(2)}) collective-permute-start(bf16[528,576]{1,0:T(8,128)(2,1)} %collective-permute-done.14.do2), channel_id=1, source_target_pairs={{0,1},{1,0},{2,3},{3,2},{4,5},{5,4},{6,7},{7,6},{8,9},{9,8},{10,11... | collective-permute-start | bytes 1824776 | tf_op jit(solution)/shard_map/ppermute | solution.py:763
  56.6 6.7 %collective-permute-start.12 = (bf16[144,3072]{1,0:T(8,128)(2,1)}, bf16[144,3072]{1,0:T(8,128)(2,1)}, u32[]{:S(2)}, u32[]{:S(2)}) collective-permute-start(bf16[144,3072]{1,0:T(8,128)(2,1)} %collective-permute-done.11.gu2), channel_id=1, source_target_pairs={{0,1},{1,0},{2,3},{3,2},{4,5},{5,4},{6,7},{7,6},{8,9},{9,8},{10,11... | collective-permute-start | bytes 2654216 | tf_op jit(solution)/shard_map/ppermute | solution.py:763
  57.2 9.2 %collective-permute-start.9 = (bf16[9,128,128]{2,1,0:T(8,128)(2,1)}, bf16[9,128,128]{2,1,0:T(8,128)(2,1)}, u32[]{:S(2)}, u32[]{:S(2)}) collective-permute-start(bf16[9,128,128]{2,1,0:T(8,128)(2,1)} %collective-permute-done.8), channel_id=1, source_target_pairs={{0,4},{4,0},{8,12},{12,8},{16,20},{20,16},{24,28},{28,24},{1,5},{5... | collective-permute-start | bytes 884744 | tf_op jit(solution)/shard_map/ppermute | solution.py:763
  87.1 6.1 %collective-permute-start.16 = (bf16[2,8,256,384]{3,2,1,0:T(8,128)(2,1)}, bf16[2,8,256,384]{3,2,1,0:T(8,128)(2,1)}, u32[]{:S(2)}, u32[]{:S(2)}) collective-permute-start(bf16[2,8,256,384]{3,2,1,0:T(8,128)(2,1)} %get-tuple-element.88), channel_id=1, source_target_pairs={{0,1},{1,0},{2,3},{3,2},{4,5},{5,4},{6,7},{7,6},{8,9},{9,8},{10,11... | collective-permute-start | bytes 9437192 | tf_op jit(solution)/shard_map/ppermute | solution.py:763
  96.7 36.8 %collective-permute-start.24 = (bf16[8,256,384]{2,1,0:T(8,128)(2,1)}, bf16[8,256,384]{2,1,0:T(8,128)(2,1)}, u32[]{:S(2)}, u32[]{:S(2)}) collective-permute-start(bf16[8,256,384]{2,1,0:T(8,128)(2,1)} %shard_map.220.refs_1_), channel_id=1, source_target_pairs={{0,2},{1,3},{2,0},{3,1},{4,6},{5,7},{6,4},{7,5},{8,10},{9,11},{10,... | collective-permute-start | bytes 4718600 | tf_op jit(solution)/shard_map/ppermute | solution.py:763
  98.3 10.2 %collective-permute-start.17 = (bf16[9,128,128]{2,1,0:T(8,128)(2,1)}, bf16[9,128,128]{2,1,0:T(8,128)(2,1)}, u32[]{:S(2)}, u32[]{:S(2)}) collective-permute-start(bf16[9,128,128]{2,1,0:T(8,128)(2,1)} %bitcast.56), channel_id=1, source_target_pairs={{0,4},{4,0},{8,12},{12,8},{16,20},{20,16},{24,28},{28,24},{1,5},{5... | collective-permute-start | bytes 884744 | tf_op jit(solution)/shard_map/ppermute | solution.py:763
  102.7 11.7 %collective-permute-start.18 = (bf16[9,128,128]{2,1,0:T(8,128)(2,1)}, bf16[9,128,128]{2,1,0:T(8,128)(2,1)}, u32[]{:S(2)}, u32[]{:S(2)}) collective-permute-start(bf16[9,128,128]{2,1,0:T(8,128)(2,1)} %bitcast.55), channel_id=1, source_target_pairs={{0,4},{4,0},{8,12},{12,8},{16,20},{20,16},{24,28},{28,24},{1,5},{5... | collective-permute-start | bytes 884744 | tf_op jit(solution)/shard_map/ppermute | solution.py:763
  112.6 12.3 %collective-permute-start.22 = (bf16[9,128,128]{2,1,0:T(8,128)(2,1)}, bf16[9,128,128]{2,1,0:T(8,128)(2,1)}, u32[]{:S(2)}, u32[]{:S(2)}) collective-permute-start(bf16[9,128,128]{2,1,0:T(8,128)(2,1)} %bitcast.54), channel_id=1, source_target_pairs={{0,4},{4,0},{8,12},{12,8},{16,20},{20,16},{24,28},{28,24},{1,5},{5... | collective-permute-start | bytes 884744 | tf_op jit(solution)/shard_map/ppermute | solution.py:763
  113.2 25.3 %collective-permute-start.20 = (bf16[9,128,128]{2,1,0:T(8,128)(2,1)}, bf16[9,128,128]{2,1,0:T(8,128)(2,1)}, u32[]{:S(2)}, u32[]{:S(2)}) collective-permute-start(bf16[9,128,128]{2,1,0:T(8,128)(2,1)} %get-tuple-element.99), channel_id=1, source_target_pairs={{24,0},{28,4},{25,1},{29,5},{26,2},{30,6},{27,3},{31,7}} | collective-permute-start | bytes 884744 | tf_op jit(solution)/shard_map/ppermute | solution.py:927
  122.2 16.2 %collective-permute-start.19 = (bf16[9,128,128]{2,1,0:T(8,128)(2,1)}, bf16[9,128,128]{2,1,0:T(8,128)(2,1)}, u32[]{:S(2)}, u32[]{:S(2)}) collective-permute-start(bf16[9,128,128]{2,1,0:T(8,128)(2,1)} %bitcast.53), channel_id=1, source_target_pairs={{0,4},{4,0},{8,12},{12,8},{16,20},{20,16},{24,28},{28,24},{1,5},{5... | collective-permute-start | bytes 884744 | tf_op jit(solution)/shard_map/ppermute | solution.py:763
  123.7 20.6 %collective-permute-start.21 = (bf16[9,128,128]{2,1,0:T(8,128)(2,1)}, bf16[9,128,128]{2,1,0:T(8,128)(2,1)}, u32[]{:S(2)}, u32[]{:S(2)}) collective-permute-start(bf16[9,128,128]{2,1,0:T(8,128)(2,1)} %get-tuple-element.100), channel_id=1, source_target_pairs={{16,0},{20,4},{24,8},{28,12},{17,1},{21,5},{25,9},{29,13},{18,2},{... | collective-permute-start | bytes 884744 | tf_op jit(solution)/shard_map/ppermute | solution.py:927
  126.8 18.3 %collective-permute-start.23 = (bf16[9,128,128]{2,1,0:T(8,128)(2,1)}, bf16[9,128,128]{2,1,0:T(8,128)(2,1)}, u32[]{:S(2)}, u32[]{:S(2)}) collective-permute-start(bf16[9,128,128]{2,1,0:T(8,128)(2,1)} %shard_map.224.refs_0_), channel_id=1, source_target_pairs={{8,0},{12,4},{16,8},{20,12},{24,16},{28,20},{9,1},{13,5},{17,9},{2... | collective-permute-start | bytes 884744 | tf_op jit(solution)/shard_map/ppermute | solution.py:927
  137.8 19.1 %collective-permute-start.26 = (bf16[4,256,384]{2,1,0:T(8,128)(2,1)}, bf16[4,256,384]{2,1,0:T(8,128)(2,1)}, u32[]{:S(2)}, u32[]{:S(2)}) collective-permute-start(bf16[4,256,384]{2,1,0:T(8,128)(2,1)} %get-tuple-element.107), channel_id=1, source_target_pairs={{0,4},{4,0},{8,12},{12,8},{16,20},{20,16},{24,28},{28,24},{1,5},{5... | collective-permute-start | bytes 2359304 | tf_op jit(solution)/shard_map/ppermute | solution.py:763
  152.3 6.9 %collective-permute-start.25 = (bf16[2,8,144,128]{3,2,1,0:T(8,128)(2,1)}, bf16[2,8,144,128]{3,2,1,0:T(8,128)(2,1)}, u32[]{:S(2)}, u32[]{:S(2)}) collective-permute-start(bf16[2,8,144,128]{3,2,1,0:T(8,128)(2,1)} %get-tuple-element.106), channel_id=1, source_target_pairs={{0,1},{1,0},{2,3},{3,2},{4,5},{5,4},{6,7},{7,6},{8,9},{9,8},{10,11... | collective-permute-start | bytes 1769480 | tf_op jit(solution)/shard_map/ppermute | solution.py:763
  161.8 28.7 %collective-permute-start.27 = (bf16[8,144,128]{2,1,0:T(8,128)(2,1)}, bf16[8,144,128]{2,1,0:T(8,128)(2,1)}, u32[]{:S(2)}, u32[]{:S(2)}) collective-permute-start(bf16[8,144,128]{2,1,0:T(8,128)(2,1)} %shard_map.228.refs_5_), channel_id=1, source_target_pairs={{0,2},{1,3},{2,0},{3,1},{4,6},{5,7},{6,4},{7,5},{8,10},{9,11},{10,... | collective-permute-start | bytes 884744 | tf_op jit(solution)/shard_map/ppermute | solution.py:763
  163.4 8.7 %collective-permute-start.28 = (bf16[256,384]{1,0:T(8,128)(2,1)}, bf16[256,384]{1,0:T(8,128)(2,1)}, u32[]{:S(2)}, u32[]{:S(2)}) collective-permute-start(bf16[256,384]{1,0:T(8,128)(2,1)} %get-tuple-element.109), channel_id=1, source_target_pairs={{0,8},{4,12},{8,0},{12,4},{16,24},{20,28},{24,16},{28,20},{1,9},{5... | collective-permute-start | bytes 589832 | tf_op jit(solution)/shard_map/ppermute | solution.py:763
  165.7 16.6 %collective-permute-start.29 = (bf16[256,384]{1,0:T(8,128)(2,1)}, bf16[256,384]{1,0:T(8,128)(2,1)}, u32[]{:S(2)}, u32[]{:S(2)}) collective-permute-start(bf16[256,384]{1,0:T(8,128)(2,1)} %get-tuple-element.110), channel_id=1, source_target_pairs={{0,16},{4,20},{8,24},{12,28},{16,0},{20,4},{24,8},{28,12},{1,17},{... | collective-permute-start | bytes 589832 | tf_op jit(solution)/shard_map/ppermute | solution.py:763
  167.7 14.6 %collective-permute-start.30 = (bf16[256,384]{1,0:T(8,128)(2,1)}, bf16[256,384]{1,0:T(8,128)(2,1)}, u32[]{:S(2)}, u32[]{:S(2)}) collective-permute-start(bf16[256,384]{1,0:T(8,128)(2,1)} %get-tuple-element.111), channel_id=1, source_target_pairs={{0,24},{4,28},{8,16},{12,20},{16,8},{20,12},{24,0},{28,4},{1,25},{... | collective-permute-start | bytes 589832 | tf_op jit(solution)/shard_map/ppermute | solution.py:763
  184.2 16.2 %collective-permute-start.37 = (bf16[256,384]{1,0:T(8,128)(2,1)}, bf16[256,384]{1,0:T(8,128)(2,1)}, u32[]{:S(2)}, u32[]{:S(2)}) collective-permute-start(bf16[256,384]{1,0:T(8,128)(2,1)} %shard_map.229.refs_0_.refs_1_), channel_id=1, source_target_pairs={{0,24},{4,28},{8,16},{12,20},{16,8},{20,12},{24,0},{28,4},{1,25},{... | collective-permute-start | bytes 589832 | tf_op jit(solution)/shard_map/ppermute | solution.py:763
  186.6 15.6 %collective-permute-start.36 = (bf16[256,384]{1,0:T(8,128)(2,1)}, bf16[256,384]{1,0:T(8,128)(2,1)}, u32[]{:S(2)}, u32[]{:S(2)}) collective-permute-start(bf16[256,384]{1,0:T(8,128)(2,1)} %shard_map.229.refs_0_.refs_1_), channel_id=1, source_target_pairs={{0,16},{4,20},{8,24},{12,28},{16,0},{20,4},{24,8},{28,12},{1,17},{... | collective-permute-start | bytes 589832 | tf_op jit(solution)/shard_map/ppermute | solution.py:763
  190.5 11.6 %collective-permute-start.35 = (bf16[256,384]{1,0:T(8,128)(2,1)}, bf16[256,384]{1,0:T(8,128)(2,1)}, u32[]{:S(2)}, u32[]{:S(2)}) collective-permute-start(bf16[256,384]{1,0:T(8,128)(2,1)} %shard_map.229.refs_0_.refs_1_), channel_id=1, source_target_pairs={{0,8},{4,12},{8,0},{12,4},{16,24},{20,28},{24,16},{28,20},{1,9},{5... | collective-permute-start | bytes 589832 | tf_op jit(solution)/shard_map/ppermute | solution.py:763
  193.3 5.5 %collective-permute-start.31 = (bf16[4,144,128]{2,1,0:T(8,128)(2,1)}, bf16[4,144,128]{2,1,0:T(8,128)(2,1)}, u32[]{:S(2)}, u32[]{:S(2)}) collective-permute-start(bf16[4,144,128]{2,1,0:T(8,128)(2,1)} %get-tuple-element.113), channel_id=1, source_target_pairs={{0,4},{4,0},{8,12},{12,8},{16,20},{20,16},{24,28},{28,24},{1,5},{5... | collective-permute-start | bytes 442376 | tf_op jit(solution)/shard_map/ppermute | solution.py:763
  204.4 21.1 %collective-permute-start.42 = (bf16[4,256,384]{2,1,0:T(8,128)(2,1)}, bf16[4,256,384]{2,1,0:T(8,128)(2,1)}, u32[]{:S(2)}, u32[]{:S(2)}) collective-permute-start(bf16[4,256,384]{2,1,0:T(8,128)(2,1)} %shard_map.232.refs_5_.refs_0_), channel_id=1, source_target_pairs={{0,4},{4,0},{8,12},{12,8},{16,20},{20,16},{24,28},{28,24},{1,5},{5... | collective-permute-start | bytes 2359304 | tf_op jit(solution)/shard_map/ppermute | solution.py:763
  206.0 4.4 %collective-permute-start.32 = (bf16[144,128]{1,0:T(8,128)(2,1)}, bf16[144,128]{1,0:T(8,128)(2,1)}, u32[]{:S(2)}, u32[]{:S(2)}) collective-permute-start(bf16[144,128]{1,0:T(8,128)(2,1)} %get-tuple-element.115), channel_id=1, source_target_pairs={{0,8},{4,12},{8,0},{12,4},{16,24},{20,28},{24,16},{28,20},{1,9},{5... | collective-permute-start | bytes 110600 | tf_op jit(solution)/shard_map/ppermute | solution.py:763
  206.0 5.5 %collective-permute-start.33 = (bf16[144,128]{1,0:T(8,128)(2,1)}, bf16[144,128]{1,0:T(8,128)(2,1)}, u32[]{:S(2)}, u32[]{:S(2)}) collective-permute-start(bf16[144,128]{1,0:T(8,128)(2,1)} %get-tuple-element.116), channel_id=1, source_target_pairs={{0,16},{4,20},{8,24},{12,28},{16,0},{20,4},{24,8},{28,12},{1,17},{... | collective-permute-start | bytes 110600 | tf_op jit(solution)/shard_map/ppermute | solution.py:763
  209.2 6.1 %collective-permute-start.34 = (bf16[144,128]{1,0:T(8,128)(2,1)}, bf16[144,128]{1,0:T(8,128)(2,1)}, u32[]{:S(2)}, u32[]{:S(2)}) collective-permute-start(bf16[144,128]{1,0:T(8,128)(2,1)} %get-tuple-element.117), channel_id=1, source_target_pairs={{0,24},{4,28},{8,16},{12,20},{16,8},{20,12},{24,0},{28,4},{1,25},{... | collective-permute-start | bytes 110600 | tf_op jit(solution)/shard_map/ppermute | solution.py:763
  216.8 6.1 %collective-permute-start.40 = (bf16[144,128]{1,0:T(8,128)(2,1)}, bf16[144,128]{1,0:T(8,128)(2,1)}, u32[]{:S(2)}, u32[]{:S(2)}) collective-permute-start(bf16[144,128]{1,0:T(8,128)(2,1)} %shard_map.233.refs_1_.refs_5_), channel_id=1, source_target_pairs={{0,24},{4,28},{8,16},{12,20},{16,8},{20,12},{24,0},{28,4},{1,25},{... | collective-permute-start | bytes 110600 | tf_op jit(solution)/shard_map/ppermute | solution.py:763
  218.0 5.8 %collective-permute-start.39 = (bf16[144,128]{1,0:T(8,128)(2,1)}, bf16[144,128]{1,0:T(8,128)(2,1)}, u32[]{:S(2)}, u32[]{:S(2)}) collective-permute-start(bf16[144,128]{1,0:T(8,128)(2,1)} %shard_map.233.refs_1_.refs_5_), channel_id=1, source_target_pairs={{0,16},{4,20},{8,24},{12,28},{16,0},{20,4},{24,8},{28,12},{1,17},{... | collective-permute-start | bytes 110600 | tf_op jit(solution)/shard_map/ppermute | solution.py:763
  218.0 5.9 %collective-permute-start.38 = (bf16[144,128]{1,0:T(8,128)(2,1)}, bf16[144,128]{1,0:T(8,128)(2,1)}, u32[]{:S(2)}, u32[]{:S(2)}) collective-permute-start(bf16[144,128]{1,0:T(8,128)(2,1)} %shard_map.233.refs_1_.refs_5_), channel_id=1, source_target_pairs={{0,8},{4,12},{8,0},{12,4},{16,24},{20,28},{24,16},{28,20},{1,9},{5... | collective-permute-start | bytes 110600 | tf_op jit(solution)/shard_map/ppermute | solution.py:763
  225.3 5.5 %collective-permute-start.41 = (bf16[4,144,128]{2,1,0:T(8,128)(2,1)}, bf16[4,144,128]{2,1,0:T(8,128)(2,1)}, u32[]{:S(2)}, u32[]{:S(2)}) collective-permute-start(bf16[4,144,128]{2,1,0:T(8,128)(2,1)} %shard_map.234.refs_0_), channel_id=1, source_target_pairs={{0,4},{4,0},{8,12},{12,8},{16,20},{20,16},{24,28},{28,24},{1,5},{5... | collective-permute-start | bytes 442376 | tf_op jit(solution)/shard_map/ppermute | solution.py:763
